TPU v7x, 128 devices: a whole 4x4x4 slice. The times are simulated.
128 devices in a mesh: row: 8 (over z_lo, y), col: 16 (over x, z_hi, core).
Axes of the slice: x: 4, y: 4, z: 4 (z_hi: 2, z_lo: 2; z = z_hi * 2 + z_lo), core: 2. Of those that a mesh axis runs over, the one named last changes fastest.
Arguments:
- x_input: bfloat16 [64, 2048, 256], P('row', 'col'), may hold values from -70 to 70
- grad_output: bfloat16 [64, 2048, 256], P('row', 'col'), may hold values from -6 to 6
- in_scale: float32 [256], replicated, may hold values from 0.5 to 2
- in_shift: float32 [256], replicated, may hold values from -3 to 3
- w_expand: bfloat16 [256, 1024], replicated, may hold values from -0.375 to 0.375
- dw_kernel: float32 [9, 1024], replicated, may hold values from -2 to 2
- w_project: bfloat16 [1024, 256], replicated, may hold values from -0.1875 to 0.1875
- gain_block: float32 [256], replicated, may hold values from 0.5 to 2
- w_qkv_block: bfloat16 [256, 768], replicated, may hold values from -0.375 to 0.375
- w_out_block: bfloat16 [256, 256], replicated, may hold values from -0.375 to 0.375
- bias_block: float32 [8, 225], replicated, may hold values from -3 to 330
- gain_grid: float32 [256], replicated, may hold values from 0.5 to 2
- w_qkv_grid: bfloat16 [256, 768], replicated, may hold values from -0.375 to 0.375
- w_out_grid: bfloat16 [256, 256], replicated, may hold values from -0.375 to 0.375
- bias_grid: float32 [8, 225], replicated, may hold values from -3 to 330
Outputs:
- grad_input: bfloat16 [64, 2048, 256], P('row', 'col')
- grad_expand: float32 [256, 1024], replicated
- grad_kernel: float32 [9, 1024], replicated
- grad_project: float32 [1024, 256], replicated
- grad_qkv_block: float32 [256, 768], replicated
- grad_out_block: float32 [256, 256], replicated
- grad_qkv_grid: float32 [256, 768], replicated
- grad_out_grid: float32 [256, 256], replicated
All inputs are finite; a program needn't handle non-finite values.
Results may differ from a plain program's by a relative error of at most 0.02.
Values may be sent and summed in bfloat16 or wider, within the bound.
No kernel may reach another device: no remote copies, remote signals or barrier semaphores. Data moves between devices by JAX's collectives and lax.ppermute only.
A program may use at most 128 MiB of HBM per device.

v0:
```python
import jax
import jax.numpy as jnp
from jax import lax
from jax.sharding import PartitionSpec as P

HEADS = 8


EPSILON = 1e-05


def with_halo(cells, sides, width):
    for axis, dim in sides:
        count = lax.axis_size(axis)
        ends = count - 1
        head = lax.slice_in_dim(cells, 0, width, axis=dim)
        tail = lax.slice_in_dim(cells, cells.shape[dim] - width, cells.shape[dim], axis=dim)
        cells = jnp.concatenate(
            [
                lax.ppermute(tail, axis, [(i, (i + 1) % count) for i in range(ends)]),
                cells,
                lax.ppermute(head, axis, [((i + 1) % count, i) for i in range(ends)]),
            ],
            axis=dim,
        )
    return cells


def settle(values):
    return lax.optimization_barrier(values)


def project(left_side, matrix):
    return lax.dot_general(
        left_side,
        matrix,
        (((left_side.ndim - 1,), (0,)), ((), ())),
        preferred_element_type=jnp.float32,
    )


def project_back(left_side, matrix):
    return lax.dot_general(
        left_side,
        matrix,
        (((left_side.ndim - 1,), (1,)), ((), ())),
        preferred_element_type=jnp.float32,
    )


def outer_total(left_side, right_side):
    leading = tuple(range(left_side.ndim - 1))
    return lax.dot_general(
        left_side, right_side, ((leading, leading), ((), ())), preferred_element_type=jnp.float32
    )


def gelu_slope(values):
    return jax.jvp(jax.nn.gelu, (values,), (jnp.ones_like(values),))[1]


def normalize(values, gain_vec):
    average = jnp.mean(values, axis=-1, keepdims=True)
    centered = values - average
    spread = jnp.mean(centered * centered, axis=-1, keepdims=True)
    return centered * lax.rsqrt(spread + EPSILON) * gain_vec


def layer_norm(values, gain_vec):
    return normalize(values.astype(jnp.float32), gain_vec).astype(jnp.bfloat16)


def norm_backward(values, gain_vec, grad_normed):
    _, pullback = jax.vjp(lambda inputs: normalize(inputs, gain_vec), values.astype(jnp.float32))
    return pullback(grad_normed.astype(jnp.float32))[0]


def bias_full(bias_table):
    position = jnp.arange(64, dtype=jnp.int32)
    pos_row = position // 8
    pos_col = position % 8
    relative = (pos_row[:, None] - pos_row[None, :] + 7) * 15 + (
        pos_col[:, None] - pos_col[None, :] + 7
    )
    onehot = (relative[:, :, None] == jnp.arange(225, dtype=jnp.int32)[None, None, :]).astype(
        jnp.float32
    )
    return jnp.einsum("pqr,hr->hpq", onehot, bias_table, precision=lax.Precision.HIGHEST)


def split_heads(values):
    groups, places, features = values.shape
    return values.reshape(groups, places, HEADS, features // HEADS)


def attend_parts(query_part, key_part, value_part, bias_cube):
    query_heads = split_heads(query_part)
    key_heads = split_heads(key_part)
    value_heads = split_heads(value_part)
    scale = query_heads.shape[-1] ** (-0.5)
    scores = (
        jnp.einsum("gphd,gqhd->ghpq", query_heads, key_heads, preferred_element_type=jnp.float32)
        * scale
        + bias_cube[None]
    )
    probs = jax.nn.softmax(scores, axis=-1)
    weights = settle(probs.astype(jnp.bfloat16))
    mixture = jnp.einsum(
        "ghpq,gqhd->gphd", weights, value_heads, preferred_element_type=jnp.float32
    )
    return (mixture.reshape(query_part.shape).astype(jnp.bfloat16), probs, weights)


def attend_core(query_part, key_part, value_part, bias_cube):
    return attend_parts(query_part, key_part, value_part, bias_cube)[0]


def attend_front(normed, w_qkv):
    features = normed.shape[-1]
    joined = project(normed, w_qkv)
    return (
        joined[..., :features].astype(jnp.bfloat16),
        joined[..., features : 2 * features].astype(jnp.bfloat16),
        joined[..., 2 * features :].astype(jnp.bfloat16),
    )


def attend_grads(normed, query_part, key_part, value_part, grad_out, w_qkv, w_out, bias_cube):
    mixture, probs, weights = attend_parts(query_part, key_part, value_part, bias_cube)
    total_out = outer_total(mixture, grad_out)
    grad_mixture = project_back(grad_out, w_out).astype(jnp.bfloat16)
    grad_heads = split_heads(grad_mixture)
    query_heads = split_heads(query_part)
    key_heads = split_heads(key_part)
    value_heads = split_heads(value_part)
    scale = query_heads.shape[-1] ** (-0.5)
    grad_weights = settle(
        jnp.einsum(
            "gphd,gqhd->ghpq", grad_heads, value_heads, preferred_element_type=jnp.float32
        ).astype(jnp.bfloat16)
    ).astype(jnp.float32)
    grad_value = jnp.einsum(
        "ghpq,gphd->gqhd", weights, grad_heads, preferred_element_type=jnp.float32
    ).astype(jnp.bfloat16)
    grad_scores = probs * (grad_weights - jnp.sum(grad_weights * probs, axis=-1, keepdims=True))
    grad_scaled = grad_scores * scale
    grad_query = jnp.einsum(
        "ghpq,gqhd->gphd",
        grad_scaled,
        key_heads.astype(jnp.float32),
        precision=lax.Precision.HIGHEST,
    ).astype(jnp.bfloat16)
    grad_key = jnp.einsum(
        "ghpq,gphd->gqhd",
        grad_scaled,
        query_heads.astype(jnp.float32),
        precision=lax.Precision.HIGHEST,
    ).astype(jnp.bfloat16)
    shape = query_part.shape
    grad_joined = jnp.concatenate(
        [grad_query.reshape(shape), grad_key.reshape(shape), grad_value.reshape(shape)], axis=-1
    )
    total_qkv = outer_total(normed, grad_joined)
    grad_normed = project_back(grad_joined, w_qkv).astype(jnp.bfloat16)
    return (grad_normed, total_qkv, total_out)


def to_windows(tile_cells):
    tile_rows, tile_cols, channels = tile_cells.shape
    return (
        tile_cells.reshape(tile_rows // 8, 8, tile_cols // 8, 8, channels)
        .transpose(0, 2, 1, 3, 4)
        .reshape(-1, 64, channels)
    )


def from_windows(windows, tile_rows, tile_cols):
    channels = windows.shape[-1]
    return (
        windows.reshape(tile_rows // 8, tile_cols // 8, 8, 8, channels)
        .transpose(0, 2, 1, 3, 4)
        .reshape(tile_rows, tile_cols, channels)
    )


def grid_order(tile_cells, row_devices, col_devices):
    tile_rows, tile_cols, channels = tile_cells.shape
    per_row = 8 // row_devices
    divided = tile_cells.reshape(
        per_row, row_devices, tile_rows // 8, col_devices, tile_cols // col_devices, channels
    )
    return divided.transpose(1, 3, 0, 2, 4, 5)


def tile_order(grid_cells, tile_rows, tile_cols):
    channels = grid_cells.shape[-1]
    return grid_cells.transpose(2, 0, 3, 1, 4, 5).reshape(tile_rows, tile_cols, channels)


def to_groups(received, col_devices):
    row_devices, _, per_row, part_rows, part_cols, channels = received.shape
    per_col = col_devices // 8
    divided = received.reshape(row_devices, 8, per_col, per_row, part_rows, part_cols, channels)
    return divided.transpose(2, 4, 5, 0, 3, 1, 6).reshape(
        per_col * part_rows * part_cols, 64, channels
    )


def from_groups(groups, layout):
    row_devices, col_devices, per_row, part_rows, part_cols, channels = layout
    per_col = col_devices // 8
    divided = groups.reshape(per_col, part_rows, part_cols, row_devices, per_row, 8, channels)
    return divided.transpose(3, 5, 0, 4, 1, 2, 6).reshape(
        row_devices, col_devices, per_row, part_rows, part_cols, channels
    )


def expand_front(row_block, inside, in_scale, in_shift, w_expand):
    shifted = (row_block.astype(jnp.float32) * in_scale + in_shift).astype(jnp.bfloat16)
    preact = project(shifted, w_expand)
    lifted = jnp.where(inside, jax.nn.gelu(preact), 0.0).astype(jnp.bfloat16)
    return (shifted, preact, settle(lifted))


def depthwise(padded, kernel, row_count, col_count):
    summed = jnp.zeros((row_count, col_count, padded.shape[-1]), jnp.float32)
    for offset in range(9):
        row_off, col_off = (offset // 3, offset % 3)
        summed = summed + kernel[offset] * padded[
            row_off : row_off + row_count, col_off : col_off + col_count
        ].astype(jnp.float32)
    return summed


def depthwise_back(padded, kernel, row_count, col_count):
    summed = jnp.zeros((row_count, col_count, padded.shape[-1]), jnp.float32)
    for offset in range(9):
        row_off, col_off = (offset // 3, offset % 3)
        summed = summed + kernel[offset] * padded[
            2 - row_off : 2 - row_off + row_count, 2 - col_off : 2 - col_off + col_count
        ].astype(jnp.float32)
    return summed


def kernel_grad(padded, grad_inner, row_count, col_count):
    grad_values = grad_inner.astype(jnp.float32)
    return jnp.stack(
        [
            jnp.sum(
                padded[
                    offset // 3 : offset // 3 + row_count, offset % 3 : offset % 3 + col_count
                ].astype(jnp.float32)
                * grad_values,
                axis=(0, 1),
            )
            for offset in range(9)
        ]
    )


def shards(
    x_input,
    grad_output,
    in_scale,
    in_shift,
    w_expand,
    dw_kernel,
    w_project,
    gain_block,
    w_qkv_block,
    w_out_block,
    bias_block,
    gain_grid,
    w_qkv_grid,
    w_out_grid,
    bias_grid,
):
    tile_rows, tile_cols, features = x_input.shape
    row_devices = lax.axis_size("row")
    col_devices = lax.axis_size("col")
    tokens_all = tile_rows * tile_cols * row_devices * col_devices
    everywhere = jnp.ones((1, 1, 1), jnp.bool_)
    shifted, preact, lifted = expand_front(x_input, everywhere, in_scale, in_shift, w_expand)
    lifted_pad = with_halo(lifted, (("row", 0), ("col", 1)), 1)
    lifted_pad = settle(lifted_pad)
    convolved = depthwise(lifted_pad, dw_kernel, tile_rows, tile_cols)
    second = jax.nn.gelu(convolved).astype(jnp.bfloat16)
    section_one = settle(
        (x_input.astype(jnp.float32) + project(second, w_project)).astype(jnp.bfloat16)
    )
    block_cube = bias_full(bias_block)
    windows = to_windows(layer_norm(section_one, gain_block))
    projected = attend_front(windows, w_qkv_block)
    attended = project(
        attend_core(projected[0], projected[1], projected[2], block_cube), w_out_block
    )
    section_two = settle(
        (section_one.astype(jnp.float32) + from_windows(attended, tile_rows, tile_cols)).astype(
            jnp.bfloat16
        )
    )
    normed_grid = layer_norm(section_two, gain_grid)
    sendable = grid_order(normed_grid, row_devices, col_devices)
    cotangent = grid_order(grad_output, row_devices, col_devices)
    layout = sendable.shape
    flat_shape = (row_devices * col_devices,) + layout[2:]
    got_normed, got_grad = (
        lax.all_to_all(
            sendable.reshape(flat_shape), ("row", "col"), split_axis=0, concat_axis=0, tiled=True
        ),
        lax.all_to_all(
            cotangent.reshape(flat_shape), ("row", "col"), split_axis=0, concat_axis=0, tiled=True
        ),
    )
    got_normed = got_normed.reshape(layout)
    got_grad = got_grad.reshape(layout)
    group_normed = to_groups(got_normed, col_devices)
    group_grad = to_groups(got_grad, col_devices)
    grid_projected = attend_front(group_normed, w_qkv_grid)
    grad_groups, qkv_grid_total, out_grid_total = attend_grads(
        group_normed,
        grid_projected[0],
        grid_projected[1],
        grid_projected[2],
        group_grad,
        w_qkv_grid,
        w_out_grid,
        bias_full(bias_grid),
    )
    outgoing = from_groups(grad_groups, layout)
    returned = lax.all_to_all(
        outgoing.reshape(flat_shape), ("row", "col"), split_axis=0, concat_axis=0, tiled=True
    ).reshape(layout)
    grad_normed_grid = settle(tile_order(returned, tile_rows, tile_cols))
    grad_section_two = settle(
        (
            grad_output.astype(jnp.float32)
            + norm_backward(section_two, gain_grid, grad_normed_grid)
        ).astype(jnp.bfloat16)
    )
    grad_windows, qkv_block_total, out_block_total = attend_grads(
        windows,
        projected[0],
        projected[1],
        projected[2],
        to_windows(grad_section_two),
        w_qkv_block,
        w_out_block,
        block_cube,
    )
    grad_rows = settle(from_windows(grad_windows, tile_rows, tile_cols))
    grad_section_one = settle(
        (
            grad_section_two.astype(jnp.float32) + norm_backward(section_one, gain_block, grad_rows)
        ).astype(jnp.bfloat16)
    )
    attention_totals = lax.psum(
        (qkv_block_total, out_block_total, qkv_grid_total, out_grid_total), ("row", "col")
    )
    through = project_back(grad_section_one, w_project)
    grad_inner = settle((through * gelu_slope(convolved)).astype(jnp.bfloat16))
    grad_pad = settle(with_halo(grad_inner, (("row", 0), ("col", 1)), 1))
    grad_lifted = depthwise_back(grad_pad, dw_kernel, tile_rows, tile_cols)
    grad_preact = (grad_lifted * gelu_slope(preact)).astype(jnp.bfloat16)
    project_total = outer_total(second, grad_section_one)
    kernel_total = kernel_grad(lifted_pad, grad_inner, tile_rows, tile_cols)
    expand_total = outer_total(shifted, grad_preact)
    returned_input = project_back(grad_preact, w_expand)
    grad_input = (grad_section_one.astype(jnp.float32) + returned_input * in_scale).astype(
        jnp.bfloat16
    )
    conv_totals = lax.psum((expand_total, kernel_total, project_total), ("row", "col"))
    factor = tokens_all ** (-0.5)
    return (
        grad_input,
        conv_totals[0] * factor,
        conv_totals[1] * factor,
        conv_totals[2] * factor,
        attention_totals[0] * factor,
        attention_totals[1] * factor,
        attention_totals[2] * factor,
        attention_totals[3] * factor,
    )


def solution(mesh):
    placed = (
        P("row", "col", None),
        P("row", "col", None),
        P(),
        P(),
        P(),
        P(),
        P(),
        P(),
        P(),
        P(),
        P(),
        P(),
        P(),
        P(),
        P(),
    )
    return jax.shard_map(
        shards,
        mesh=mesh,
        in_specs=placed,
        out_specs=(P("row", "col", None), P(), P(), P(), P(), P(), P(), P()),
        check_vma=False,
    )
```

profile of v0, /device:TPU:1, one launch (start us, length us, event | category | flops | bytes accessed | tf_op | source)
XLA Modules:
  0.0 436.2 jit_solution(7459722915932023471)
XLA Ops:
  7.2 12.0 %all-to-all-start.1 = ((bf16[128,1,1,8,256]{4,3,2,1,0:T(8,128)(2,1)}), bf16[128,1,1,8,256]{4,3,2,1,0:T(8,128)(2,1)}, u32[]{:S(2)}, u32[]{:S(2)}) async-start(bf16[128,1,1,8,256]{4,3,2,1,0:T(8,128)(2,1)} %bitcast.220), calls=%async_computation.1 | async-start | bytes 1048576 | tf_op jit(solution)/shard_map/all_to_all | solution.py:311
  19.2 4.5 %multiply_convert_fusion.1 = (bf16[8,128,1024]{2,1,0:T(8,128)(2,1)S(1)}, f32[8,128,1024]{2,1,0:T(8,128)}) fusion(bf16[256,1024]{1,0:T(8,128)(2,1)S(1)} %copy-done, bf16[8,128,256]{2,1,0:T(8,128)(2,1)} %param.15, f32[256]{0:T(256)} %param.18, f32[256]{0:T(256)} %param.17), kind=kOutput, calls=%fused_computation.83 | convolution fusion | flops 547356672 | bytes 7342080 | tf_op jit(solution)/shard_map/dot_general | solution.py:34
  23.7 3.4 collective-permute-start
  28.6 3.5 fusion.99
  32.5 3.8 collective-permute-done.1
  36.3 6.4 %collective-permute-start.2 = (bf16[10,1,1024]{2,1,0:T(2,128)(2,1)S(1)}, bf16[10,1,1024]{2,1,0:T(2,128)(2,1)S(1)}, u32[]{:S(2)}, u32[]{:S(2)}) collective-permute-start(bf16[10,1,1024]{2,1,0:T(2,128)(2,1)S(1)} %get-tuple-element.27), channel_id=1, source_target_pairs={{0,1},{1,2},{2,3},{3,4},{4,5},{5,6},{6,7},{7,8},{8,9},{9,10},{10,1... | collective-permute-start | bytes 61448 | tf_op jit(solution)/shard_map/ppermute | solution.py:20
  46.8 2.8 collective-permute-done.3
  49.6 2.5 pad_maximum_fusion
  52.2 4.5 %fusion.9 = f32[8,128,1024]{2,1,0:T(8,128)S(1)} fusion(f32[1024]{0:T(1024)S(1)} %bitcast.249, f32[1024]{0:T(1024)S(1)} %bitcast.251, f32[1024]{0:T(1024)S(1)} %bitcast.237, f32[1024]{0:T(1024)S(1)} %bitcast.239, f32[1024]{0:T(1024)S(1)} %bitcast.241, f32[1024]{0:T(1024)S(1)} %bitcast.243, f32[1024]{0:T(1024)S(1)} %bitcast.245, f32[1024]{0:T(1024)S(1)} %bitcast.247, ...), kind=kLoop, calls=%fused_computation.35 | loop fusion | flops 27262976 | bytes 23105536 | tf_op jit(solution)/shard_map/add | solution.py:229
  61.4 2.4 copy.109
  63.9 2.4 copy.108
  68.6 5.3 %fusion.163 = (f32[16,8,64]{2,1,0:T(8,128)S(1)}, f32[16,8,64,64]{2,3,1,0:T(8,128)}) fusion(f32[8,64,64]{1,2,0:T(8,128)} %copy.110, bf16[16,64,8,32]{1,3,2,0:T(8,128)(2,1)} %bitcast.223, bf16[16,64,8,32]{1,3,2,0:T(8,128)(2,1)} %bitcast.221), kind=kOutput, calls=%fused_computation.247 | convolution fusion | flops 35651648 | bytes 3309568 | tf_op jit(solution)/shard_map/sub | solution.py:106
  73.9 3.0 fusion.156
  79.9 3.0 copy.112
  82.8 3.8 convert_element_type.256
  91.2 9.8 %all-to-all-start = ((bf16[128,1,1,8,256]{4,3,2,1,0:T(8,128)(2,1)}), bf16[128,1,1,8,256]{4,3,2,1,0:T(8,128)(2,1)}, u32[]{:S(2)}, u32[]{:S(2)}) async-start(bf16[128,1,1,8,256]{4,3,2,1,0:T(8,128)(2,1)} %bitcast.216), calls=%async_computation | async-start | bytes 1048576 | tf_op jit(solution)/shard_map/all_to_all | solution.py:308
  101.0 4.4 %fusion.100 = f32[8,64,64]{2,0,1:T(8,128)} fusion(s32[64,64]{1,0:T(8,128)} %copy-done.49, f32[8,225]{1,0:T(8,128)} %param.29), kind=kOutput, calls=%fused_computation.154 | convolution fusion | flops 89395200 | bytes 154656 | tf_op jit(solution)/shard_map/pqr,hr->hpq/dot_general | solution.py:88
  111.2 2.4 copy.120
  118.1 2.4 copy.121
  120.5 2.4 copy.117
  122.9 2.4 copy.116
  125.3 3.6 convolution_convert_fusion.1
  128.9 5.9 %fusion.164 = (f32[16,8,64]{2,1,0:T(8,128)}, f32[16,8,64,64]{2,3,1,0:T(8,128)}) fusion(f32[8,64,64]{1,2,0:T(8,128)} %copy.118, bf16[16,64,8,32]{1,3,2,0:T(8,128)(2,1)} %bitcast.226, bf16[16,64,8,32]{1,3,2,0:T(8,128)(2,1)} %bitcast.228), kind=kOutput, calls=%fused_computation.248 | convolution fusion | flops 35651648 | bytes 3309568 | tf_op jit(solution)/shard_map/sub | solution.py:106
  134.8 4.3 fusion.10
  139.8 5.0 %fusion.82 = bf16[16,8,32,64]{3,2,1,0:T(8,128)(2,1)} fusion(bf16[16,64,8,32]{1,3,2,0:T(8,128)(2,1)S(1)} %bitcast.227, bf16[16,8,64,64]{2,3,1,0:T(8,128)(2,1)S(1)} %copy-done.13, f32[16,8,64]{2,1,0:T(8,128)S(1)} %get-tuple-element.23, f32[16,8,64,64]{2,3,1,0:T(8,128)S(1)} %copy-done.19, f32[16,8,64]{2,1,0:T(8,128)S(1)} %copy-done.42), kind=kOutput, calls=%fused_computation.124 | convolution fusion | flops 204210176 | bytes 4259840 | tf_op jit(solution)/shard_map/ghpq,gphd->gqhd/dot_general | solution.py:153
  144.8 4.1 fusion.79
  153.5 2.4 copy.126
  161.4 9.8 %all-to-all-start.2 = ((bf16[128,1,1,8,256]{4,3,2,1,0:T(8,128)(2,1)}), bf16[128,1,1,8,256]{4,3,2,1,0:T(8,128)(2,1)}, u32[]{:S(2)}, u32[]{:S(2)}) async-start(bf16[128,1,1,8,256]{4,3,2,1,0:T(8,128)(2,1)} %bitcast.219), calls=%async_computation.2 | async-start | bytes 1048576 | tf_op jit(solution)/shard_map/all_to_all | solution.py:331
  171.2 2.7 convolution_convert_fusion.4
  175.0 2.6 convolution_bitcast_fusion.3
  177.6 6.6 %all-to-all-done.2 = bf16[128,1,1,8,256]{4,3,2,1,0:T(8,128)(2,1)} async-done(((bf16[128,1,1,8,256]{4,3,2,1,0:T(8,128)(2,1)}), bf16[128,1,1,8,256]{4,3,2,1,0:T(8,128)(2,1)}, u32[]{:S(2)}, u32[]{:S(2)}) %all-to-all-start.2) | async-done | bytes 524320 | tf_op jit(solution)/shard_map/all_to_all | solution.py:331
  194.0 4.3 convolution_convert_fusion.5
  200.3 5.0 %fusion.88 = bf16[16,8,32,64]{3,2,1,0:T(8,128)(2,1)} fusion(bf16[16,64,8,32]{1,3,2,0:T(8,128)(2,1)S(1)} %bitcast.224, bf16[16,8,64,64]{2,3,1,0:T(8,128)(2,1)S(1)} %convolution_convert_fusion, f32[16,8,64]{2,1,0:T(8,128)S(1)} %fusion.13, f32[16,8,64,64]{2,3,1,0:T(8,128)S(1)} %copy-done.7, f32[16,8,64]{2,1,0:T(8,128)S(1)} %get-tuple-element.50), kind=kOutput, calls=%fused_computation.126 | convolution fusion | flops 204210176 | bytes 4259840 | tf_op jit(solution)/shard_map/ghpq,gphd->gqhd/dot_general | solution.py:153
  205.3 3.7 fusion.85
  209.0 2.4 copy.138
  211.4 2.4 copy.136
  213.8 2.4 copy.137
  220.6 2.5 convolution_bitcast_fusion
  223.1 2.8 fusion.39
  232.9 4.0 collective-permute-done.5
  236.9 5.3 %collective-permute-start.6 = (bf16[10,1,1024]{2,1,0:T(2,128)(2,1)S(1)}, bf16[10,1,1024]{2,1,0:T(2,128)(2,1)S(1)}, u32[]{:S(2)}, u32[]{:S(2)}) collective-permute-start(bf16[10,1,1024]{2,1,0:T(2,128)(2,1)S(1)} %get-tuple-element.25), channel_id=1, source_target_pairs={{0,1},{1,2},{2,3},{3,4},{4,5},{5,6},{6,7},{7,8},{8,9},{9,10},{10,1... | collective-permute-start | bytes 61448 | tf_op jit(solution)/shard_map/ppermute | solution.py:20
  245.2 3.8 collective-permute-done.7
  250.4 7.4 %fusion.27 = bf16[8,128,1024]{2,1,0:T(8,128)(2,1)S(1)} fusion(f32[8,128,1024]{2,1,0:T(8,128)S(1)} %copy-done.21, bf16[10,130,1024]{2,1,0:T(8,128)(2,1)S(1)} %pad_maximum_fusion.1, f32[1024]{0:T(1024)S(1)} %bitcast.250, f32[1024]{0:T(1024)S(1)} %bitcast.252, f32[1024]{0:T(1024)S(1)} %bitcast.238, f32[1024]{0:T(1024)S(1)} %bitcast.240, f32[1024]{0:T(1024)S(1)} %bitcast.242, ...), kind=kLoop, calls=%fused_computation.53 | loop fusion | flops 46137344 | bytes 25202688 | tf_op jit(solution)/shard_map/convert_element_type | solution.py:364
  260.9 5.8 %fusion.48 = (f32[1024]{0:T(1024)S(1)}, f32[1024]{0:T(1024)S(1)}, f32[1024]{0:T(1024)S(1)}, f32[1024]{0:T(1024)S(1)}, f32[1024]{0:T(1024)S(1)}, /*index=5*/f32[1...) fusion(bf16[8,128,1024]{2,1,0:T(8,128)(2,1)} %copy-done.2, ...), kind=kLoop, calls=%fused_computation.74 | loop fusion | flops 29350912 | bytes 21008384 | tf_op jit(solution)/shard_map/reduce_sum | solution.py:249
  266.8 68.2 %psum.50 = f32[9,1024]{1,0:T(8,128)S(1)} all-reduce(f32[9,1024]{1,0:T(8,128)S(1)} %stack.39), channel_id=1, replica_groups=mesh['row'=8,'col'=16] {'row','col'}, use_global_device_ids=true, to_apply=%region_24.25 | all-reduce | flops 9216 | bytes 73728 | tf_op jit(solution)/shard_map/psum | solution.py:372
  335.6 3.2 fusion.97
  338.8 80.3 %all-reduce.3.cloned.1.call-done = (f32[256,1024]{1,0:T(8,128)}, f32[1024,256]{1,0:T(8,128)}, f32[256,768]{1,0:T(8,128)}, f32[256,256]{1,0:T(8,128)}, f32[256,768]{1,0:T(8,128)}, /*index=5*/f32[256,256]{1,0:T(8,128)}) async-done(((f32[256,1024]{1,0:T(8,128)}, f32[1024,256]{1,0:T(8,128)}, f32[256,768]{1,0:T(8,128)}, f32[256,256]{1,0:T(8,128)}, f32[256,768]{1,0:T(8,128)}, /*index=5*/f32[256,256]{1,0:T(8,128)}), ...) | async-done | bytes 4194320 | tf_op jit(solution)/shard_map/psum | solution.py:372
  419.2 2.5 broadcast_multiply_fusion.1
  (196 shorter events, 80.9 us)
Async XLA Ops:
  7.2 12.0 %copy-start = (bf16[256,1024]{1,0:T(8,128)(2,1)S(1)}, bf16[256,1024]{1,0:T(8,128)(2,1)}, u32[]{:S(2)}) copy-start(bf16[256,1024]{1,0:T(8,128)(2,1)} %param.19) | copy-start | bytes 1572868
  7.2 84.0 %all-to-all-start.1 = ((bf16[128,1,1,8,256]{4,3,2,1,0:T(8,128)(2,1)}), bf16[128,1,1,8,256]{4,3,2,1,0:T(8,128)(2,1)}, u32[]{:S(2)}, u32[]{:S(2)}) async-start(bf16[128,1,1,8,256]{4,3,2,1,0:T(8,128)(2,1)} %bitcast.220), calls=%async_computation.1 | async-start | bytes 1048576 | tf_op jit(solution)/shard_map/all_to_all | solution.py:311
  19.2 9.4 %copy-start.59 = (f32[8,225]{1,0:T(8,128)S(1)}, f32[8,225]{1,0:T(8,128)}, u32[]{:S(2)}) copy-start(f32[8,225]{1,0:T(8,128)} %param.25) | copy-start | bytes 21604
  23.7 23.1 %copy-start.8 = (bf16[8,128,1024]{2,1,0:T(8,128)(2,1)}, bf16[8,128,1024]{2,1,0:T(8,128)(2,1)S(1)}, u32[]{:S(2)}) copy-start(bf16[8,128,1024]{2,1,0:T(8,128)(2,1)S(1)} %get-tuple-element.48) | copy-start | bytes 6291460
  23.7 21.2 %copy-start.50 = (f32[9,1024]{1,0:T(8,128)S(1)}, f32[9,1024]{1,0:T(8,128)}, u32[]{:S(2)}) copy-start(f32[9,1024]{1,0:T(8,128)} %param.20) | copy-start | bytes 110596
  23.7 8.7 %collective-permute-start = (bf16[1,128,1024]{2,1,0:T(8,128)(2,1)S(1)}, bf16[1,128,1024]{2,1,0:T(8,128)(2,1)S(1)}, u32[]{:S(2)}, u32[]{:S(2)}) collective-permute-start(bf16[1,128,1024]{2,1,0:T(8,128)(2,1)S(1)} %get-tuple-element.31), channel_id=1, source_target_pairs={{0,16},{16,32},{32,48},{48,64},{64,80},{80,96},{96,112},{1,17},{17... | collective-permute-start | bytes 786440 | tf_op jit(solution)/shard_map/ppermute | solution.py:20
  27.2 9.1 %collective-permute-start.1 = (bf16[1,128,1024]{2,1,0:T(8,128)(2,1)S(1)}, bf16[1,128,1024]{2,1,0:T(8,128)(2,1)S(1)}, u32[]{:S(2)}, u32[]{:S(2)}) collective-permute-start(bf16[1,128,1024]{2,1,0:T(8,128)(2,1)S(1)} %get-tuple-element.32), channel_id=1, source_target_pairs={{16,0},{32,16},{48,32},{64,48},{80,64},{96,80},{112,96},{17,1},{33... | collective-permute-start | bytes 786440 | tf_op jit(solution)/shard_map/ppermute | solution.py:22
  32.5 14.3 %copy-start.29 = (bf16[1,128,1024]{2,1,0:T(8,128)(2,1)}, bf16[1,128,1024]{2,1,0:T(8,128)(2,1)S(1)}, u32[]{:S(2)}) copy-start(bf16[1,128,1024]{2,1,0:T(8,128)(2,1)S(1)} %collective-permute-done) | copy-start | bytes 786436
  36.3 10.5 %copy-start.30 = (bf16[1,128,1024]{2,1,0:T(8,128)(2,1)}, bf16[1,128,1024]{2,1,0:T(8,128)(2,1)S(1)}, u32[]{:S(2)}) copy-start(bf16[1,128,1024]{2,1,0:T(8,128)(2,1)S(1)} %collective-permute-done.1) | copy-start | bytes 786436
  36.3 10.4 %collective-permute-start.2 = (bf16[10,1,1024]{2,1,0:T(2,128)(2,1)S(1)}, bf16[10,1,1024]{2,1,0:T(2,128)(2,1)S(1)}, u32[]{:S(2)}, u32[]{:S(2)}) collective-permute-start(bf16[10,1,1024]{2,1,0:T(2,128)(2,1)S(1)} %get-tuple-element.27), channel_id=1, source_target_pairs={{0,1},{1,2},{2,3},{3,4},{4,5},{5,6},{6,7},{7,8},{8,9},{9,10},{10,1... | collective-permute-start | bytes 61448 | tf_op jit(solution)/shard_map/ppermute | solution.py:20
  42.8 6.8 %collective-permute-start.3 = (bf16[10,1,1024]{2,1,0:T(2,128)(2,1)S(1)}, bf16[10,1,1024]{2,1,0:T(2,128)(2,1)S(1)}, u32[]{:S(2)}, u32[]{:S(2)}) collective-permute-start(bf16[10,1,1024]{2,1,0:T(2,128)(2,1)S(1)} %get-tuple-element.28), channel_id=1, source_target_pairs={{1,0},{2,1},{3,2},{4,3},{5,4},{6,5},{7,6},{8,7},{9,8},{10,9},{11,1... | collective-permute-start | bytes 61448 | tf_op jit(solution)/shard_map/ppermute | solution.py:22
  44.9 11.7 %copy-start.43 = (f32[1,1024]{1,0:T(1,128)}, f32[1,1024]{1,0:T(1,128)S(1)}, u32[]{:S(2)}) copy-start(f32[1,1024]{1,0:T(1,128)S(1)} %get-tuple-element.45) | copy-start | bytes 12292
  45.0 11.7 %copy-start.45 = (f32[1,1024]{1,0:T(1,128)}, f32[1,1024]{1,0:T(1,128)S(1)}, u32[]{:S(2)}) copy-start(f32[1,1024]{1,0:T(1,128)S(1)} %get-tuple-element.46) | copy-start | bytes 12292
  45.0 11.7 %copy-start.47 = (f32[1,1024]{1,0:T(1,128)}, f32[1,1024]{1,0:T(1,128)S(1)}, u32[]{:S(2)}) copy-start(f32[1,1024]{1,0:T(1,128)S(1)} %get-tuple-element.47) | copy-start | bytes 12292
  52.2 4.5 %copy-start.38 = (bf16[8,128,256]{2,1,0:T(8,128)(2,1)S(1)}, bf16[8,128,256]{2,1,0:T(8,128)(2,1)}, u32[]{:S(2)}) copy-start(bf16[8,128,256]{2,1,0:T(8,128)(2,1)} %param.15) | copy-start | bytes 1572868
  52.2 4.5 %copy-start.56 = (bf16[1024,256]{1,0:T(8,128)(2,1)S(1)}, bf16[1024,256]{1,0:T(8,128)(2,1)}, u32[]{:S(2)}) copy-start(bf16[1024,256]{1,0:T(8,128)(2,1)} %param.21) | copy-start | bytes 1572868
  78.2 8.5 %copy-start.41 = (bf16[256,256]{1,0:T(8,128)(2,1)S(1)}, bf16[256,256]{1,0:T(8,128)(2,1)}, u32[]{:S(2)}) copy-start(bf16[256,256]{1,0:T(8,128)(2,1)} %param.24) | copy-start | bytes 393220
  91.2 22.9 %all-to-all-start = ((bf16[128,1,1,8,256]{4,3,2,1,0:T(8,128)(2,1)}), bf16[128,1,1,8,256]{4,3,2,1,0:T(8,128)(2,1)}, u32[]{:S(2)}, u32[]{:S(2)}) async-start(bf16[128,1,1,8,256]{4,3,2,1,0:T(8,128)(2,1)} %bitcast.216), calls=%async_computation | async-start | bytes 1048576 | tf_op jit(solution)/shard_map/all_to_all | solution.py:308
  134.8 4.4 %copy-start.13 = (bf16[16,8,64,64]{2,3,1,0:T(8,128)(2,1)S(1)}, bf16[16,8,64,64]{2,3,1,0:T(8,128)(2,1)}, u32[]{:S(2)}) copy-start(bf16[16,8,64,64]{2,3,1,0:T(8,128)(2,1)} %convolution_convert_fusion.1) | copy-start | bytes 3145732
  134.8 4.7 %copy-start.19 = (f32[16,8,64,64]{2,3,1,0:T(8,128)S(1)}, f32[16,8,64,64]{2,3,1,0:T(8,128)}, u32[]{:S(2)}) copy-start(f32[16,8,64,64]{2,3,1,0:T(8,128)} %get-tuple-element.53) | copy-start | bytes 6291460
  134.8 4.9 %copy-start.26 = (bf16[16,64,256]{1,2,0:T(8,128)(2,1)S(1)}, bf16[16,64,256]{1,2,0:T(8,128)(2,1)}, u32[]{:S(2)}) copy-start(bf16[16,64,256]{1,2,0:T(8,128)(2,1)} %copy.117) | copy-start | bytes 1572868
  134.8 4.9 %copy-start.42 = (f32[16,8,64]{2,1,0:T(8,128)S(1)}, f32[16,8,64]{2,1,0:T(8,128)}, u32[]{:S(2)}) copy-start(f32[16,8,64]{2,1,0:T(8,128)} %get-tuple-element.52) | copy-start | bytes 98308
  139.2 9.7 %copy-start.6 = (bf16[16,8,64,64]{2,3,1,0:T(8,128)(2,1)}, bf16[16,8,64,64]{2,3,1,0:T(8,128)(2,1)S(1)}, u32[]{:S(2)}) copy-start(bf16[16,8,64,64]{2,3,1,0:T(8,128)(2,1)S(1)} %get-tuple-element.24) | copy-start | bytes 3145732
  139.8 5.0 %copy-start.27 = (bf16[16,64,256]{1,2,0:T(8,128)(2,1)S(1)}, bf16[16,64,256]{1,2,0:T(8,128)(2,1)}, u32[]{:S(2)}) copy-start(bf16[16,64,256]{1,2,0:T(8,128)(2,1)} %copy.116) | copy-start | bytes 1572868
  161.4 22.8 %all-to-all-start.2 = ((bf16[128,1,1,8,256]{4,3,2,1,0:T(8,128)(2,1)}), bf16[128,1,1,8,256]{4,3,2,1,0:T(8,128)(2,1)}, u32[]{:S(2)}, u32[]{:S(2)}) async-start(bf16[128,1,1,8,256]{4,3,2,1,0:T(8,128)(2,1)} %bitcast.219), calls=%async_computation.2 | async-start | bytes 1048576 | tf_op jit(solution)/shard_map/all_to_all | solution.py:331
  171.1 248.0 %all-reduce.3.cloned.1.call-start = ((), (), s32[]{:S(2)}) async-start(), calls=%async_computation.3 | async-start | bytes 8388608 | tf_op jit(solution)/shard_map/psum | solution.py:372
  194.0 5.1 %copy-start.7 = (f32[16,8,64,64]{2,3,1,0:T(8,128)S(1)}, f32[16,8,64,64]{2,3,1,0:T(8,128)}, u32[]{:S(2)}) copy-start(f32[16,8,64,64]{2,3,1,0:T(8,128)} %get-tuple-element.51) | copy-start | bytes 6291460
  200.3 5.0 %copy-start.24 = (bf16[16,64,256]{1,2,0:T(8,128)(2,1)S(1)}, bf16[16,64,256]{1,2,0:T(8,128)(2,1)}, u32[]{:S(2)}) copy-start(bf16[16,64,256]{1,2,0:T(8,128)(2,1)} %copy.109) | copy-start | bytes 1572868
  213.8 4.7 %copy-start.53 = (f32[256]{0:T(256)S(1)}, f32[256]{0:T(256)}, u32[]{:S(2)}) copy-start(f32[256]{0:T(256)} %param.22) | copy-start | bytes 3076
  216.1 4.5 %copy-start.18 = (f32[8,128,1024]{2,1,0:T(8,128)S(1)}, f32[8,128,1024]{2,1,0:T(8,128)}, u32[]{:S(2)}) copy-start(f32[8,128,1024]{2,1,0:T(8,128)} %copy-done.17) | copy-start | bytes 12582916
  223.1 6.0 %copy-start.32 = (bf16[16,64,256]{2,1,0:T(8,128)(2,1)S(1)}, bf16[16,64,256]{2,1,0:T(8,128)(2,1)}, u32[]{:S(2)}) copy-start(bf16[16,64,256]{2,1,0:T(8,128)(2,1)} %copy.138) | copy-start | bytes 1572868
  223.1 6.0 %copy-start.33 = (bf16[16,64,256]{2,1,0:T(8,128)(2,1)S(1)}, bf16[16,64,256]{2,1,0:T(8,128)(2,1)}, u32[]{:S(2)}) copy-start(bf16[16,64,256]{2,1,0:T(8,128)(2,1)} %copy.136) | copy-start | bytes 1572868
  223.1 6.0 %copy-start.34 = (bf16[16,64,256]{2,1,0:T(8,128)(2,1)S(1)}, bf16[16,64,256]{2,1,0:T(8,128)(2,1)}, u32[]{:S(2)}) copy-start(bf16[16,64,256]{2,1,0:T(8,128)(2,1)} %copy.137) | copy-start | bytes 1572868
  225.9 23.1 %copy-start.2 = (bf16[8,128,1024]{2,1,0:T(8,128)(2,1)}, bf16[8,128,1024]{2,1,0:T(8,128)(2,1)S(1)}, u32[]{:S(2)}) copy-start(bf16[8,128,1024]{2,1,0:T(8,128)(2,1)S(1)} %fusion.39) | copy-start | bytes 6291460
  226.0 6.9 %collective-permute-start.4 = (bf16[1,128,1024]{2,1,0:T(8,128)(2,1)S(1)}, bf16[1,128,1024]{2,1,0:T(8,128)(2,1)S(1)}, u32[]{:S(2)}, u32[]{:S(2)}) collective-permute-start(bf16[1,128,1024]{2,1,0:T(8,128)(2,1)S(1)} %get-tuple-element.29), channel_id=1, source_target_pairs={{0,16},{16,32},{32,48},{48,64},{64,80},{80,96},{96,112},{1,17},{17... | collective-permute-start | bytes 786440 | tf_op jit(solution)/shard_map/ppermute | solution.py:20
  227.7 16.5 %copy-start.20 = (bf16[16,8,32,64]{3,2,1,0:T(8,128)(2,1)S(1)}, bf16[16,8,32,64]{3,2,1,0:T(8,128)(2,1)}, u32[]{:S(2)}) copy-start(bf16[16,8,32,64]{3,2,1,0:T(8,128)(2,1)} %convolution_convert_fusion.7) | copy-start | bytes 1572868
  227.7 9.2 %collective-permute-start.5 = (bf16[1,128,1024]{2,1,0:T(8,128)(2,1)S(1)}, bf16[1,128,1024]{2,1,0:T(8,128)(2,1)S(1)}, u32[]{:S(2)}, u32[]{:S(2)}) collective-permute-start(bf16[1,128,1024]{2,1,0:T(8,128)(2,1)S(1)} %get-tuple-element.30), channel_id=1, source_target_pairs={{16,0},{32,16},{48,32},{64,48},{80,64},{96,80},{112,96},{17,1},{33... | collective-permute-start | bytes 786440 | tf_op jit(solution)/shard_map/ppermute | solution.py:22
  236.9 13.4 %copy-start.21 = (f32[8,128,1024]{2,1,0:T(8,128)S(1)}, f32[8,128,1024]{2,1,0:T(8,128)}, u32[]{:S(2)}) copy-start(f32[8,128,1024]{2,1,0:T(8,128)} %get-tuple-element.49) | copy-start | bytes 12582916
  236.9 13.4 %copy-start.44 = (f32[1,1024]{1,0:T(1,128)S(1)}, f32[1,1024]{1,0:T(1,128)}, u32[]{:S(2)}) copy-start(f32[1,1024]{1,0:T(1,128)} %copy-done.43) | copy-start | bytes 12292
  236.9 13.4 %copy-start.46 = (f32[1,1024]{1,0:T(1,128)S(1)}, f32[1,1024]{1,0:T(1,128)}, u32[]{:S(2)}) copy-start(f32[1,1024]{1,0:T(1,128)} %copy-done.45) | copy-start | bytes 12292
  236.9 13.4 %copy-start.48 = (f32[1,1024]{1,0:T(1,128)S(1)}, f32[1,1024]{1,0:T(1,128)}, u32[]{:S(2)}) copy-start(f32[1,1024]{1,0:T(1,128)} %copy-done.47) | copy-start | bytes 12292
  236.9 8.3 %collective-permute-start.6 = (bf16[10,1,1024]{2,1,0:T(2,128)(2,1)S(1)}, bf16[10,1,1024]{2,1,0:T(2,128)(2,1)S(1)}, u32[]{:S(2)}, u32[]{:S(2)}) collective-permute-start(bf16[10,1,1024]{2,1,0:T(2,128)(2,1)S(1)} %get-tuple-element.25), channel_id=1, source_target_pairs={{0,1},{1,2},{2,3},{3,4},{4,5},{5,6},{6,7},{7,8},{8,9},{9,10},{10,1... | collective-permute-start | bytes 61448 | tf_op jit(solution)/shard_map/ppermute | solution.py:20
  242.2 6.8 %collective-permute-start.7 = (bf16[10,1,1024]{2,1,0:T(2,128)(2,1)S(1)}, bf16[10,1,1024]{2,1,0:T(2,128)(2,1)S(1)}, u32[]{:S(2)}, u32[]{:S(2)}) collective-permute-start(bf16[10,1,1024]{2,1,0:T(2,128)(2,1)S(1)} %get-tuple-element.26), channel_id=1, source_target_pairs={{1,0},{2,1},{3,2},{4,3},{5,4},{6,5},{7,6},{8,7},{9,8},{10,9},{11,1... | collective-permute-start | bytes 61448 | tf_op jit(solution)/shard_map/ppermute | solution.py:22
  250.3 8.8 %copy-start.39 = (bf16[8,128,256]{2,1,0:T(8,128)(2,1)S(1)}, bf16[8,128,256]{2,1,0:T(8,128)(2,1)}, u32[]{:S(2)}) copy-start(bf16[8,128,256]{2,1,0:T(8,128)(2,1)} %param.15) | copy-start | bytes 1572868
  250.4 8.8 %copy-start.54 = (f32[256]{0:T(256)S(1)}, f32[256]{0:T(256)}, u32[]{:S(2)}) copy-start(f32[256]{0:T(256)} %param.18) | copy-start | bytes 3076
  250.4 8.8 %copy-start.55 = (f32[256]{0:T(256)S(1)}, f32[256]{0:T(256)}, u32[]{:S(2)}) copy-start(f32[256]{0:T(256)} %param.17) | copy-start | bytes 3076
  419.2 7.9 %copy-start.31 = (f32[256,768]{1,0:T(8,128)S(1)}, f32[256,768]{1,0:T(8,128)}, u32[]{:S(2)}) copy-start(f32[256,768]{1,0:T(8,128)} %get-tuple-element.21) | copy-start | bytes 2359300
  419.2 8.9 %copy-start.28 = (f32[1024,256]{1,0:T(8,128)S(1)}, f32[1024,256]{1,0:T(8,128)}, u32[]{:S(2)}) copy-start(f32[1024,256]{1,0:T(8,128)} %get-tuple-element.18) | copy-start | bytes 3145732
  (24 other events, 64.1 us)
Sparse Core Ops, SparseCore 0:
  261.0 158.1 all-reduce.2
where the time goes:
time: 442 us; the launch traced here: 436 us
  waiting for transfers between devices  104 us (24%)
  matrix products  86 us (19%)
  blocking collectives  68.2 us (15%)
  local copies, waits for them, and re-layouts  55.6 us (13%)
  starting transfers between devices  55.1 us (12%)
  other arithmetic  51.7 us (12%)
  between operations  15.4 us (3%)
    psum x1, waiting for transfers between devices, shards(): lax.psum((expand_total, kernel_total, project_total), ('row', 'col'))  80.3 us
    psum x1, blocking collectives, shards(): lax.psum((expand_total, kernel_total, project_total), ('row', 'col'))  68.2 us
    ppermute x4, starting transfers between devices, with_halo(): lax.ppermute(tail, axis, [(i, (i + 1) % count) for i in range(ends)])  16.8 us
    ppermute x4, waiting for transfers between devices, with_halo(): lax.ppermute(head, axis, [((i + 1) % count, i) for i in range(ends)])  14.4 us
    dot_general x6, matrix products, project_back(): lax.dot_general(left_side, matrix, (((left_side.ndim - 1,), (1,)), ((), (...  13.5 us
    all_to_all x1, starting transfers between devices, shards(): lax.all_to_all(cotangent.reshape(flat_shape), ('row', 'col'), split_axis=...  12 us
    sub x2, matrix products, attend_parts(): probs = jax.nn.softmax(scores, axis=-1)  11.2 us
    dot_general x6, matrix products, outer_total(): lax.dot_general(left_side, right_side, ((leading, leading), ((), ())), pr...  10.7 us
  transfers between devices with their start and end apart: 12, of which 9 were waited for; matrix products, arithmetic and copies ran while one was open for 18% of the time, Pallas kernels for 0%

commit v1 on v0

v1 whole, which is shorter than its diff:
```python
import jax
import jax.numpy as jnp
from jax import lax
from jax.experimental import pallas as pl
from jax.experimental.pallas import tpu as pltpu
from jax.sharding import Mesh
from jax.sharding import PartitionSpec as P

F32 = jnp.float32
BF16 = jnp.bfloat16
EPSILON = 1e-05
HEADS = 8
HEAD = 32
SCALE = HEAD ** (-0.5)
ROWS = 8
COLS = 128
TOKENS = ROWS * COLS
D = 256
E = 1024
BLOCKS = E // 128
LEFT = 8
WIDE = COLS + 2 * LEFT
GELU_1 = 0.7978845608028654
GELU_3 = 0.044715 * GELU_1


def dot(left, right, left_dim, right_dim):
    return lax.dot_general(
        left, right, (((left_dim,), (right_dim,)), ((), ())), preferred_element_type=F32
    )


def gelu_pair(values):
    square = values * values
    half = 0.5 + 0.5 * jnp.tanh(values * (GELU_1 + GELU_3 * square))
    value = values * half
    slope = half + value * (1.0 - half) * (2.0 * GELU_1 + (6.0 * GELU_3) * square)
    return value, slope


def norm_parts(values):
    centered = values - jnp.mean(values, axis=-1, keepdims=True)
    spread = jnp.mean(centered * centered, axis=-1, keepdims=True)
    inverse = lax.rsqrt(spread + EPSILON)
    return centered * inverse, inverse


def norm_back(values, gain, grad):
    unit, inverse = norm_parts(values)
    scaled = grad * gain
    mean_grad = jnp.mean(scaled, axis=-1, keepdims=True)
    mean_unit = jnp.mean(scaled * unit, axis=-1, keepdims=True)
    return inverse * (scaled - mean_grad - unit * mean_unit)


def four_windows(cells):
    return jnp.concatenate(
        [cells[:, 8 * m : 8 * m + 8, :].reshape(64, D) for m in range(4)], axis=0
    )


def from_four_windows(tokens):
    return jnp.concatenate(
        [tokens[64 * m : 64 * m + 64].reshape(8, 8, D) for m in range(4)], axis=1
    )


def make_bias(rows_ref, bias_ref):
    for head in range(HEADS):
        rows = rows_ref[head]
        for a_k in range(8):
            start = 8 * (7 - a_k)
            bias_ref[
                head // 4, 8 * a_k : 8 * a_k + 8, 64 * (head % 4) : 64 * (head % 4) + 64
            ] = rows[:, start : start + 64]


def stacked(part, heads_mask):
    return jnp.concatenate([part] * 4, axis=0) * heads_mask


def pick(product):
    lane = lax.broadcasted_iota(jnp.int32, (64, 128), 1)
    low = jnp.where(lane < 32, product[0:64], product[64:128])
    high = jnp.where(lane < 96, product[128:192], product[192:256])
    return jnp.where(lane < 64, low, high)


def softmax_keys(scores):
    shifted = jnp.exp(scores - jnp.max(scores, axis=0, keepdims=True))
    return shifted * (1.0 / jnp.sum(shifted, axis=0, keepdims=True))


def half_of(joined, part, half, group):
    start = part * D + half * 128
    return joined[64 * group : 64 * group + 64, start : start + 128]


def attend(joined, bias_ref, heads_mask, group, half):
    query = half_of(joined, 0, half, group)
    key = half_of(joined, 1, half, group)
    value = half_of(joined, 2, half, group)
    query_stack = stacked(query, heads_mask)
    probs = softmax_keys(dot(key, query_stack, 1, 1) * SCALE + bias_ref[half])
    mixture = pick(dot(probs.astype(BF16), value, 0, 0)).astype(BF16)
    return probs, mixture


def attend_back(joined, probs, grad_mix, heads_mask, group, half):
    query = half_of(joined, 0, half, group)
    key = half_of(joined, 1, half, group)
    value = half_of(joined, 2, half, group)
    query_stack = stacked(query, heads_mask)
    grad_stack = stacked(grad_mix, heads_mask)
    grad_weights = dot(value, grad_stack, 1, 1).astype(BF16).astype(F32)
    centre = jnp.sum(grad_weights * probs, axis=0, keepdims=True)
    grad_scores = (probs * (grad_weights - centre) * SCALE).astype(BF16)
    grad_value = dot(probs.astype(BF16), grad_stack, 1, 0).astype(BF16)
    grad_key = dot(grad_scores, query_stack, 1, 0).astype(BF16)
    grad_query = pick(dot(grad_scores, key, 0, 0)).astype(BF16)
    return grad_query, grad_key, grad_value


def heads_mask_of():
    row = lax.broadcasted_iota(jnp.int32, (256, 128), 0) // 64
    lane = lax.broadcasted_iota(jnp.int32, (256, 128), 1) // HEAD
    return jnp.where(row == lane, 1.0, 0.0).astype(BF16)


def attention_totals(total_ref, normed_ref, grad_joined_ref, mixture_ref, grad_ref):
    for part in range(3):
        total = dot(normed_ref[...], grad_joined_ref[:, D * part : D * part + D], 0, 0)
        for k in range(2):
            start = 256 * (2 * part + k)
            total_ref[start : start + 256, :] = total[:, 128 * k : 128 * k + 128]
    total = dot(mixture_ref[...], grad_ref[...], 0, 0)
    for k in range(2):
        total_ref[1536 + 256 * k : 1792 + 256 * k, :] = total[:, 128 * k : 128 * k + 128]


def front_kernel(
    edge_ref,
    x_ref,
    top_ref,
    bottom_ref,
    side_ref,
    scale_ref,
    shift_ref,
    w_expand_ref,
    dw_ref,
    w_project_ref,
    gain_block_ref,
    w_qkv_ref,
    w_out_ref,
    rows_ref,
    gain_grid_ref,
    lifted_ref,
    slope_pre_ref,
    second_ref,
    slope_conv_ref,
    section_one_ref,
    section_two_ref,
    normed_grid_ref,
    normed_block_ref,
    joined_ref,
    probs_ref,
    mixture_ref,
    pad,
    cells,
    outcome,
    bias,
):
    make_bias(rows_ref, bias)
    heads_mask = heads_mask_of()

    def shifted_of(tokens):
        return (tokens.astype(F32) * scale_ref[...] + shift_ref[...]).astype(BF16)

    for source, row, flag in ((top_ref, 0, edge_ref[0]), (bottom_ref, 9, edge_ref[1])):
        shifted = shifted_of(source[...])
        for pair in range(4):
            value, _ = gelu_pair(dot(shifted, w_expand_ref[:, 256 * pair : 256 * pair + 256], 1, 0))
            value = value.astype(BF16).astype(F32) * flag
            for k in range(2):
                pad[2 * pair + k, row, LEFT : LEFT + COLS, :] = value[:, 128 * k : 128 * k + 128]
    shifted = shifted_of(side_ref[...])
    place = lax.broadcasted_iota(jnp.int32, (32, 1), 0)
    flags = jnp.where(place < 16, edge_ref[2], edge_ref[3])
    flags = flags * jnp.where(place % 16 == 0, edge_ref[0], 1.0)
    flags = flags * jnp.where(place % 16 == 9, edge_ref[1], 1.0)
    for pair in range(4):
        value, _ = gelu_pair(dot(shifted, w_expand_ref[:, 256 * pair : 256 * pair + 256], 1, 0))
        value = value.astype(BF16).astype(F32) * flags
        for k in range(2):
            for row in range(10):
                part = value[:, 128 * k : 128 * k + 128]
                pad[2 * pair + k, row, LEFT - 1 : LEFT, :] = part[row : row + 1]
                pad[2 * pair + k, row, LEFT + COLS : LEFT + COLS + 1, :] = part[16 + row : 17 + row]

    @pl.loop(0, ROWS)
    def _(row):
        here = pl.ds(pl.multiple_of(row * COLS, COLS), COLS)
        shifted = shifted_of(x_ref[here, :])
        for pair in range(4):
            value, slope = gelu_pair(
                dot(shifted, w_expand_ref[:, 256 * pair : 256 * pair + 256], 1, 0)
            )
            value = value.astype(BF16)
            slope = slope.astype(BF16)
            for k in range(2):
                lanes = slice(128 * k, 128 * k + 128)
                lifted_ref[2 * pair + k, here, :] = value[:, lanes]
                slope_pre_ref[2 * pair + k, here, :] = slope[:, lanes]
                pad[2 * pair + k, row + 1, LEFT : LEFT + COLS, :] = value[:, lanes].astype(F32)

    @pl.loop(0, BLOCKS)
    def _(block):
        taps = [
            dw_ref[t : t + 1, pl.ds(pl.multiple_of(block * 128, 128), 128)] for t in range(9)
        ]

        @pl.loop(0, ROWS)
        def _(row):
            for chunk in range(4):
                summed = None
                for t in range(9):
                    start = LEFT - 1 + t % 3 + 32 * chunk
                    term = taps[t] * pad[block, row + t // 3, start : start + 32, :]
                    summed = term if summed is None else summed + term
                value, slope = gelu_pair(summed)
                here = pl.ds(pl.multiple_of(row * COLS + 32 * chunk, 32), 32)
                second_ref[block, here, :] = value.astype(BF16)
                slope_conv_ref[block, here, :] = slope.astype(BF16)

    @pl.loop(0, 4)
    def _(part):
        here = pl.ds(pl.multiple_of(part * 256, 256), 256)
        summed = x_ref[here, :].astype(F32)
        for pair in range(4):
            joined = jnp.concatenate(
                [second_ref[2 * pair, here, :], second_ref[2 * pair + 1, here, :]], axis=1
            )
            summed = summed + dot(joined, w_project_ref[256 * pair : 256 * pair + 256, :], 1, 0)
        section_one = summed.astype(BF16)
        section_one_ref[here, :] = section_one
        cells[pl.ds(part * 2, 2)] = section_one.astype(F32).reshape(2, COLS, D)

    @pl.loop(0, 4)
    def _(part):
        here = pl.ds(pl.multiple_of(part * 256, 256), 256)
        columns = pl.ds(pl.multiple_of(part * 32, 32), 32)
        section_one = four_windows(cells[:, columns, :])
        normed = (norm_parts(section_one)[0] * gain_block_ref[...]).astype(BF16)
        normed_block_ref[here, :] = normed
        joined = dot(normed, w_qkv_ref[...], 1, 0).astype(BF16)
        joined_ref[here, :] = joined
        mixtures = []
        for group in range(4):
            halves = []
            for half in range(2):
                probs, mixture = attend(joined, bias, heads_mask, group, half)
                probs_ref[part * 8 + group * 2 + half] = probs
                halves.append(mixture)
            mixtures.append(jnp.concatenate(halves, axis=1))
        mixture = jnp.concatenate(mixtures, axis=0)
        mixture_ref[here, :] = mixture
        section_two = (section_one + dot(mixture, w_out_ref[...], 1, 0)).astype(BF16).astype(F32)
        cells[:, columns, :] = from_four_windows(section_two)
        normed = norm_parts(section_two)[0] * gain_grid_ref[...]
        outcome[:, columns, :] = from_four_windows(normed)

    section_two_ref[...] = cells[...].reshape(TOKENS, D).astype(BF16)
    normed_grid_ref[...] = outcome[...].reshape(TOKENS, D).astype(BF16)


def grid_kernel(
    normed_ref,
    grad_ref,
    w_qkv_ref,
    w_out_ref,
    rows_ref,
    grad_normed_ref,
    total_ref,
    bias,
    mixture_ref,
    grad_joined_ref,
):
    make_bias(rows_ref, bias)
    heads_mask = heads_mask_of()

    @pl.loop(0, 4)
    def _(part):
        here = pl.ds(pl.multiple_of(part * 256, 256), 256)
        joined = dot(normed_ref[here, :], w_qkv_ref[...], 1, 0).astype(BF16)
        grad_mix = dot(grad_ref[here, :], w_out_ref[...], 1, 1).astype(BF16)
        mixtures = []
        grads = []
        for group in range(4):
            halves = []
            pieces = []
            for half in range(2):
                probs, mixture = attend(joined, bias, heads_mask, group, half)
                halves.append(mixture)
                grad_half = half_of(grad_mix, 0, half, group)
                pieces.append(attend_back(joined, probs, grad_half, heads_mask, group, half))
            mixtures.append(jnp.concatenate(halves, axis=1))
            grads.append(
                jnp.concatenate([pieces[half][k] for k in range(3) for half in range(2)], axis=1)
            )
        mixture_ref[here, :] = jnp.concatenate(mixtures, axis=0)
        grad_joined = jnp.concatenate(grads, axis=0)
        grad_joined_ref[here, :] = grad_joined
        grad_normed_ref[here, :] = dot(grad_joined, w_qkv_ref[...], 1, 1).astype(BF16)

    attention_totals(total_ref, normed_ref, grad_joined_ref, mixture_ref, grad_ref)


def block_kernel(
    returned_ref,
    grad_output_ref,
    section_two_ref,
    section_one_ref,
    normed_block_ref,
    joined_ref,
    probs_ref,
    mixture_ref,
    second_ref,
    slope_conv_ref,
    gain_grid_ref,
    gain_block_ref,
    w_qkv_ref,
    w_out_ref,
    w_project_ref,
    grad_one_ref,
    inner_ref,
    total_ref,
    cells,
    base,
    grad_windows_ref,
    grad_joined_ref,
):
    heads_mask = heads_mask_of()

    @pl.loop(0, ROWS)
    def _(row):
        here = pl.ds(pl.multiple_of(row * COLS, COLS), COLS)
        grad = grad_output_ref[here, :].astype(F32) + norm_back(
            section_two_ref[here, :].astype(F32),
            gain_grid_ref[...],
            returned_ref[here, :].astype(F32),
        )
        cells[row] = grad.astype(BF16).astype(F32)
        base[row] = section_one_ref[here, :].astype(F32)

    @pl.loop(0, 4)
    def _(part):
        here = pl.ds(pl.multiple_of(part * 256, 256), 256)
        columns = pl.ds(pl.multiple_of(part * 32, 32), 32)
        grad_two = four_windows(cells[:, columns, :])
        grad_windows = grad_two.astype(BF16)
        grad_windows_ref[here, :] = grad_windows
        joined = joined_ref[here, :]
        grad_mix = dot(grad_windows, w_out_ref[...], 1, 1).astype(BF16)
        grads = []
        for group in range(4):
            pieces = []
            for half in range(2):
                probs = probs_ref[part * 8 + group * 2 + half]
                grad_half = half_of(grad_mix, 0, half, group)
                pieces.append(attend_back(joined, probs, grad_half, heads_mask, group, half))
            grads.append(
                jnp.concatenate([pieces[half][k] for k in range(3) for half in range(2)], axis=1)
            )
        grad_joined = jnp.concatenate(grads, axis=0)
        grad_joined_ref[here, :] = grad_joined
        grad_normed = dot(grad_joined, w_qkv_ref[...], 1, 1).astype(BF16).astype(F32)
        section_one = four_windows(base[:, columns, :])
        grad_one = grad_two + norm_back(section_one, gain_block_ref[...], grad_normed)
        cells[:, columns, :] = from_four_windows(grad_one)

    @pl.loop(0, ROWS)
    def _(row):
        here = pl.ds(pl.multiple_of(row * COLS, COLS), COLS)
        grad_one = cells[row].astype(BF16)
        grad_one_ref[here, :] = grad_one
        for pair in range(4):
            through = dot(grad_one, w_project_ref[256 * pair : 256 * pair + 256, :], 1, 1)
            for k in range(2):
                block = 2 * pair + k
                slope = slope_conv_ref[block, here, :].astype(F32)
                inner = through[:, 128 * k : 128 * k + 128] * slope
                inner_ref[block, here, :] = inner.astype(BF16)

    attention_totals(total_ref, normed_block_ref, grad_joined_ref, mixture_ref, grad_windows_ref)
    for block in range(BLOCKS):
        total = dot(second_ref[block], grad_one_ref[...], 0, 0)
        for k in range(2):
            start = 2048 + 1024 * k + 128 * block
            total_ref[start : start + 128, :] = total[:, 128 * k : 128 * k + 128]


def back_kernel(
    x_ref,
    lifted_ref,
    slope_pre_ref,
    inner_ref,
    grad_one_ref,
    top_ref,
    bottom_ref,
    side_ref,
    scale_ref,
    shift_ref,
    w_expand_ref,
    dw_ref,
    grad_input_ref,
    total_expand_ref,
    total_kernel_ref,
    pad,
    preact_ref,
    shifted_ref,
):
    for block in range(BLOCKS):
        pad[block, 0, LEFT : LEFT + COLS, :] = top_ref[block].astype(F32)
        pad[block, 9, LEFT : LEFT + COLS, :] = bottom_ref[block].astype(F32)
        side = side_ref[block].astype(F32)
        for row in range(10):
            pad[block, row, LEFT - 1 : LEFT, :] = side[row : row + 1]
            pad[block, row, LEFT + COLS : LEFT + COLS + 1, :] = side[16 + row : 17 + row]

    @pl.loop(0, BLOCKS)
    def _(block):
        taps = [
            dw_ref[t : t + 1, pl.ds(pl.multiple_of(block * 128, 128), 128)] for t in range(9)
        ]

        @pl.loop(0, ROWS)
        def _(row):
            here = pl.ds(pl.multiple_of(row * COLS, COLS), COLS)
            pad[block, row + 1, LEFT : LEFT + COLS, :] = inner_ref[block, here, :].astype(F32)

        def step(row, totals):
            totals = list(totals)
            for chunk in range(4):
                here = pl.ds(pl.multiple_of(row * COLS + 32 * chunk, 32), 32)
                lifted = lifted_ref[block, here, :].astype(F32)
                summed = None
                for t in range(9):
                    start = LEFT + 1 - t % 3 + 32 * chunk
                    cells = pad[block, row + 2 - t // 3, start : start + 32, :]
                    term = taps[t] * cells
                    summed = term if summed is None else summed + term
                    totals[t] = totals[t] + jnp.sum((lifted * cells).reshape(4, 8, 128), axis=0)
                grad = summed * slope_pre_ref[block, here, :].astype(F32)
                preact_ref[block, here, :] = grad.astype(BF16)
            return tuple(totals)

        totals = lax.fori_loop(0, ROWS, step, (jnp.zeros((8, 128), F32),) * 9)
        for t in range(9):
            total_kernel_ref[t, pl.ds(block, 1), :] = jnp.sum(totals[t], axis=0, keepdims=True)

    @pl.loop(0, 4)
    def _(part):
        here = pl.ds(pl.multiple_of(part * 256, 256), 256)
        summed = jnp.zeros((256, D), F32)
        for pair in range(4):
            joined = jnp.concatenate(
                [preact_ref[2 * pair, here, :], preact_ref[2 * pair + 1, here, :]], axis=1
            )
            summed = summed + dot(joined, w_expand_ref[:, 256 * pair : 256 * pair + 256], 1, 1)
        grad_one = grad_one_ref[here, :].astype(F32)
        grad_input_ref[here, :] = (grad_one + summed * scale_ref[...]).astype(BF16)
        shifted_ref[here, :] = (
            x_ref[here, :].astype(F32) * scale_ref[...] + shift_ref[...]
        ).astype(BF16)

    for pair in range(4):
        joined = jnp.concatenate([preact_ref[2 * pair], preact_ref[2 * pair + 1]], axis=1)
        total = dot(shifted_ref[...], joined, 0, 0)
        for k in range(2):
            start = 256 * (2 * pair + k)
            total_expand_ref[start : start + 256, :] = total[:, 128 * k : 128 * k + 128]


VMEM = pl.BlockSpec(memory_space=pltpu.VMEM)
SMEM = pl.BlockSpec(memory_space=pltpu.SMEM)
PARAMS = pltpu.CompilerParams(vmem_limit_bytes=60 * 1024 * 1024)


def shape(dims, kind):
    return jax.ShapeDtypeStruct(dims, kind)


def call(kernel, ins, outs, scratch, smem_first=False):
    specs = [VMEM] * len(ins)
    if smem_first:
        specs[0] = SMEM
    return pl.pallas_call(
        kernel,
        out_shape=outs,
        in_specs=specs,
        out_specs=[VMEM] * len(outs),
        scratch_shapes=scratch,
        compiler_params=PARAMS,
    )(*ins)


def bias_rows(table):
    cube = table.reshape(HEADS, 15, 15)
    rows = jnp.stack([cube[:, :, 7 - e : 15 - e] for e in range(8)], axis=1)
    return jnp.pad(rows.reshape(HEADS, 8, 120), ((0, 0), (0, 0), (0, 8)))


CHUNKS = 64
CHUNK = 72
FACTOR = float((64 * 2048) ** (-0.5))


def pack_kernel(core_ref, block_ref, grid_ref, expand_ref, taps_ref, send_ref, keep_ref):
    core = core_ref[0]

    def low(index):
        return block_ref[64 * index : 64 * index + 64, :], jnp.zeros((8, 128), F32)

    def high(index):
        start = 64 * (index % 32)
        source = grid_ref if index < 32 else expand_ref
        tap = taps_ref[index] if index < 9 else jnp.zeros((8, 128), F32)
        return source[start : start + 64, :], tap

    def fill(kept, sent):
        for index in range(CHUNKS):
            keep_ref[index, :64, :], keep_ref[index, 64:, :] = kept(index)
            send_ref[index] = jnp.concatenate(sent(index), axis=0).astype(BF16)

    @pl.when(core == 0)
    def _():
        fill(low, high)

    @pl.when(core == 1)
    def _():
        fill(high, low)


def pair_kernel(keep_ref, got_ref, out_ref):
    for index in range(CHUNKS):
        out_ref[index] = (keep_ref[index] + got_ref[index].astype(F32)).astype(BF16)


def sum_kernel(got_ref, out_ref):
    def step(index, total):
        return total + got_ref[index].astype(F32)

    total = lax.fori_loop(0, CHUNKS, step, jnp.zeros((CHUNK, 128), F32), unroll=8)
    total = total.astype(BF16)
    for index in range(CHUNKS):
        out_ref[index] = total


def unpack_kernel(
    core_ref,
    mine_ref,
    other_ref,
    expand_ref,
    kernel_ref,
    project_ref,
    qkv_block_ref,
    out_block_ref,
    qkv_grid_ref,
    out_grid_ref,
):
    core = core_ref[0]

    def place(target, row, column, value):
        target[row : row + 64, column : column + 128] = value

    def fill(low_ref, high_ref):
        for index in range(CHUNKS):
            value = low_ref[index].astype(F32) * FACTOR
            start = 64 * index
            if start < 1536:
                place(qkv_block_ref, start % 256, start // 256 * 128, value[:64])
            elif start < 2048:
                place(out_block_ref, start % 256, (start - 1536) // 256 * 128, value[:64])
            else:
                place(project_ref, start % 1024, (start - 2048) // 1024 * 128, value[:64])
            value = high_ref[index].astype(F32) * FACTOR
            if start < 1536:
                place(qkv_grid_ref, start % 256, start // 256 * 128, value[:64])
            elif start < 2048:
                place(out_grid_ref, start % 256, (start - 1536) // 256 * 128, value[:64])
            else:
                place(expand_ref, start % 256, (start - 2048) // 256 * 128, value[:64])
            if index < 9:
                for block in range(BLOCKS):
                    kernel_ref[index : index + 1, 128 * block : 128 * block + 128] = value[
                        64 + block : 65 + block
                    ]

    @pl.when(core == 0)
    def _():
        fill(mine_ref, other_ref)

    @pl.when(core == 1)
    def _():
        fill(other_ref, mine_ref)


def beside_rows(first, last, fill_axis="row"):
    count = lax.axis_size(fill_axis)
    down = [(i, i + 1) for i in range(count - 1)]
    up = [(i + 1, i) for i in range(count - 1)]
    return lax.ppermute(last, fill_axis, down), lax.ppermute(first, fill_axis, up)


def beside_columns(first, last):
    axes = ("hi", "core")
    count = lax.axis_size("hi") * lax.axis_size("core")
    right = [(i, i + 1) for i in range(count - 1)]
    left = [(i + 1, i) for i in range(count - 1)]
    return lax.ppermute(last, axes, right), lax.ppermute(first, axes, left)


def across(values):
    return lax.all_to_all(values, ("row", "hi"), split_axis=0, concat_axis=0, tiled=True)


def sibling(values):
    return lax.ppermute(values, "core", [(0, 1), (1, 0)])


def shards(
    x_input,
    grad_output,
    in_scale,
    in_shift,
    w_expand,
    dw_kernel,
    w_project,
    gain_block,
    w_qkv_block,
    w_out_block,
    bias_block,
    gain_grid,
    w_qkv_grid,
    w_out_grid,
    bias_grid,
):
    row_index = lax.axis_index("row")
    core = lax.axis_index("core")
    col_index = lax.axis_index("hi") * 2 + core
    edge = jnp.stack(
        [
            row_index > 0,
            row_index < lax.axis_size("row") - 1,
            col_index > 0,
            col_index < lax.axis_size("hi") * 2 - 1,
        ]
    ).astype(F32)
    core_flag = core.reshape(1).astype(jnp.int32)
    scale = in_scale.reshape(1, D)
    shift = in_shift.reshape(1, D)
    gain_block = gain_block.reshape(1, D)
    gain_grid = gain_grid.reshape(1, D)
    rows_block = bias_rows(bias_block)
    rows_grid = bias_rows(bias_grid)

    x_top, x_bottom = beside_rows(x_input[0], x_input[ROWS - 1])
    ends = [
        jnp.concatenate([x_top[c : c + 1], x_input[:, c], x_bottom[c : c + 1]], axis=0)
        for c in (0, COLS - 1)
    ]
    ends = [jnp.pad(e, ((0, 6), (0, 0))) for e in ends]
    x_side = jnp.concatenate(beside_columns(ends[0], ends[1]), axis=0)
    x_flat = x_input.reshape(TOKENS, D)
    grad_flat = grad_output.reshape(TOKENS, D)
    hidden = shape((BLOCKS, TOKENS, 128), BF16)
    tokens = shape((TOKENS, D), BF16)
    (
        lifted,
        slope_pre,
        second,
        slope_conv,
        section_one,
        section_two,
        normed_grid,
        normed_block,
        joined,
        probs,
        mixture,
    ) = call(
        front_kernel,
        [
            edge,
            x_flat,
            x_top,
            x_bottom,
            x_side,
            scale,
            shift,
            w_expand,
            dw_kernel,
            w_project,
            gain_block,
            w_qkv_block,
            w_out_block,
            rows_block,
            gain_grid,
        ],
        [
            hidden,
            hidden,
            hidden,
            hidden,
            tokens,
            tokens,
            tokens,
            tokens,
            shape((TOKENS, 3 * D), BF16),
            shape((32, 64, 256), F32),
            tokens,
        ],
        [
            pltpu.VMEM((BLOCKS, ROWS + 2, WIDE, 128), F32),
            pltpu.VMEM((ROWS, COLS, D), F32),
            pltpu.VMEM((ROWS, COLS, D), F32),
            pltpu.VMEM((2, 64, 256), F32),
        ],
        smem_first=True,
    )

    sendable = jnp.stack(
        [normed_grid.reshape(64, 16, D), grad_flat.reshape(64, 16, D)], axis=1
    ).reshape(64, 32, D)
    got = across(sendable).reshape(64, 2, 16, D).transpose(1, 2, 0, 3).reshape(2, TOKENS, D)
    grad_groups, grid_total = call(
        grid_kernel,
        [got[0], got[1], w_qkv_grid, w_out_grid, rows_grid],
        [tokens, shape((2048, 128), F32)],
        [
            pltpu.VMEM((2, 64, 256), F32),
            pltpu.VMEM((TOKENS, D), BF16),
            pltpu.VMEM((TOKENS, 3 * D), BF16),
        ],
    )
    returned = across(grad_groups.reshape(16, 64, D).transpose(1, 0, 2)).reshape(TOKENS, D)

    grad_one, inner, block_total = call(
        block_kernel,
        [
            returned,
            grad_flat,
            section_two,
            section_one,
            normed_block,
            joined,
            probs,
            mixture,
            second,
            slope_conv,
            gain_grid,
            gain_block,
            w_qkv_block,
            w_out_block,
            w_project,
        ],
        [tokens, hidden, shape((4096, 128), F32)],
        [
            pltpu.VMEM((ROWS, COLS, D), F32),
            pltpu.VMEM((ROWS, COLS, D), F32),
            pltpu.VMEM((TOKENS, D), BF16),
            pltpu.VMEM((TOKENS, 3 * D), BF16),
        ],
    )

    cells = inner.reshape(BLOCKS, ROWS, COLS, 128)
    top, bottom = beside_rows(cells[:, 0], cells[:, ROWS - 1])
    ends = [
        jnp.concatenate([top[:, c : c + 1], cells[:, :, c], bottom[:, c : c + 1]], axis=1)
        for c in (0, COLS - 1)
    ]
    ends = [jnp.pad(e, ((0, 0), (0, 6), (0, 0))) for e in ends]
    side = jnp.concatenate(beside_columns(ends[0], ends[1]), axis=1)
    grad_input, expand_total, tap_total = call(
        back_kernel,
        [
            x_flat,
            lifted,
            slope_pre,
            inner,
            grad_one,
            top,
            bottom,
            side,
            scale,
            shift,
            w_expand,
            dw_kernel,
        ],
        [tokens, shape((2048, 128), F32), shape((9, BLOCKS, 128), F32)],
        [
            pltpu.VMEM((BLOCKS, ROWS + 2, WIDE, 128), F32),
            pltpu.VMEM((BLOCKS, TOKENS, 128), BF16),
            pltpu.VMEM((TOKENS, D), BF16),
        ],
    )

    parts = shape((CHUNKS, CHUNK, 128), BF16)
    sent, kept = call(
        pack_kernel,
        [core_flag, block_total, grid_total, expand_total, tap_total],
        [parts, shape((CHUNKS, CHUNK, 128), F32)],
        [],
        smem_first=True,
    )
    (paired,) = call(pair_kernel, [kept, sibling(sent)], [parts], [])
    (summed,) = call(sum_kernel, [across(paired)], [parts], [])
    mine = across(summed)
    totals = call(
        unpack_kernel,
        [core_flag, mine, sibling(mine)],
        [
            shape((D, E), F32),
            shape((9, E), F32),
            shape((E, D), F32),
            shape((D, 3 * D), F32),
            shape((D, D), F32),
            shape((D, 3 * D), F32),
            shape((D, D), F32),
        ],
        [],
        smem_first=True,
    )
    return (grad_input.reshape(ROWS, COLS, D), *totals)


def solution(mesh):
    split = Mesh(mesh.devices.reshape(8, 8, 2), ("row", "hi", "core"))
    tile = P("row", ("hi", "core"), None)
    return jax.shard_map(
        shards,
        mesh=split,
        in_specs=(tile, tile) + (P(),) * 13,
        out_specs=(tile,) + (P(),) * 7,
        check_vma=False,
    )
```

time: 442 us -> 241 us (0.55); the launches traced: 436 us -> 240 us
  matrix products: 86 us -> 0 us
  Pallas kernels: 0 us -> 83.8 us
  waiting for transfers between devices: 104 us -> 23.7 us
  other arithmetic: 51.7 us -> 4.01 us
  local copies, waits for them, and re-layouts: 55.6 us -> 12.9 us
  between operations: 15.4 us -> 0.95 us
  starting transfers between devices: 55.1 us -> 44.3 us
    pallas_call x0 -> x8, Pallas kernels: none -> 83.8 us  [call(): pl.pallas_call(kernel, out_shape=outs, in_specs=specs, out_specs=[VMEM] *...]
    psum x1 -> x0, waiting for transfers between devices: 80.3 us -> none  [shards(): lax.psum((expand_total, kernel_total, project_total), ('row', 'col'))]
    dot_general x29 -> x0, matrix products: 74.8 us -> none  [the longest x6 13.5 us: project_back(): lax.dot_general(left_side, matrix, (((left_side.ndim - 1,), (1,)), ((), (...]
    all_to_all x0 -> x3, blocking collectives: none -> 70.6 us  [across(): lax.all_to_all(values, ('row', 'hi'), split_axis=0, concat_axis=0, tiled=...]
    psum x1 -> x0, blocking collectives: 68.2 us -> none  [shards(): lax.psum((expand_total, kernel_total, project_total), ('row', 'col'))]
    all_to_all x3 -> x1, starting transfers between devices: 31.6 us -> 12.4 us  [across(): lax.all_to_all(values, ('row', 'hi'), split_axis=0, concat_axis=0, tiled=...]
    reduce_sum x11 -> x0, other arithmetic: 17.1 us -> none  [the longest x1 5.84 us: kernel_grad(): jnp.sum(padded[offset // 3:offset // 3 + row_count, offset % 3:offset % 3...]
    convert_element_type x6 -> x1, other arithmetic: 15.5 us -> 0.58 us  [shards(): edge = jnp.stack([row_index > 0, row_index < lax.axis_size('row') - 1, co...]
  transfers between devices with their start and end apart: 12 -> 11, of which waited for: 9 -> 6; matrix products, arithmetic and copies ran while one was open for 18% -> 3% of each run, Pallas kernels for 0% -> 0%
where the time goes in v1:
time: 241 us; the launch traced here: 240 us
  Pallas kernels  83.8 us (35%)
  blocking collectives  70.6 us (29%)
  starting transfers between devices  44.3 us (18%)
  waiting for transfers between devices  23.7 us (10%)
  local copies, waits for them, and re-layouts  12.9 us (5%)
  other arithmetic  4.01 us (2%)
    pallas_call x8, Pallas kernels, call(): pl.pallas_call(kernel, out_shape=outs, in_specs=specs, out_specs=[VMEM] *...  83.8 us
    all_to_all x3, blocking collectives, across(): lax.all_to_all(values, ('row', 'hi'), split_axis=0, concat_axis=0, tiled=...  70.6 us
    ppermute x4, starting transfers between devices, beside_columns(): return (lax.ppermute(last, axes, right), lax.ppermute(first, axes, left))  17.1 us
    all_to_all x1, waiting for transfers between devices, across(): lax.all_to_all(values, ('row', 'hi'), split_axis=0, concat_axis=0, tiled=...  15 us
    all_to_all x1, starting transfers between devices, across(): lax.all_to_all(values, ('row', 'hi'), split_axis=0, concat_axis=0, tiled=...  12.4 us
    ppermute x2, starting transfers between devices, beside_rows(): lax.ppermute(last, fill_axis, down)  8.66 us
    ppermute x2, waiting for transfers between devices, sibling(): return lax.ppermute(values, 'core', [(0, 1), (1, 0)])  5.53 us
  transfers between devices with their start and end apart: 11, of which 6 were waited for; matrix products, arithmetic and copies ran while one was open for 3% of the time, Pallas kernels for 0%

profile of v1, /device:TPU:1, one launch (start us, length us, event | category | flops | bytes accessed | tf_op | source)
XLA Modules:
  0.0 240.3 jit_solution(14998891190971732991)
XLA Ops:
  0.6 0.9 slice_bitcast_fusion.2
  1.5 1.3 collective-permute-start.1
  2.8 4.7 %collective-permute-start = (bf16[128,256]{1,0:T(8,128)(2,1)S(1)}, bf16[128,256]{1,0:T(8,128)(2,1)S(1)}, u32[]{:S(2)}, u32[]{:S(2)}) collective-permute-start(bf16[128,256]{1,0:T(8,128)(2,1)S(1)} %get-tuple-element.73), channel_id=1, source_target_pairs={{0,16},{16,32},{32,48},{48,64},{64,80},{80,96},{96,112},{1,17},{17... | collective-permute-start | bytes 196616 | tf_op jit(solution)/shard_map/ppermute | solution.py:612
  7.5 0.8 reshape.104
  8.3 0.2 fusion.26
  8.5 0.8 fusion.22
  9.4 3.2 %collective-permute-start.3 = (bf16[16,256]{1,0:T(8,128)(2,1)S(1)}, bf16[16,256]{1,0:T(8,128)(2,1)S(1)}, u32[]{:S(2)}, u32[]{:S(2)}) collective-permute-start(bf16[16,256]{1,0:T(8,128)(2,1)S(1)} %fusion.19), channel_id=1, source_target_pairs={{1,0},{2,1},{3,2},{4,3},{5,4},{6,5},{7,6},{8,7},{9,8},{10,9},{11,1... | collective-permute-start | bytes 24584 | tf_op jit(solution)/shard_map/ppermute | solution.py:620
  12.6 5.5 %collective-permute-start.2 = (bf16[16,256]{1,0:T(8,128)(2,1)S(1)}, bf16[16,256]{1,0:T(8,128)(2,1)S(1)}, u32[]{:S(2)}, u32[]{:S(2)}) collective-permute-start(bf16[16,256]{1,0:T(8,128)(2,1)S(1)} %fusion.17), channel_id=1, source_target_pairs={{0,1},{1,2},{2,3},{3,4},{4,5},{5,6},{6,7},{7,8},{8,9},{9,10},{10,1... | collective-permute-start | bytes 24584 | tf_op jit(solution)/shard_map/ppermute | solution.py:620
  18.1 0.6 add_convert_fusion.edge_ref
  18.9 0.1 stack.82
  19.0 0.1 stack.81
  19.5 0.6 pad.23.rows_ref
  20.1 0.6 pad_maximum_fusion.2.side_ref
  20.8 22.1 %shard_map.206 = (bf16[8,1024,128]{2,1,0:T(8,128)(2,1)}, bf16[8,1024,128]{2,1,0:T(8,128)(2,1)}, bf16[8,1024,128]{2,1,0:T(8,128)(2,1)}, bf16[8,1024,128]{2,1,0:T(...) custom-call(f32[4]{0:T(128)} %add_convert_fusion.edge_ref, ...), custom_call_target="tpu_custom_call" | custom-call | tf_op jit(solution)/shard_map/pallas_call | solution.py:497
  42.9 2.1 pad_maximum_fusion
  45.0 12.4 %all-to-all-start = ((bf16[64,32,256]{2,1,0:T(8,128)(2,1)}), bf16[64,32,256]{2,1,0:T(8,128)(2,1)S(1)}, u32[]{:S(2)}, u32[]{:S(2)}) async-start(bf16[64,32,256]{2,1,0:T(8,128)(2,1)} %bitcast.24), calls=%async_computation | async-start | bytes 2097152 | tf_op jit(solution)/shard_map/all_to_all | solution.py:624
  57.5 0.2 fusion.25
  57.7 0.1 stack.94
  58.5 0.6 pad.24.rows_ref
  59.1 15.0 %all-to-all-done = bf16[64,32,256]{2,1,0:T(8,128)(2,1)S(1)} async-done(((bf16[64,32,256]{2,1,0:T(8,128)(2,1)}), bf16[64,32,256]{2,1,0:T(8,128)(2,1)S(1)}, u32[]{:S(2)}, u32[]{:S(2)}) %all-to-all-start) | async-done | bytes 1048608 | tf_op jit(solution)/shard_map/all_to_all | solution.py:624
  74.1 0.6 copy.67
  74.7 1.0 fusion.21
  75.7 14.5 %shard_map.207 = (bf16[1024,256]{1,0:T(8,128)(2,1)}, f32[2048,128]{1,0:T(8,128)}) custom-call(bf16[1024,256]{1,0:T(8,128)(2,1)} %bitcast.79, bf16[1024,256]{1,0:T(8,128)(2,1)} %bitcast.78, bf16[256,768]{1,0:T(8,128)(2,1)} %w_qkv_ref.4, bf16[256,256]{1,0:T(8,128)(2,1)} %w_out_ref.4, f32[8,8,128]{2,1,0:T(8,128)} %pad.24.rows_ref), custom_call_target="tpu_custom_call" | custom-call | tf_op jit(solution)/shard_map/pallas_call | solution.py:497
  90.2 1.3 copy.68
  91.6 17.3 %all_to_all.20 = bf16[64,16,256]{2,1,0:T(8,128)(2,1)} all-to-all(bf16[64,16,256]{2,1,0:T(8,128)(2,1)S(1)} %bitcast.80), channel_id=1, replica_groups=mesh['row'=8,'hi'=8,'core'=2] {'row','hi'}, dimensions={0} | all-to-all | bytes 1048576 | tf_op jit(solution)/shard_map/all_to_all | solution.py:624
  108.8 20.2 %shard_map.208 = (bf16[1024,256]{1,0:T(8,128)(2,1)}, bf16[8,1024,128]{2,1,0:T(8,128)(2,1)}, f32[4096,128]{1,0:T(8,128)}) custom-call(bf16[1024,256]{1,0:T(8,128)(2,1)} %bitcast.75, bf16[1024,256]{1,0:T(8,128)(2,1)} %bitcast.76, bf16[1024,256]{1,0:T(8,128)(2,1)} %get-tuple-element.40.section_two_ref, bf16[1024,256]{1,0:T(8,128)(2,1)} %get-tuple-element.41.section_one_ref, ...), custom_call_target="tpu_custom_call" | custom-call | tf_op jit(solution)/shard_map/pallas_call | solution.py:497
  129.0 1.1 slice_bitcast_fusion
  130.1 1.3 collective-permute-start.5
  131.4 4.0 %collective-permute-start.4 = (bf16[8,128,128]{2,1,0:T(8,128)(2,1)S(1)}, bf16[8,128,128]{2,1,0:T(8,128)(2,1)S(1)}, u32[]{:S(2)}, u32[]{:S(2)}) collective-permute-start(bf16[8,128,128]{2,1,0:T(8,128)(2,1)S(1)} %get-tuple-element.67), channel_id=1, source_target_pairs={{0,16},{16,32},{32,48},{48,64},{64,80},{80,96},{96,112},{1,17},{17... | collective-permute-start | bytes 786440 | tf_op jit(solution)/shard_map/ppermute | solution.py:612
  135.4 1.0 fusion.20
  136.5 0.7 collective-permute-done.5.bottom_ref
  137.2 1.5 collective-permute-done.4.top_ref
  138.8 6.0 %collective-permute-start.7 = (bf16[8,16,128]{2,1,0:T(8,128)(2,1)S(1)}, bf16[8,16,128]{2,1,0:T(8,128)(2,1)S(1)}, u32[]{:S(2)}, u32[]{:S(2)}) collective-permute-start(bf16[8,16,128]{2,1,0:T(8,128)(2,1)S(1)} %fusion.9), channel_id=1, source_target_pairs={{1,0},{2,1},{3,2},{4,3},{5,4},{6,5},{7,6},{8,7},{9,8},{10,9},{11,1... | collective-permute-start | bytes 98312 | tf_op jit(solution)/shard_map/ppermute | solution.py:620
  144.8 2.4 collective-permute-start.6
  147.2 1.0 collective-permute-done.6
  148.2 0.6 pad_maximum_fusion.1.side_ref
  148.9 12.9 %shard_map.209 = (bf16[1024,256]{1,0:T(8,128)(2,1)}, f32[2048,128]{1,0:T(8,128)}, f32[9,8,128]{2,1,0:T(8,128)}) custom-call(bf16[1024,256]{1,0:T(8,128)(2,1)} %bitcast.74, bf16[8,1024,128]{2,1,0:T(8,128)(2,1)} %get-tuple-element.36.lifted_ref, bf16[8,1024,128]{2,1,0:T(8,128)(2,1)} %get-tuple-element.37.slope_pre_ref, ...), custom_call_target="tpu_custom_call" | custom-call | tf_op jit(solution)/shard_map/pallas_call | solution.py:497
  161.7 4.2 %shard_map.210 = (bf16[64,72,128]{2,1,0:T(8,128)(2,1)}, f32[64,72,128]{2,1,0:T(8,128)}) custom-call(s32[1]{0:T(128)} %bitcast.45.core_ref, f32[4096,128]{1,0:T(8,128)} %get-tuple-element.51.block_ref, f32[2048,128]{1,0:T(8,128)} %get-tuple-element.52.grid_ref, f32[2048,128]{1,0:T(8,128)} %get-tuple-element.53.expand_ref, f32[9,8,128]{2,1,0:T(8,128)} %get-tuple-element.54.taps_ref), custom_call_target="tpu_custom_call" | custom-call | tf_op jit(solution)/shard_map/pallas_call | solution.py:497
  165.9 3.1 %collective-permute-done.8.got_ref = bf16[64,72,128]{2,1,0:T(8,128)(2,1)S(1)} collective-permute-done((bf16[64,72,128]{2,1,0:T(8,128)(2,1)}, bf16[64,72,128]{2,1,0:T(8,128)(2,1)S(1)}, u32[]{:S(2)}, u32[]{:S(2)}) %collective-permute-start.8) | collective-permute-done | bytes 1179680 | tf_op jit(solution)/shard_map/ppermute | solution.py:628
  169.0 1.0 copy-done.3
  170.0 3.2 %shard_map.211 = bf16[64,72,128]{2,1,0:T(8,128)(2,1)} custom-call(f32[64,72,128]{2,1,0:T(8,128)} %get-tuple-element.55.keep_ref, bf16[64,72,128]{2,1,0:T(8,128)(2,1)} %copy-done.3), custom_call_target="tpu_custom_call" | custom-call | tf_op jit(solution)/shard_map/pallas_call | solution.py:497
  173.2 30.5 %all_to_all.21.got_ref = bf16[64,72,128]{2,1,0:T(8,128)(2,1)} all-to-all(bf16[64,72,128]{2,1,0:T(8,128)(2,1)} %shard_map.211), channel_id=1, replica_groups=mesh['row'=8,'hi'=8,'core'=2] {'row','hi'}, dimensions={0} | all-to-all | bytes 2359296 | tf_op jit(solution)/shard_map/all_to_all | solution.py:624
  203.8 2.5 %shard_map.212 = bf16[64,72,128]{2,1,0:T(8,128)(2,1)} custom-call(bf16[64,72,128]{2,1,0:T(8,128)(2,1)} %all_to_all.21.got_ref), custom_call_target="tpu_custom_call" | custom-call | tf_op jit(solution)/shard_map/pallas_call | solution.py:497
  206.3 22.8 %all_to_all.22.mine_ref = bf16[64,72,128]{2,1,0:T(8,128)(2,1)S(1)} all-to-all(bf16[64,72,128]{2,1,0:T(8,128)(2,1)} %shard_map.212), channel_id=1, replica_groups=mesh['row'=8,'hi'=8,'core'=2] {'row','hi'}, dimensions={0} | all-to-all | bytes 2359296 | tf_op jit(solution)/shard_map/all_to_all | solution.py:624
  229.1 3.6 %collective-permute-start.9 = (bf16[64,72,128]{2,1,0:T(8,128)(2,1)S(1)}, bf16[64,72,128]{2,1,0:T(8,128)(2,1)S(1)}, u32[]{:S(2)}, u32[]{:S(2)}) collective-permute-start(bf16[64,72,128]{2,1,0:T(8,128)(2,1)S(1)} %all_to_all.22.mine_ref), channel_id=1, source_target_pairs={{0,1},{1,0},{2,3},{3,2},{4,5},{5,4},{6,7},{7,6},{8,9},{9,8},{10,11... | collective-permute-start | bytes 3538952 | tf_op jit(solution)/shard_map/ppermute | solution.py:628
  232.7 2.5 %collective-permute-done.9.other_ref = bf16[64,72,128]{2,1,0:T(8,128)(2,1)S(1)} collective-permute-done((bf16[64,72,128]{2,1,0:T(8,128)(2,1)S(1)}, bf16[64,72,128]{2,1,0:T(8,128)(2,1)S(1)}, u32[]{:S(2)}, u32[]{:S(2)}) %collective-permute-start.9) | collective-permute-done | bytes 1179680 | tf_op jit(solution)/shard_map/ppermute | solution.py:628
  235.2 1.0 copy-done.2
  236.2 4.0 %shard_map.213 = (f32[256,1024]{1,0:T(8,128)}, f32[9,1024]{1,0:T(8,128)}, f32[1024,256]{1,0:T(8,128)}, f32[256,768]{1,0:T(8,128)}, f32[256,256]{1,0:T(8,128)}, /*index=5*/f32[256,768]{1,0:T(8,128)}, f32[256,256]{1,0:T(8,128)}) custom-call(s32[1]{0:T(128)} %bitcast.45.core_ref, bf16[64,72,128]{2,1,0:T(8,128)(2,1)} %copy-done, bf16[64,72,128]{2,1,0:T(8,128)(2,1)} %copy-done.2), custom_call_target="tpu_custom_call" | custom-call | tf_op jit(solution)/shard_map/pallas_call | solution.py:497
  (50 shorter events, 1.6 us)
Async XLA Ops:
  1.5 7.8 %collective-permute-start.1 = (bf16[128,256]{1,0:T(8,128)(2,1)S(1)}, bf16[128,256]{1,0:T(8,128)(2,1)S(1)}, u32[]{:S(2)}, u32[]{:S(2)}) collective-permute-start(bf16[128,256]{1,0:T(8,128)(2,1)S(1)} %get-tuple-element.72), channel_id=1, source_target_pairs={{16,0},{32,16},{48,32},{64,48},{80,64},{96,80},{112,96},{17,1},{33... | collective-permute-start | bytes 196616 | tf_op jit(solution)/shard_map/ppermute | solution.py:612
  2.8 6.5 %collective-permute-start = (bf16[128,256]{1,0:T(8,128)(2,1)S(1)}, bf16[128,256]{1,0:T(8,128)(2,1)S(1)}, u32[]{:S(2)}, u32[]{:S(2)}) collective-permute-start(bf16[128,256]{1,0:T(8,128)(2,1)S(1)} %get-tuple-element.73), channel_id=1, source_target_pairs={{0,16},{16,32},{32,48},{48,64},{64,80},{80,96},{96,112},{1,17},{17... | collective-permute-start | bytes 196616 | tf_op jit(solution)/shard_map/ppermute | solution.py:612
  8.3 34.6 %copy-start.1 = (bf16[8,128,256]{2,1,0:T(8,128)(2,1)S(1)}, bf16[8,128,256]{2,1,0:T(8,128)(2,1)}, u32[]{:S(2)}) copy-start(bf16[8,128,256]{2,1,0:T(8,128)(2,1)} %param.16) | copy-start | bytes 1572868
  9.3 11.4 %copy-start.6 = (bf16[128,256]{1,0:T(8,128)(2,1)}, bf16[128,256]{1,0:T(8,128)(2,1)S(1)}, u32[]{:S(2)}) copy-start(bf16[128,256]{1,0:T(8,128)(2,1)S(1)} %collective-permute-done.1.bottom_ref) | copy-start | bytes 196612
  9.4 11.4 %copy-start.7 = (bf16[128,256]{1,0:T(8,128)(2,1)}, bf16[128,256]{1,0:T(8,128)(2,1)S(1)}, u32[]{:S(2)}) copy-start(bf16[128,256]{1,0:T(8,128)(2,1)S(1)} %collective-permute-done.top_ref) | copy-start | bytes 196612
  9.4 10.7 %collective-permute-start.3 = (bf16[16,256]{1,0:T(8,128)(2,1)S(1)}, bf16[16,256]{1,0:T(8,128)(2,1)S(1)}, u32[]{:S(2)}, u32[]{:S(2)}) collective-permute-start(bf16[16,256]{1,0:T(8,128)(2,1)S(1)} %fusion.19), channel_id=1, source_target_pairs={{1,0},{2,1},{3,2},{4,3},{5,4},{6,5},{7,6},{8,7},{9,8},{10,9},{11,1... | collective-permute-start | bytes 24584 | tf_op jit(solution)/shard_map/ppermute | solution.py:620
  12.6 7.5 %collective-permute-start.2 = (bf16[16,256]{1,0:T(8,128)(2,1)S(1)}, bf16[16,256]{1,0:T(8,128)(2,1)S(1)}, u32[]{:S(2)}, u32[]{:S(2)}) collective-permute-start(bf16[16,256]{1,0:T(8,128)(2,1)S(1)} %fusion.17), channel_id=1, source_target_pairs={{0,1},{1,2},{2,3},{3,4},{4,5},{5,6},{6,7},{7,8},{8,9},{9,10},{10,1... | collective-permute-start | bytes 24584 | tf_op jit(solution)/shard_map/ppermute | solution.py:620
  42.9 14.5 %copy-start.8 = (f32[8,225]{1,0:T(8,128)S(1)}, f32[8,225]{1,0:T(8,128)}, u32[]{:S(2)}) copy-start(f32[8,225]{1,0:T(8,128)} %param.29) | copy-start | bytes 21604
  45.0 29.0 %all-to-all-start = ((bf16[64,32,256]{2,1,0:T(8,128)(2,1)}), bf16[64,32,256]{2,1,0:T(8,128)(2,1)S(1)}, u32[]{:S(2)}, u32[]{:S(2)}) async-start(bf16[64,32,256]{2,1,0:T(8,128)(2,1)} %bitcast.24), calls=%async_computation | async-start | bytes 2097152 | tf_op jit(solution)/shard_map/all_to_all | solution.py:624
  130.1 7.1 %collective-permute-start.5 = (bf16[8,128,128]{2,1,0:T(8,128)(2,1)S(1)}, bf16[8,128,128]{2,1,0:T(8,128)(2,1)S(1)}, u32[]{:S(2)}, u32[]{:S(2)}) collective-permute-start(bf16[8,128,128]{2,1,0:T(8,128)(2,1)S(1)} %get-tuple-element.66), channel_id=1, source_target_pairs={{16,0},{32,16},{48,32},{64,48},{80,64},{96,80},{112,96},{17,1},{33... | collective-permute-start | bytes 786440 | tf_op jit(solution)/shard_map/ppermute | solution.py:612
  131.4 7.3 %collective-permute-start.4 = (bf16[8,128,128]{2,1,0:T(8,128)(2,1)S(1)}, bf16[8,128,128]{2,1,0:T(8,128)(2,1)S(1)}, u32[]{:S(2)}, u32[]{:S(2)}) collective-permute-start(bf16[8,128,128]{2,1,0:T(8,128)(2,1)S(1)} %get-tuple-element.67), channel_id=1, source_target_pairs={{0,16},{16,32},{32,48},{48,64},{64,80},{80,96},{96,112},{1,17},{17... | collective-permute-start | bytes 786440 | tf_op jit(solution)/shard_map/ppermute | solution.py:612
  137.2 11.6 %copy-start.4 = (bf16[8,128,128]{2,1,0:T(8,128)(2,1)}, bf16[8,128,128]{2,1,0:T(8,128)(2,1)S(1)}, u32[]{:S(2)}) copy-start(bf16[8,128,128]{2,1,0:T(8,128)(2,1)S(1)} %collective-permute-done.5.bottom_ref) | copy-start | bytes 786436
  138.7 10.1 %copy-start.5 = (bf16[8,128,128]{2,1,0:T(8,128)(2,1)}, bf16[8,128,128]{2,1,0:T(8,128)(2,1)S(1)}, u32[]{:S(2)}) copy-start(bf16[8,128,128]{2,1,0:T(8,128)(2,1)S(1)} %collective-permute-done.4.top_ref) | copy-start | bytes 786436
  138.8 8.5 %collective-permute-start.7 = (bf16[8,16,128]{2,1,0:T(8,128)(2,1)S(1)}, bf16[8,16,128]{2,1,0:T(8,128)(2,1)S(1)}, u32[]{:S(2)}, u32[]{:S(2)}) collective-permute-start(bf16[8,16,128]{2,1,0:T(8,128)(2,1)S(1)} %fusion.9), channel_id=1, source_target_pairs={{1,0},{2,1},{3,2},{4,3},{5,4},{6,5},{7,6},{8,7},{9,8},{10,9},{11,1... | collective-permute-start | bytes 98312 | tf_op jit(solution)/shard_map/ppermute | solution.py:620
  144.8 3.4 %collective-permute-start.6 = (bf16[8,16,128]{2,1,0:T(8,128)(2,1)S(1)}, bf16[8,16,128]{2,1,0:T(8,128)(2,1)S(1)}, u32[]{:S(2)}, u32[]{:S(2)}) collective-permute-start(bf16[8,16,128]{2,1,0:T(8,128)(2,1)S(1)} %fusion.7), channel_id=1, source_target_pairs={{0,1},{1,2},{2,3},{3,4},{4,5},{5,6},{6,7},{7,8},{8,9},{9,10},{10,1... | collective-permute-start | bytes 98312 | tf_op jit(solution)/shard_map/ppermute | solution.py:620
  165.9 3.1 %collective-permute-start.8 = (bf16[64,72,128]{2,1,0:T(8,128)(2,1)}, bf16[64,72,128]{2,1,0:T(8,128)(2,1)S(1)}, u32[]{:S(2)}, u32[]{:S(2)}) collective-permute-start(bf16[64,72,128]{2,1,0:T(8,128)(2,1)} %get-tuple-element.56), channel_id=1, source_target_pairs={{0,1},{1,0},{2,3},{3,2},{4,5},{5,4},{6,7},{7,6},{8,9},{9,8},{10,11... | collective-permute-start | bytes 3538952 | tf_op jit(solution)/shard_map/ppermute | solution.py:628
  169.0 1.0 copy-start.3
  229.1 6.1 %copy-start = (bf16[64,72,128]{2,1,0:T(8,128)(2,1)}, bf16[64,72,128]{2,1,0:T(8,128)(2,1)S(1)}, u32[]{:S(2)}) copy-start(bf16[64,72,128]{2,1,0:T(8,128)(2,1)S(1)} %all_to_all.22.mine_ref) | copy-start | bytes 3538948
  229.1 6.1 %collective-permute-start.9 = (bf16[64,72,128]{2,1,0:T(8,128)(2,1)S(1)}, bf16[64,72,128]{2,1,0:T(8,128)(2,1)S(1)}, u32[]{:S(2)}, u32[]{:S(2)}) collective-permute-start(bf16[64,72,128]{2,1,0:T(8,128)(2,1)S(1)} %all_to_all.22.mine_ref), channel_id=1, source_target_pairs={{0,1},{1,0},{2,3},{3,2},{4,5},{5,4},{6,7},{7,6},{8,9},{9,8},{10,11... | collective-permute-start | bytes 3538952 | tf_op jit(solution)/shard_map/ppermute | solution.py:628
  235.2 1.0 copy-start.2

commit v2 on v1

v2 whole, which is shorter than its diff:
```python
import functools

import jax
import jax.numpy as jnp
from jax import lax
from jax.experimental import pallas as pl
from jax.experimental.pallas import tpu as pltpu
from jax.sharding import Mesh
from jax.sharding import PartitionSpec as P

F32 = jnp.float32
BF16 = jnp.bfloat16
EPSILON = 1e-05
HEADS = 8
HEAD = 32
SCALE = HEAD ** (-0.5)
ROWS = 8
COLS = 128
TOKENS = ROWS * COLS
D = 256
E = 1024
BLOCKS = E // 128
LEFT = 8
WIDE = COLS + 2 * LEFT
GELU_1 = 0.7978845608028654
GELU_3 = 0.044715 * GELU_1


def dot(left, right, left_dim, right_dim):
    return lax.dot_general(
        left, right, (((left_dim,), (right_dim,)), ((), ())), preferred_element_type=F32
    )


def gelu_pair(values):
    square = values * values
    half = 0.5 + 0.5 * jnp.tanh(values * (GELU_1 + GELU_3 * square))
    value = values * half
    slope = half + value * (1.0 - half) * (2.0 * GELU_1 + (6.0 * GELU_3) * square)
    return value, slope


def norm_parts(values):
    centered = values - jnp.mean(values, axis=-1, keepdims=True)
    spread = jnp.mean(centered * centered, axis=-1, keepdims=True)
    inverse = lax.rsqrt(spread + EPSILON)
    return centered * inverse, inverse


def norm_back(values, gain, grad):
    unit, inverse = norm_parts(values)
    scaled = grad * gain
    mean_grad = jnp.mean(scaled, axis=-1, keepdims=True)
    mean_unit = jnp.mean(scaled * unit, axis=-1, keepdims=True)
    return inverse * (scaled - mean_grad - unit * mean_unit)


def four_windows(cells):
    return jnp.concatenate(
        [cells[:, 8 * m : 8 * m + 8, :].reshape(64, D) for m in range(4)], axis=0
    )


def from_four_windows(tokens):
    return jnp.concatenate(
        [tokens[64 * m : 64 * m + 64].reshape(8, 8, D) for m in range(4)], axis=1
    )


def load_kernel(*refs):
    count = (len(refs) - 4) // 2
    sources, targets = refs[:count], refs[count : 2 * count]
    left_ref, right_ref, sems, ends = refs[2 * count :]
    copies = [
        pltpu.make_async_copy(source, target, sems.at[k])
        for k, (source, target) in enumerate(zip(sources, targets))
    ]
    for copy in copies:
        copy.start()
    copies[0].wait()
    x_ref = targets[0]
    for row in range(ROWS):
        ends[0, row : row + 1, :] = x_ref[row, 0:16, :].astype(F32)[0:1]
        ends[1, row : row + 1, :] = x_ref[row, COLS - 16 : COLS, :].astype(F32)[15:16]
    left_ref[...] = ends[0].astype(BF16)
    right_ref[...] = ends[1].astype(BF16)
    for copy in copies[1:]:
        copy.wait()


def with_corners(cells, left, right):
    rest = jnp.zeros((14, cells.shape[1]), F32)
    corners = jnp.concatenate([left, right, rest], axis=0).astype(BF16)
    return jnp.concatenate([cells, corners], axis=0)


def x_edge_kernel(x_ref, left_ref, right_ref, first_ref, last_ref):
    left = left_ref[...].astype(F32)
    right = right_ref[...].astype(F32)
    for row, target in ((0, first_ref), (ROWS - 1, last_ref)):
        target[...] = with_corners(x_ref[row], left[row : row + 1], right[row : row + 1])


def inner_edge_kernel(outer_ref, middle_ref, left_ref, right_ref, first_ref, last_ref):
    for block in range(BLOCKS):
        left = left_ref[block].astype(F32)
        right = right_ref[block].astype(F32)
        for row, target in ((0, first_ref), (ROWS - 1, last_ref)):
            cells = whole_row(outer_ref[block, row], middle_ref[block, row])
            target[block] = with_corners(cells, left[row : row + 1], right[row : row + 1])


def whole_row(outer, middle):
    axis = outer.ndim - 2
    first = lax.slice_in_dim(outer, 0, 32, axis=axis)
    last = lax.slice_in_dim(outer, 32, 64, axis=axis)
    return jnp.concatenate([first, middle, last], axis=axis)


def bias_kernel(block_ref, grid_ref, bias_block_ref, bias_grid_ref, table):
    source = lax.broadcasted_iota(jnp.int32, (256, 1024), 0)
    place = lax.broadcasted_iota(jnp.int32, (256, 1024), 1)
    wanted = 15 * (place % 128 // 8) + 7 + place % 8 - place // 128
    onehot = jnp.where(source == wanted, 1.0, 0.0).astype(BF16)
    table[...] = jnp.zeros((2 * HEADS, 256), F32)
    table[0:HEADS, 0:225] = block_ref[...]
    table[HEADS : 2 * HEADS, 0:225] = grid_ref[...]
    rest = table[...]
    spread = jnp.zeros((2 * HEADS, 1024), F32)
    for _ in range(3):
        part = rest.astype(BF16)
        spread = spread + dot(part, onehot, 1, 0)
        rest = rest - part.astype(F32)
    for which, bias_ref in enumerate((bias_block_ref, bias_grid_ref)):
        for head in range(HEADS):
            line = HEADS * which + head
            rows = jnp.concatenate(
                [spread[line : line + 1, 128 * e : 128 * e + 128] for e in range(8)], axis=0
            )
            for a_k in range(8):
                start = 8 * (7 - a_k)
                bias_ref[
                    head // 4, 8 * a_k : 8 * a_k + 8, 64 * (head % 4) : 64 * (head % 4) + 64
                ] = rows[:, start : start + 64]


def stacked(part, heads_mask):
    return jnp.concatenate([part] * 4, axis=0) * heads_mask


def pick(product):
    lane = lax.broadcasted_iota(jnp.int32, (64, 128), 1)
    low = jnp.where(lane < 32, product[0:64], product[64:128])
    high = jnp.where(lane < 96, product[128:192], product[192:256])
    return jnp.where(lane < 64, low, high)


def softmax_keys(scores):
    shifted = jnp.exp(scores - jnp.max(scores, axis=0, keepdims=True))
    return shifted * (1.0 / jnp.sum(shifted, axis=0, keepdims=True))


def half_of(joined, part, half, group):
    start = part * D + half * 128
    return joined[64 * group : 64 * group + 64, start : start + 128]


PAIRS = [(group, half) for group in range(4) for half in range(2)]


def quarter(parts):
    return jnp.concatenate(
        [jnp.concatenate(parts[2 * g : 2 * g + 2], axis=1) for g in range(4)], axis=0
    )


def attend(joined, bias_ref, heads_mask):
    scores = [
        dot(half_of(joined, 1, h, g), stacked(half_of(joined, 0, h, g), heads_mask), 1, 1)
        for g, h in PAIRS
    ]
    probs = [softmax_keys(s * SCALE + bias_ref[h]) for s, (_, h) in zip(scores, PAIRS)]
    products = [dot(p.astype(BF16), half_of(joined, 2, h, g), 0, 0) for p, (g, h) in zip(probs, PAIRS)]
    return probs, quarter([pick(p).astype(BF16) for p in products])


def attend_back(joined, probs, grad_mix, heads_mask):
    stacks = [stacked(half_of(grad_mix, 0, h, g), heads_mask) for g, h in PAIRS]
    grad_weights = [
        dot(half_of(joined, 2, h, g), stack, 1, 1).astype(BF16).astype(F32)
        for stack, (g, h) in zip(stacks, PAIRS)
    ]
    grad_values = [dot(p.astype(BF16), stack, 1, 0) for p, stack in zip(probs, stacks)]
    grad_scores = []
    for p, w in zip(probs, grad_weights):
        centre = jnp.sum(w * p, axis=0, keepdims=True)
        grad_scores.append((p * (w - centre) * SCALE).astype(BF16))
    grad_keys = [
        dot(s, stacked(half_of(joined, 0, h, g), heads_mask), 1, 0)
        for s, (g, h) in zip(grad_scores, PAIRS)
    ]
    grad_queries = [
        pick(dot(s, half_of(joined, 1, h, g), 0, 0)) for s, (g, h) in zip(grad_scores, PAIRS)
    ]
    return jnp.concatenate(
        [quarter(grad_queries), quarter(grad_keys), quarter(grad_values)], axis=1
    ).astype(BF16)


def heads_mask_of():
    row = lax.broadcasted_iota(jnp.int32, (256, 128), 0) // 64
    lane = lax.broadcasted_iota(jnp.int32, (256, 128), 1) // HEAD
    return jnp.where(row == lane, 1.0, 0.0).astype(BF16)


def attention_totals(total_ref, normed_ref, grad_joined_ref, mixture_ref, grad_ref):
    for part in range(3):
        total = dot(normed_ref[...], grad_joined_ref[:, D * part : D * part + D], 0, 0)
        for k in range(2):
            start = 256 * (2 * part + k)
            total_ref[start : start + 256, :] = total[:, 128 * k : 128 * k + 128]
    total = dot(mixture_ref[...], grad_ref[...], 0, 0)
    for k in range(2):
        total_ref[1536 + 256 * k : 1792 + 256 * k, :] = total[:, 128 * k : 128 * k + 128]


def front_kernel(
    x_ref,
    top_ref,
    bottom_ref,
    left_ref,
    right_ref,
    scale_ref,
    shift_ref,
    w_expand_ref,
    dw_ref,
    w_project_ref,
    gain_block_ref,
    w_qkv_ref,
    w_out_ref,
    bias,
    gain_grid_ref,
    grad_output_ref,
    lifted_out,
    slope_pre_out,
    second_out,
    slope_conv_ref,
    section_one_ref,
    section_two_ref,
    send_ref,
    normed_block_out,
    joined_ref,
    probs_ref,
    mixture_out,
    pad,
    cells,
    outcome,
    lifted_ref,
    slope_pre_ref,
    second_ref,
    normed_block_ref,
    mixture_ref,
    sems,
):
    stores = [
        pltpu.make_async_copy(source, target, sems.at[k])
        for k, (source, target) in enumerate(
            (
                (lifted_ref, lifted_out),
                (slope_pre_ref, slope_pre_out),
                (second_ref, second_out),
                (normed_block_ref, normed_block_out),
                (mixture_ref, mixture_out),
            )
        )
    ]
    send_ref[:, 16:32, :] = grad_output_ref[...].reshape(64, 16, D)
    heads_mask = heads_mask_of()
    row_index = lax.axis_index("row")
    col_index = 2 * lax.axis_index("hi") + lax.axis_index("core")
    inside = [
        jnp.where(flag, 1.0, 0.0).astype(F32)
        for flag in (row_index > 0, row_index < 7, col_index > 0, col_index < 15)
    ]

    def shifted_of(tokens):
        return (tokens.astype(F32) * scale_ref[...] + shift_ref[...]).astype(BF16)

    for source, row, flag in ((top_ref, 0, inside[0]), (bottom_ref, 9, inside[1])):
        shifted = shifted_of(source[...])
        for pair in range(4):
            value, _ = gelu_pair(dot(shifted, w_expand_ref[:, 256 * pair : 256 * pair + 256], 1, 0))
            value = value.astype(BF16).astype(F32) * flag
            for k in range(2):
                block = 2 * pair + k
                part = value[:, 128 * k : 128 * k + 128]
                pad[block, row, LEFT : LEFT + COLS, :] = part[:COLS]
                pad[block, row, LEFT - 1 : LEFT, :] = part[COLS : COLS + 1] * inside[2]
                pad[block, row, LEFT + COLS : LEFT + COLS + 1, :] = (
                    part[COLS + 1 : COLS + 2] * inside[3]
                )
    shifted = shifted_of(jnp.concatenate([left_ref[...], right_ref[...]], axis=0))
    place = lax.broadcasted_iota(jnp.int32, (16, 1), 0)
    flags = jnp.where(place < 8, inside[2], inside[3])
    for pair in range(4):
        value, _ = gelu_pair(dot(shifted, w_expand_ref[:, 256 * pair : 256 * pair + 256], 1, 0))
        value = value.astype(BF16).astype(F32) * flags
        for k in range(2):
            block = 2 * pair + k
            part = value[:, 128 * k : 128 * k + 128]
            for row in range(ROWS):
                pad[block, row + 1, LEFT - 1 : LEFT, :] = part[row : row + 1]
                pad[block, row + 1, LEFT + COLS : LEFT + COLS + 1, :] = part[8 + row : 9 + row]

    @pl.loop(0, ROWS)
    def _(row):
        here = pl.ds(pl.multiple_of(row * COLS, COLS), COLS)
        shifted = shifted_of(x_ref[row])
        for pair in range(4):
            value, slope = gelu_pair(
                dot(shifted, w_expand_ref[:, 256 * pair : 256 * pair + 256], 1, 0)
            )
            value = value.astype(BF16)
            slope = slope.astype(BF16)
            for k in range(2):
                lanes = slice(128 * k, 128 * k + 128)
                lifted_ref[2 * pair + k, here, :] = value[:, lanes]
                slope_pre_ref[2 * pair + k, here, :] = slope[:, lanes]
                pad[2 * pair + k, row + 1, LEFT : LEFT + COLS, :] = value[:, lanes].astype(F32)

    stores[0].start()
    stores[1].start()

    @pl.loop(0, BLOCKS)
    def _(block):
        taps = [
            dw_ref[t : t + 1, pl.ds(pl.multiple_of(block * 128, 128), 128)] for t in range(9)
        ]

        @pl.loop(0, ROWS)
        def _(row):
            for chunk in range(4):
                summed = None
                for t in range(9):
                    start = LEFT - 1 + t % 3 + 32 * chunk
                    term = taps[t] * pad[block, row + t // 3, start : start + 32, :]
                    summed = term if summed is None else summed + term
                value, slope = gelu_pair(summed)
                here = pl.ds(pl.multiple_of(row * COLS + 32 * chunk, 32), 32)
                second_ref[block, here, :] = value.astype(BF16)
                slope_conv_ref[block, here, :] = slope.astype(BF16)

    stores[2].start()

    @pl.loop(0, 4)
    def _(part):
        here = pl.ds(pl.multiple_of(part * 256, 256), 256)
        summed = x_ref[pl.ds(2 * part, 2)].reshape(256, D).astype(F32)
        for pair in range(4):
            joined = jnp.concatenate(
                [second_ref[2 * pair, here, :], second_ref[2 * pair + 1, here, :]], axis=1
            )
            summed = summed + dot(joined, w_project_ref[256 * pair : 256 * pair + 256, :], 1, 0)
        section_one = summed.astype(BF16)
        section_one_ref[pl.ds(2 * part, 2)] = section_one.reshape(2, COLS, D)
        cells[pl.ds(2 * part, 2)] = section_one.astype(F32).reshape(2, COLS, D)

    @pl.loop(0, 4)
    def _(part):
        here = pl.ds(pl.multiple_of(part * 256, 256), 256)
        columns = pl.ds(pl.multiple_of(part * 32, 32), 32)
        section_one = four_windows(cells[:, columns, :])
        normed = (norm_parts(section_one)[0] * gain_block_ref[...]).astype(BF16)
        normed_block_ref[here, :] = normed
        joined = dot(normed, w_qkv_ref[...], 1, 0).astype(BF16)
        joined_ref[here, :] = joined
        probs, mixture = attend(joined, bias, heads_mask)
        for index in range(8):
            probs_ref[part * 8 + index] = probs[index]
        mixture_ref[here, :] = mixture
        section_two = (section_one + dot(mixture, w_out_ref[...], 1, 0)).astype(BF16).astype(F32)
        cells[:, columns, :] = from_four_windows(section_two)
        normed = norm_parts(section_two)[0] * gain_grid_ref[...]
        outcome[:, columns, :] = from_four_windows(normed)

    stores[3].start()
    stores[4].start()
    send_ref[:, 0:16, :] = outcome[...].astype(BF16).reshape(64, 16, D)
    section_two_ref[...] = cells[...].astype(BF16)
    for copy in stores:
        copy.wait()


def grid_kernel(
    got_ref,
    w_qkv_ref,
    w_out_ref,
    bias,
    grad_normed_ref,
    total_ref,
    mixture_ref,
    grad_joined_ref,
):
    heads_mask = heads_mask_of()
    normed_ref = got_ref.at[0]
    grad_ref = got_ref.at[1]

    @pl.loop(0, 4)
    def _(part):
        here = pl.ds(pl.multiple_of(part * 256, 256), 256)
        joined = dot(normed_ref[here, :], w_qkv_ref[...], 1, 0).astype(BF16)
        grad_mix = dot(grad_ref[here, :], w_out_ref[...], 1, 1).astype(BF16)
        probs, mixture = attend(joined, bias, heads_mask)
        mixture_ref[here, :] = mixture
        grad_joined = attend_back(joined, probs, grad_mix, heads_mask)
        grad_joined_ref[here, :] = grad_joined
        grad_normed_ref[here, :] = dot(grad_joined, w_qkv_ref[...], 1, 1).astype(BF16)

    attention_totals(total_ref, normed_ref, grad_joined_ref, mixture_ref, grad_ref)


def block_kernel(
    parts,
    returned_ref,
    grad_output_ref,
    section_two_ref,
    section_one_ref,
    joined_ref,
    probs_ref,
    slope_conv_ref,
    gain_grid_ref,
    gain_block_ref,
    w_qkv_ref,
    w_out_ref,
    w_project_ref,
    normed_block_in,
    mixture_in,
    *rest,
):
    normed_block_ref, mixture_ref, sems = rest[-3:]
    if len(rest) == 9:
        before_ref = None
        grad_one_ref, inner_ref, total_ref, left_ref, right_ref, ends = rest[:-3]
    else:
        before_ref, grad_one_ref, inner_ref, total_ref = rest[:-3]
    fetches = []
    for index, part in enumerate(parts):
        for k, (source, target) in enumerate(
            ((normed_block_in, normed_block_ref), (mixture_in, mixture_ref))
        ):
            fetches.append(
                pltpu.make_async_copy(
                    source.at[pl.ds(256 * part, 256), :],
                    target.at[pl.ds(256 * index, 256), :],
                    sems.at[2 * index + k],
                )
            )
            fetches[-1].start()
    heads_mask = heads_mask_of()
    all_windows = []
    all_joined = []
    for index, part in enumerate(parts):
        here = slice(256 * part, 256 * part + 256)
        columns = slice(32 * part, 32 * part + 32)
        out_columns = slice(32 * index, 32 * index + 32)

        def windows_of(ref):
            return four_windows(ref[:, columns, :].astype(F32))

        grad_two = windows_of(grad_output_ref) + norm_back(
            windows_of(section_two_ref), gain_grid_ref[...], windows_of(returned_ref)
        )
        grad_windows = grad_two.astype(BF16)
        grad_two = grad_windows.astype(F32)
        joined = joined_ref[here, :]
        grad_mix = dot(grad_windows, w_out_ref[...], 1, 1).astype(BF16)
        probs = [probs_ref[part * 8 + k] for k in range(8)]
        grad_joined = attend_back(joined, probs, grad_mix, heads_mask)
        all_windows.append(grad_windows)
        all_joined.append(grad_joined)
        grad_normed = dot(grad_joined, w_qkv_ref[...], 1, 1).astype(BF16).astype(F32)
        grad_one = grad_two + norm_back(
            windows_of(section_one_ref), gain_block_ref[...], grad_normed
        )
        grad_one = from_four_windows(grad_one).astype(BF16)
        grad_one_ref[:, out_columns, :] = grad_one
        grad_one = grad_one.reshape(256, D)
        for pair in range(4):
            through = dot(grad_one, w_project_ref[256 * pair : 256 * pair + 256, :], 1, 1)
            for k in range(2):
                block = 2 * pair + k
                slope = slope_conv_ref[block, :, columns, :].astype(F32)
                inner = through[:, 128 * k : 128 * k + 128].reshape(ROWS, 32, 128) * slope
                inner_ref[block, :, out_columns, :] = inner.astype(BF16)
                if before_ref is None:
                    side, column = (0, 0) if part == 0 else (1, 31)
                    for row in range(ROWS):
                        ends[side, block, row : row + 1, :] = inner[row, column : column + 1]
    if before_ref is None:
        left_ref[...] = ends[0].astype(BF16)
        right_ref[...] = ends[1].astype(BF16)
    for copy in fetches:
        copy.wait()
    joined = jnp.concatenate(all_joined, axis=0)
    windows = jnp.concatenate(all_windows, axis=0)
    products = [
        (normed_block_ref, joined[:, D * part : D * part + D], 512 * part) for part in range(3)
    ]
    for left, right, start in products + [(mixture_ref, windows, 1536)]:
        total = dot(left[...], right, 0, 0)
        for k in range(2):
            place = slice(start + 256 * k, start + 256 * k + 256)
            value = total[:, 128 * k : 128 * k + 128]
            total_ref[place, :] = value if before_ref is None else before_ref[place, :] + value


def total_kernel(
    core_ref,
    outer_ref,
    middle_ref,
    second_in,
    block_total_ref,
    grid_total_ref,
    grad_one_ref,
    early_send_ref,
    early_keep_ref,
    total_ref,
    second_ref,
    sem,
):
    fetch = pltpu.make_async_copy(second_in, second_ref, sem)
    fetch.start()
    grad_one = whole_row(outer_ref[...], middle_ref[...])
    grad_one_ref[...] = grad_one
    grad_one = grad_one.reshape(TOKENS, D)
    total_ref[0:2048, :] = block_total_ref[...]
    total_ref[4096:6144, :] = grid_total_ref[...]
    fetch.wait()
    for pair in range(4):
        joined = jnp.concatenate([second_ref[2 * pair], second_ref[2 * pair + 1]], axis=1)
        total = dot(joined, grad_one, 0, 0)
        for k in range(2):
            start = 2048 + 1024 * k + 256 * pair
            total_ref[start : start + 256, :] = total[:, 128 * k : 128 * k + 128]
    own = pl.ds(pl.multiple_of(core_ref[0] * 3072, 3072), 3072)
    other = pl.ds(pl.multiple_of((1 - core_ref[0]) * 3072, 3072), 3072)
    early_keep_ref[...] = total_ref[own, :].astype(BF16)
    early_send_ref[...] = total_ref[other, :].astype(BF16)


def back_kernel(
    core_ref,
    x_ref,
    lifted_in,
    slope_pre_in,
    outer_ref,
    middle_ref,
    top_ref,
    bottom_ref,
    left_ref,
    right_ref,
    scale_ref,
    shift_ref,
    dw_ref,
    _,
    preact_ref,
    late_send_ref,
    late_keep_ref,
    pad,
    shifted_ref,
    total_ref,
    taps_ref,
    lifted_ref,
    slope_pre_ref,
    sems,
):
    def fetches(block):
        return [
            pltpu.make_async_copy(source.at[block], target.at[block], sems.at[block, k])
            for k, (source, target) in enumerate(
                ((lifted_in, lifted_ref), (slope_pre_in, slope_pre_ref))
            )
        ]

    for block in range(BLOCKS):
        for copy in fetches(block):
            copy.start()
    for block in range(BLOCKS):
        for source, row in ((top_ref, 0), (bottom_ref, 9)):
            cells = source[block].astype(F32)
            pad[block, row, LEFT : LEFT + COLS, :] = cells[:COLS]
            pad[block, row, LEFT - 1 : LEFT, :] = cells[COLS : COLS + 1]
            pad[block, row, LEFT + COLS : LEFT + COLS + 1, :] = cells[COLS + 1 : COLS + 2]
        left = left_ref[block].astype(F32)
        right = right_ref[block].astype(F32)
        for row in range(ROWS):
            pad[block, row + 1, LEFT - 1 : LEFT, :] = left[row : row + 1]
            pad[block, row + 1, LEFT + COLS : LEFT + COLS + 1, :] = right[row : row + 1]

    @pl.loop(0, BLOCKS)
    def _(block):
        for copy in fetches(block):
            copy.wait()
        taps = [
            dw_ref[t : t + 1, pl.ds(pl.multiple_of(block * 128, 128), 128)] for t in range(9)
        ]

        @pl.loop(0, ROWS)
        def _(row):
            cells = whole_row(outer_ref[block, row], middle_ref[block, row])
            pad[block, row + 1, LEFT : LEFT + COLS, :] = cells.astype(F32)

        def step(row, totals):
            totals = list(totals)
            for chunk in range(4):
                here = pl.ds(pl.multiple_of(row * COLS + 32 * chunk, 32), 32)
                lifted = lifted_ref[block, here, :].astype(F32)
                summed = None
                for t in range(9):
                    start = LEFT + 1 - t % 3 + 32 * chunk
                    cells = pad[block, row + 2 - t // 3, start : start + 32, :]
                    term = taps[t] * cells
                    summed = term if summed is None else summed + term
                    totals[t] = totals[t] + jnp.sum((lifted * cells).reshape(4, 8, 128), axis=0)
                grad = summed * slope_pre_ref[block, here, :].astype(F32)
                preact_ref[block, here, :] = grad.astype(BF16)
            return tuple(totals)

        totals = lax.fori_loop(0, ROWS, step, (jnp.zeros((8, 128), F32),) * 9)
        for t in range(9):
            taps_ref[t, pl.ds(block, 1), :] = jnp.sum(totals[t], axis=0, keepdims=True)

    shifted_ref[...] = (
        x_ref[...].reshape(TOKENS, D).astype(F32) * scale_ref[...] + shift_ref[...]
    ).astype(BF16)
    for pair in range(4):
        joined = jnp.concatenate([preact_ref[2 * pair], preact_ref[2 * pair + 1]], axis=1)
        total = dot(shifted_ref[...], joined, 0, 0)
        for k in range(2):
            start = 256 * (2 * pair + k)
            total_ref[start : start + 256, :] = total[:, 128 * k : 128 * k + 128]
    own = pl.ds(pl.multiple_of(core_ref[0] * 1024, 1024), 1024)
    other = pl.ds(pl.multiple_of((1 - core_ref[0]) * 1024, 1024), 1024)
    for target, rows in ((late_keep_ref, own), (late_send_ref, other)):
        large = total_ref[rows, :].reshape(CHUNKS, 16, 128)
        for index in range(CHUNKS):
            taps = taps_ref[index] if index < 9 else jnp.zeros((8, 128), F32)
            target[index] = jnp.concatenate([large[index], taps], axis=0).astype(BF16)


def input_kernel(preact_ref, grad_one_ref, w_expand_ref, scale_ref, grad_input_ref):
    for part in range(4):
        here = slice(256 * part, 256 * part + 256)
        summed = jnp.zeros((256, D), F32)
        for pair in range(4):
            joined = jnp.concatenate(
                [preact_ref[2 * pair, here, :], preact_ref[2 * pair + 1, here, :]], axis=1
            )
            summed = summed + dot(joined, w_expand_ref[:, 256 * pair : 256 * pair + 256], 1, 1)
        grad_one = grad_one_ref[2 * part : 2 * part + 2].reshape(256, D).astype(F32)
        grad_input_ref[here, :] = (grad_one + summed * scale_ref[...]).astype(BF16)


VMEM = pl.BlockSpec(memory_space=pltpu.VMEM)
SMEM = pl.BlockSpec(memory_space=pltpu.SMEM)
HBM = pl.BlockSpec(memory_space=pltpu.HBM)


def shape(dims, kind):
    return jax.ShapeDtypeStruct(dims, kind)


def call(kernel, ins, outs, scratch, smem=(), far=(), far_out=(), keep=(), limit=16, flops=10**9):
    ins = [pltpu.with_memory_space_constraint(x, pltpu.HBM) if k in far else x for k, x in enumerate(ins)]
    specs = [SMEM if k in smem else HBM if k in far else VMEM for k in range(len(ins))]
    return pl.pallas_call(
        kernel,
        out_shape=[
            pltpu.VMEM(o.shape, o.dtype)
            if k in keep
            else pltpu.HBM(o.shape, o.dtype)
            if k in far_out
            else o
            for k, o in enumerate(outs)
        ],
        in_specs=specs,
        out_specs=[HBM if k in far_out else VMEM for k in range(len(outs))],
        scratch_shapes=scratch,
        compiler_params=pltpu.CompilerParams(vmem_limit_bytes=limit * 1024 * 1024),
        cost_estimate=pl.CostEstimate(flops=flops, bytes_accessed=flops // 100, transcendentals=0),
    )(*ins)


CHUNKS = 64
CHUNK = 72
FACTOR = float((64 * 2048) ** (-0.5))


def pair_kernel(early_keep_ref, early_got_ref, late_keep_ref, late_got_ref, parts_ref):
    early = early_keep_ref[...].astype(F32) + early_got_ref[...].astype(F32)
    early = early.reshape(CHUNKS, 48, 128)
    late = late_keep_ref[...].astype(F32) + late_got_ref[...].astype(F32)
    parts_ref[...] = jnp.concatenate([early, late], axis=1).astype(BF16)


def sum_kernel(got_ref, out_ref):
    def step(index, total):
        return total + got_ref[index].astype(F32)

    total = lax.fori_loop(0, CHUNKS, step, jnp.zeros((CHUNK, 128), F32), unroll=8)
    total = total.astype(BF16)
    for index in range(CHUNKS):
        out_ref[index] = total


def unpack_kernel(
    core_ref,
    mine_ref,
    other_ref,
    expand_ref,
    kernel_ref,
    project_ref,
    qkv_block_ref,
    out_block_ref,
    qkv_grid_ref,
    out_grid_ref,
):
    core = core_ref[0]

    targets = (
        [(qkv_block_ref, 0, 128 * k, 256) for k in range(6)]
        + [(out_block_ref, 0, 128 * k, 256) for k in range(2)]
        + [(project_ref, 0, 128 * k, 1024) for k in range(2)]
        + [(qkv_grid_ref, 0, 128 * k, 256) for k in range(6)]
        + [(out_grid_ref, 0, 128 * k, 256) for k in range(2)]
    )
    early = [
        (target, first + start, column)
        for target, first, column, count in targets
        for start in range(0, count, 16)
    ]

    def fill(low_ref, high_ref):
        for half, ref in enumerate((low_ref, high_ref)):
            for index in range(CHUNKS):
                value = ref[index].astype(F32) * FACTOR
                for k in range(3):
                    target, row, column = early[192 * half + 3 * index + k]
                    target[row : row + 16, column : column + 128] = value[16 * k : 16 * k + 16]
                start = 1024 * half + 16 * index
                column = start // 256 * 128
                expand_ref[start % 256 : start % 256 + 16, column : column + 128] = value[48:64]
                if half == 0 and index < 9:
                    for block in range(BLOCKS):
                        kernel_ref[index : index + 1, 128 * block : 128 * block + 128] = value[
                            64 + block : 65 + block
                        ]

    @pl.when(core == 0)
    def _():
        fill(mine_ref, other_ref)

    @pl.when(core == 1)
    def _():
        fill(other_ref, mine_ref)


def beside_rows(first, last):
    count = lax.axis_size("row")
    down = [(i, i + 1) for i in range(count - 1)]
    up = [(i + 1, i) for i in range(count - 1)]
    return lax.ppermute(last, "row", down), lax.ppermute(first, "row", up)


def beside_columns(first, last):
    axes = ("hi", "core")
    count = lax.axis_size("hi") * lax.axis_size("core")
    right = [(i, i + 1) for i in range(count - 1)]
    left = [(i + 1, i) for i in range(count - 1)]
    return lax.ppermute(last, axes, right), lax.ppermute(first, axes, left)


def across(values):
    return lax.all_to_all(values, ("row", "hi"), split_axis=0, concat_axis=0, tiled=True)


def sibling(values):
    return lax.ppermute(values, "core", [(0, 1), (1, 0)])


def shards(
    x_input,
    grad_output,
    in_scale,
    in_shift,
    w_expand,
    dw_kernel,
    w_project,
    gain_block,
    w_qkv_block,
    w_out_block,
    bias_block,
    gain_grid,
    w_qkv_grid,
    w_out_grid,
    bias_grid,
):
    core_flag = lax.axis_index("core").reshape(1).astype(jnp.int32)
    scale = in_scale.reshape(1, D)
    shift = in_shift.reshape(1, D)
    gain_block = gain_block.reshape(1, D)
    gain_grid = gain_grid.reshape(1, D)
    hidden = shape((BLOCKS, TOKENS, 128), BF16)
    hidden_vmem = pltpu.VMEM((BLOCKS, TOKENS, 128), BF16)
    tile = shape((ROWS, COLS, D), BF16)
    tokens = shape((TOKENS, D), BF16)
    tokens_vmem = pltpu.VMEM((TOKENS, D), BF16)
    edge_row = shape((144, D), BF16)
    edge_column = shape((ROWS, D), BF16)
    large = [
        x_input,
        w_expand,
        grad_output,
        w_project,
        w_qkv_block,
        w_out_block,
        w_qkv_grid,
        w_out_grid,
        dw_kernel,
    ]
    (
        x_input,
        w_expand,
        grad_output,
        w_project,
        w_qkv_block,
        w_out_block,
        w_qkv_grid,
        w_out_grid,
        dw_kernel,
        x_left,
        x_right,
    ) = call(
        load_kernel,
        large,
        [shape(v.shape, v.dtype) for v in large] + [edge_column, edge_column],
        [pltpu.SemaphoreType.DMA((len(large),)), pltpu.VMEM((2, ROWS, D), F32)],
        far=range(len(large)),
        keep=range(len(large) + 2),
        limit=4,
    )
    x_left, x_right = beside_columns(x_left, x_right)
    cube = shape((2, 64, 256), F32)
    cube_block, cube_grid = call(
        bias_kernel,
        [bias_block, bias_grid],
        [cube, cube],
        [pltpu.VMEM((2 * HEADS, 256), F32)],
        keep=(0, 1),
        limit=8,
    )
    x_first, x_last = call(
        x_edge_kernel,
        [x_input, x_left, x_right],
        [edge_row, edge_row],
        [],
        keep=(0, 1),
        limit=4,
    )
    x_top, x_bottom = beside_rows(x_first, x_last)
    (
        lifted,
        slope_pre,
        second,
        slope_conv,
        section_one,
        section_two,
        sendable,
        normed_block,
        joined,
        probs,
        mixture,
    ) = call(
        front_kernel,
        [
            x_input,
            x_top,
            x_bottom,
            x_left,
            x_right,
            scale,
            shift,
            w_expand,
            dw_kernel,
            w_project,
            gain_block,
            w_qkv_block,
            w_out_block,
            cube_block,
            gain_grid,
            grad_output,
        ],
        [
            hidden,
            hidden,
            hidden,
            hidden,
            tile,
            tile,
            shape((64, 32, D), BF16),
            tokens,
            shape((TOKENS, 3 * D), BF16),
            shape((32, 64, 256), F32),
            tokens,
        ],
        [
            pltpu.VMEM((BLOCKS, ROWS + 2, WIDE, 128), F32),
            pltpu.VMEM((ROWS, COLS, D), F32),
            pltpu.VMEM((ROWS, COLS, D), F32),
            hidden_vmem,
            hidden_vmem,
            hidden_vmem,
            tokens_vmem,
            tokens_vmem,
            pltpu.SemaphoreType.DMA((5,)),
        ],
        keep=(3, 4, 5, 6, 8, 9),
        far_out=(0, 1, 2, 7, 10),
        limit=24,
    )

    got = across(sendable).transpose(1, 0, 2).reshape(2, TOKENS, D)
    grad_groups, grid_total = call(
        grid_kernel,
        [got, w_qkv_grid, w_out_grid, cube_grid],
        [tokens, shape((2048, 128), F32)],
        [tokens_vmem, pltpu.VMEM((TOKENS, 3 * D), BF16)],
        keep=(0, 1),
        limit=8,
    )
    returned = across(grad_groups.reshape(16, 64, D).transpose(1, 0, 2)).reshape(ROWS, COLS, D)

    def block_half(parts, before):
        edge = [] if before else [shape((BLOCKS, ROWS, 128), BF16)] * 2
        half_vmem = pltpu.VMEM((TOKENS // 2, D), BF16)
        return call(
            functools.partial(block_kernel, parts),
            [
                returned,
                grad_output,
                section_two,
                section_one,
                joined,
                probs,
                slope_conv.reshape(BLOCKS, ROWS, COLS, 128),
                gain_grid,
                gain_block,
                w_qkv_block,
                w_out_block,
                w_project,
                normed_block,
                mixture,
            ]
            + before,
            [
                shape((ROWS, COLS // 2, D), BF16),
                shape((BLOCKS, ROWS, COLS // 2, 128), BF16),
                shape((2048, 128), F32),
            ]
            + edge,
            ([] if before else [pltpu.VMEM((2, BLOCKS, ROWS, 128), F32)])
            + [half_vmem, half_vmem, pltpu.SemaphoreType.DMA((4,))],
            far=(12, 13),
            keep=range(3 + len(edge)),
            limit=8,
            flops=4*10**9,
        )

    one_outer, inner_outer, block_total, left, right = block_half((0, 3), [])
    left, right = beside_columns(left, right)
    one_middle, inner_middle, block_total = block_half((1, 2), [block_total])
    edge_cells = shape((BLOCKS, 144, 128), BF16)
    first, last = call(
        inner_edge_kernel,
        [inner_outer, inner_middle, left, right],
        [edge_cells, edge_cells],
        [],
        keep=(0, 1),
        limit=4,
    )
    top, bottom = beside_rows(first, last)
    early = shape((3072, 128), BF16)
    grad_one, early_send, early_keep = call(
        total_kernel,
        [core_flag, one_outer, one_middle, second, block_total, grid_total],
        [tile, early, early],
        [pltpu.VMEM((6144, 128), F32), hidden_vmem, pltpu.SemaphoreType.DMA],
        smem=(0,),
        far=(3,),
        keep=range(3),
        limit=8,
        flops=3*10**9,
    )
    early_got = sibling(early_send)
    late = shape((CHUNKS, 24, 128), BF16)
    parts = shape((CHUNKS, CHUNK, 128), BF16)
    preact, late_send, late_keep = call(
        back_kernel,
        [
            core_flag,
            x_input,
            lifted,
            slope_pre,
            inner_outer,
            inner_middle,
            top,
            bottom,
            left,
            right,
            scale,
            shift,
            dw_kernel,
            early_keep,
        ],
        [hidden, late, late],
        [
            pltpu.VMEM((BLOCKS, ROWS + 2, WIDE, 128), F32),
            tokens_vmem,
            pltpu.VMEM((2048, 128), F32),
            pltpu.VMEM((9, BLOCKS, 128), F32),
            hidden_vmem,
            hidden_vmem,
            pltpu.SemaphoreType.DMA((BLOCKS, 2)),
        ],
        smem=(0,),
        far=(2, 3),
        keep=(0, 1, 2),
        limit=20,
        flops=10**10,
    )
    (grad_input,) = call(
        input_kernel, [preact, grad_one, w_expand, scale], [tokens], [], limit=8
    )

    (paired,) = call(
        pair_kernel,
        [early_keep, early_got, late_keep, sibling(late_send)],
        [parts],
        [],
        keep=(0,),
        limit=4,
    )
    (summed,) = call(sum_kernel, [across(paired)], [parts], [], keep=(0,), limit=4)
    mine = across(summed)
    totals = call(
        unpack_kernel,
        [core_flag, mine, sibling(mine)],
        [
            shape((D, E), F32),
            shape((9, E), F32),
            shape((E, D), F32),
            shape((D, 3 * D), F32),
            shape((D, D), F32),
            shape((D, 3 * D), F32),
            shape((D, D), F32),
        ],
        [],
        smem=(0,),
        limit=16,
    )
    return (grad_input.reshape(ROWS, COLS, D), *totals)


def solution(mesh):
    split = Mesh(mesh.devices.reshape(8, 8, 2), ("row", "hi", "core"))
    tile = P("row", ("hi", "core"), None)
    return jax.shard_map(
        shards,
        mesh=split,
        in_specs=(tile, tile) + (P(),) * 13,
        out_specs=(tile,) + (P(),) * 7,
        check_vma=False,
    )
```

time: 241 us -> 197 us (0.82)
  Pallas kernels: 83.8 us -> 50.7 us
  blocking collectives: 70.6 us -> 98.8 us
  starting transfers between devices: 44.3 us -> 27.8 us
  waiting for transfers between devices: 23.7 us -> 11.7 us
  local copies, waits for them, and re-layouts: 12.9 us -> 5.98 us
  other arithmetic: 4.01 us -> 0 us
    pallas_call x8 -> x14, Pallas kernels: 83.8 us -> 50.7 us  [call(): pl.pallas_call(kernel, out_shape=[pltpu.VMEM(o.shape, o.dtype) if k in ke...]
    all_to_all x3 -> x4, blocking collectives: 70.6 us -> 98.8 us  [across(): lax.all_to_all(values, ('row', 'hi'), split_axis=0, concat_axis=0, tiled=...]
    all_to_all x1 -> x0, waiting for transfers between devices: 15 us -> none  [across(): lax.all_to_all(values, ('row', 'hi'), split_axis=0, concat_axis=0, tiled=...]
    all_to_all x1 -> x0, starting transfers between devices: 12.4 us -> none  [across(): lax.all_to_all(values, ('row', 'hi'), split_axis=0, concat_axis=0, tiled=...]
    ppermute x4, waiting for transfers between devices: 1 us -> 4.5 us  [beside_columns(): return (lax.ppermute(last, axes, right), lax.ppermute(first, axes, left))]
    slice x9 -> x0, local copies, waits for them, and re-layouts: 3.26 us -> none  [the longest x1 1.04 us: shards(): got[1]]
    ppermute x4, starting transfers between devices: 11.2 us -> 8.02 us  [beside_rows(): return (lax.ppermute(last, 'row', down), lax.ppermute(first, 'row', up))]
    unnamed x22 -> x32, local copies, waits for them, and re-layouts: 2.09 us -> 5.1 us
  transfers between devices with their start and end apart: 11 -> 11, of which waited for: 6 -> 5; matrix products, arithmetic and copies ran while one was open for 3% -> 0% of each run, Pallas kernels for 0% -> 9%
where the time goes in v2:
time: 197 us; the launch traced here: 196 us
  blocking collectives  98.8 us (50%)
  Pallas kernels  50.7 us (26%)
  starting transfers between devices  27.8 us (14%)
  waiting for transfers between devices  11.7 us (6%)
  local copies, waits for them, and re-layouts  5.98 us (3%)
    all_to_all x4, blocking collectives, across(): lax.all_to_all(values, ('row', 'hi'), split_axis=0, concat_axis=0, tiled=...  98.8 us
    pallas_call x14, Pallas kernels, call(): pl.pallas_call(kernel, out_shape=[pltpu.VMEM(o.shape, o.dtype) if k in ke...  50.7 us
    ppermute x4, starting transfers between devices, beside_columns(): return (lax.ppermute(last, axes, right), lax.ppermute(first, axes, left))  16 us
    ppermute x4, starting transfers between devices, beside_rows(): return (lax.ppermute(last, 'row', down), lax.ppermute(first, 'row', up))  8.02 us
    unnamed x32, local copies, waits for them, and re-layouts  5.1 us
    ppermute x4, waiting for transfers between devices, beside_rows(): return (lax.ppermute(last, 'row', down), lax.ppermute(first, 'row', up))  4.54 us
    ppermute x4, waiting for transfers between devices, beside_columns(): return (lax.ppermute(last, axes, right), lax.ppermute(first, axes, left))  4.5 us
  transfers between devices with their start and end apart: 11, of which 5 were waited for; matrix products, arithmetic and copies ran while one was open for 0% of the time, Pallas kernels for 9%

profile of v2, /device:TPU:1, one launch (start us, length us, event | category | flops | bytes accessed | tf_op | source)
XLA Modules:
  0.0 195.9 jit_solution(4177497169569663148)
XLA Ops:
  0.6 1.9 shard_map.206
  2.5 0.0 copy-start
  2.6 0.0 copy-start.1
  2.6 6.9 %collective-permute-start = (bf16[8,256]{1,0:T(8,128)(2,1)S(1)}, bf16[8,256]{1,0:T(8,128)(2,1)S(1)}, u32[]{:S(2)}, u32[]{:S(2)}) collective-permute-start(bf16[8,256]{1,0:T(8,128)(2,1)S(1)} %get-tuple-element.60), channel_id=1, source_target_pairs={{0,1},{1,2},{2,3},{3,4},{4,5},{5,6},{6,7},{7,8},{8,9},{9,10},{10,1... | collective-permute-start | bytes 12296 | tf_op jit(solution)/shard_map/ppermute | solution.py:780
  9.5 1.9 collective-permute-start.1
  11.4 4.5 %collective-permute-done.1.right_ref = bf16[8,256]{1,0:T(8,128)(2,1)S(1)} collective-permute-done((bf16[8,256]{1,0:T(8,128)(2,1)S(1)}, bf16[8,256]{1,0:T(8,128)(2,1)S(1)}, u32[]{:S(2)}, u32[]{:S(2)}) %collective-permute-start.1) | collective-permute-done | bytes 4128 | tf_op jit(solution)/shard_map/ppermute | solution.py:780
  15.9 0.0 copy-start.2
  15.9 0.0 copy-start.3
  15.9 0.0 copy-start.4
  16.0 0.0 copy-start.5
  16.0 3.3 %collective-permute-start.2 = (bf16[144,256]{1,0:T(8,128)(2,1)S(1)}, bf16[144,256]{1,0:T(8,128)(2,1)S(1)}, u32[]{:S(2)}, u32[]{:S(2)}) collective-permute-start(bf16[144,256]{1,0:T(8,128)(2,1)S(1)} %get-tuple-element.62), channel_id=1, source_target_pairs={{0,16},{16,32},{32,48},{48,64},{64,80},{80,96},{96,112},{1,17},{17... | collective-permute-start | bytes 221192 | tf_op jit(solution)/shard_map/ppermute | solution.py:772
  19.3 1.3 collective-permute-start.3
  20.6 0.6 shard_map.208
  21.2 3.2 %collective-permute-done.3.bottom_ref = bf16[144,256]{1,0:T(8,128)(2,1)S(1)} collective-permute-done((bf16[144,256]{1,0:T(8,128)(2,1)S(1)}, bf16[144,256]{1,0:T(8,128)(2,1)S(1)}, u32[]{:S(2)}, u32[]{:S(2)}) %collective-permute-start.3) | collective-permute-done | bytes 73760 | tf_op jit(solution)/shard_map/ppermute | solution.py:772
  24.4 16.4 %shard_map.209 = (bf16[8,1024,128]{2,1,0:T(8,128)(2,1)}, bf16[8,1024,128]{2,1,0:T(8,128)(2,1)}, bf16[8,1024,128]{2,1,0:T(8,128)(2,1)}, bf16[8,1024,128]{2,1,0:T(...) custom-call(bf16[8,128,256]{2,1,0:T(8,128)(2,1)S(1)} %get-tuple-elem, ...), custom_call_target="tpu_custom_call" | custom-call | flops 1000000000 | bytes 10000000 | tf_op jit(solution)/shard_map/pallas_call | solution.py:676
  40.9 28.3 %all_to_all.20 = bf16[64,32,256]{2,1,0:T(8,128)(2,1)S(1)} all-to-all(bf16[64,32,256]{2,1,0:T(8,128)(2,1)S(1)} %get-tuple-element.73), channel_id=1, replica_groups=mesh['row'=8,'hi'=8,'core'=2] {'row','hi'}, dimensions={0} | all-to-all | bytes 2097152 | tf_op jit(solution)/shard_map/all_to_all | solution.py:784
  69.2 0.6 copy.23
  69.8 7.0 %shard_map.210 = (bf16[1024,256]{1,0:T(8,128)(2,1)S(1)}, f32[2048,128]{1,0:T(8,128)S(1)}) custom-call(bf16[2,1024,256]{2,1,0:T(8,128)(2,1)S(1)} %bitcast.14, bf16[256,768]{1,0:T(8,128)(2,1)S(1)} %get-tuple-element.74.w_qkv_ref, bf16[256,256]{1,0:T(8,128)(2,1)S(1)} %get-tuple-element.75.w_out_ref, f32[2,64,256]{2,1,0:T(8,128)S(1)} %get-tuple-element.76.bias), custom_call_target="tpu_custom_call" | custom-call | flops 1000000000 | bytes 10000000 | tf_op jit(solution)/shard_map/pallas_call | solution.py:676
  76.8 0.3 copy.26
  77.1 16.7 %all_to_all.21 = bf16[64,16,256]{2,1,0:T(8,128)(2,1)S(1)} all-to-all(bf16[64,16,256]{2,1,0:T(8,128)(2,1)S(1)} %bitcast.32), channel_id=1, replica_groups=mesh['row'=8,'hi'=8,'core'=2] {'row','hi'}, dimensions={0} | all-to-all | bytes 1048576 | tf_op jit(solution)/shard_map/all_to_all | solution.py:784
  93.8 4.6 %shard_map.211 = (bf16[8,64,256]{2,1,0:T(8,128)(2,1)S(1)}, bf16[8,8,64,128]{3,2,1,0:T(8,128)(2,1)S(1)}, f32[2048,128]{1,0:T(8,128)S(1)}, bf16[8,8,128]{2,1,0:T(8,128)(2,1)S(1)}, bf16[8,8,128]{2,1,0:T(8,128)(2,1)S(1)}) custom-call(bf16[8,128,256]{2,1,0:T(8,128)(2,1)S(1)} %bitcast.15, bf16[8,128,256]{2,1,0:T(8,128)(2,1)S(1)} %get-tuple-element.70.grad_output_ref, ...), custom_call_target="tpu_custom_call" | custom-call | flops 4000000000 | bytes 40000000 | tf_op jit(solution)/shard_map/pallas_call | solution.py:676
  98.5 0.0 copy-start.14
  98.5 0.7 copy-done.14
  99.2 5.1 %collective-permute-start.4 = (bf16[8,8,128]{2,1,0:T(8,128)(2,1)S(1)}, bf16[8,8,128]{2,1,0:T(8,128)(2,1)S(1)}, u32[]{:S(2)}, u32[]{:S(2)}) collective-permute-start(bf16[8,8,128]{2,1,0:T(8,128)(2,1)S(1)} %get-tuple-element.88), channel_id=1, source_target_pairs={{0,1},{1,2},{2,3},{3,4},{4,5},{5,6},{6,7},{7,8},{8,9},{9,10},{10,1... | collective-permute-start | bytes 49160 | tf_op jit(solution)/shard_map/ppermute | solution.py:780
  104.3 2.1 %collective-permute-start.5 = (bf16[8,8,128]{2,1,0:T(8,128)(2,1)S(1)}, bf16[8,8,128]{2,1,0:T(8,128)(2,1)S(1)}, u32[]{:S(2)}, u32[]{:S(2)}) collective-permute-start(bf16[8,8,128]{2,1,0:T(8,128)(2,1)S(1)} %get-tuple-element.89), channel_id=1, source_target_pairs={{1,0},{2,1},{3,2},{4,3},{5,4},{6,5},{7,6},{8,7},{9,8},{10,9},{11,1... | collective-permute-start | bytes 49160 | tf_op jit(solution)/shard_map/ppermute | solution.py:780
  106.4 4.7 %shard_map.212 = (bf16[8,64,256]{2,1,0:T(8,128)(2,1)S(1)}, bf16[8,8,64,128]{3,2,1,0:T(8,128)(2,1)S(1)}, f32[2048,128]{1,0:T(8,128)S(1)}) custom-call(bf16[8,128,256]{2,1,0:T(8,128)(2,1)S(1)} %bitcast.16, bf16[8,128,256]{2,1,0:T(8,128)(2,1)S(1)} %get-tuple-element.70.grad_output_ref, bf16[8,128,256]{2,1,0:T(8,128)(2,1)S(1)} %get-tuple-element.78.section_two_ref, ...), custom_call_target="tpu_custom_call" | custom-call | flops 4000000000 | bytes 40000000 | tf_op jit(solution)/shard_map/pallas_call | solution.py:676
  111.1 0.0 copy-start.6
  111.1 0.1 shard_map.213
  111.2 2.1 %collective-permute-start.6 = (bf16[8,144,128]{2,1,0:T(8,128)(2,1)S(1)}, bf16[8,144,128]{2,1,0:T(8,128)(2,1)S(1)}, u32[]{:S(2)}, u32[]{:S(2)}) collective-permute-start(bf16[8,144,128]{2,1,0:T(8,128)(2,1)S(1)} %get-tuple-element.90), channel_id=1, source_target_pairs={{0,16},{16,32},{32,48},{48,64},{64,80},{80,96},{96,112},{1,17},{17... | collective-permute-start | bytes 884744 | tf_op jit(solution)/shard_map/ppermute | solution.py:772
  113.3 1.3 collective-permute-start.7
  114.7 1.2 copy-done.9
  115.9 1.2 copy-done.11
  117.1 0.9 copy-done.13
  118.1 0.9 copy-done.15
  119.0 2.6 %shard_map.214 = (bf16[8,128,256]{2,1,0:T(8,128)(2,1)S(1)}, bf16[3072,128]{1,0:T(8,128)(2,1)S(1)}, bf16[3072,128]{1,0:T(8,128)(2,1)S(1)}) custom-call(s32[1]{0:T(128)} %bitcast.core_ref, bf16[8,64,256]{2,1,0:T(8,128)(2,1)S(1)} %copy-done.15, bf16[8,64,256]{2,1,0:T(8,128)(2,1)S(1)} %copy-done.13, bf16[8,1024,128]{2,1,0:T(8,128)(2,1)} %get-tuple-element.94.second_in, ...), custom_call_target="tpu_custom_call" | custom-call | flops 3000000000 | bytes 30000000 | tf_op jit(solution)/shard_map/pallas_call | solution.py:676
  121.6 0.1 collective-permute-start.8
  121.7 1.4 collective-permute-done.7.bottom_ref
  123.1 8.3 %shard_map.215 = (bf16[8,1024,128]{2,1,0:T(8,128)(2,1)S(1)}, bf16[64,24,128]{2,1,0:T(8,128)(2,1)S(1)}, bf16[64,24,128]{2,1,0:T(8,128)(2,1)S(1)}) custom-call(s32[1]{0:T(128)} %bitcast.core_ref, bf16[8,128,256]{2,1,0:T(8,128)(2,1)S(1)} %get-tuple-element.59.x_ref, bf16[8,1024,128]{2,1,0:T(8,128)(2,1)} %get-tuple-element.71.lifted_in, ...), custom_call_target="tpu_custom_call" | custom-call | flops 10000000000 | bytes 100000000 | tf_op jit(solution)/shard_map/pallas_call | solution.py:676
  131.4 0.1 collective-permute-start.9
  131.5 1.7 collective-permute-done.9.late_got_ref
  133.2 0.3 shard_map.217
  133.5 31.1 %all_to_all.22.got_ref = bf16[64,72,128]{2,1,0:T(8,128)(2,1)S(1)} all-to-all(bf16[64,72,128]{2,1,0:T(8,128)(2,1)S(1)} %shard_map.217), channel_id=1, replica_groups=mesh['row'=8,'hi'=8,'core'=2] {'row','hi'}, dimensions={0} | all-to-all | bytes 2359296 | tf_op jit(solution)/shard_map/all_to_all | solution.py:784
  164.6 0.3 shard_map.218
  164.8 22.6 %all_to_all.23.mine_ref = bf16[64,72,128]{2,1,0:T(8,128)(2,1)S(1)} all-to-all(bf16[64,72,128]{2,1,0:T(8,128)(2,1)S(1)} %shard_map.218), channel_id=1, replica_groups=mesh['row'=8,'hi'=8,'core'=2] {'row','hi'}, dimensions={0} | all-to-all | bytes 2359296 | tf_op jit(solution)/shard_map/all_to_all | solution.py:784
  187.5 3.6 %collective-permute-start.10 = (bf16[64,72,128]{2,1,0:T(8,128)(2,1)S(1)}, bf16[64,72,128]{2,1,0:T(8,128)(2,1)S(1)}, u32[]{:S(2)}, u32[]{:S(2)}) collective-permute-start(bf16[64,72,128]{2,1,0:T(8,128)(2,1)S(1)} %all_to_all.23.mine_ref), channel_id=1, source_target_pairs={{0,1},{1,0},{2,3},{3,2},{4,5},{5,4},{6,7},{7,6},{8,9},{9,8},{10,11... | collective-permute-start | bytes 3538952 | tf_op jit(solution)/shard_map/ppermute | solution.py:788
  191.1 1.6 shard_map.216
  192.6 0.9 collective-permute-done.10.other_ref
  193.6 2.4 %shard_map.219 = (f32[256,1024]{1,0:T(8,128)}, f32[9,1024]{1,0:T(8,128)}, f32[1024,256]{1,0:T(8,128)}, f32[256,768]{1,0:T(8,128)}, f32[256,256]{1,0:T(8,128)}, /*index=5*/f32[256,768]{1,0:T(8,128)}, f32[256,256]{1,0:T(8,128)}) custom-call(s32[1]{0:T(128)} %bitcast.core_ref, bf16[64,72,128]{2,1,0:T(8,128)(2,1)S(1)} %all_to_all.23.mine_ref, ...), custom_call_target="tpu_custom_call" | custom-call | flops 1000000000 | bytes 10000000 | tf_op jit(solution)/shard_map/pallas_call | solution.py:676
  (26 shorter events, 0.1 us)
Async XLA Ops:
  2.5 18.1 %copy-start = (f32[8,225]{1,0:T(8,128)S(1)}, f32[8,225]{1,0:T(8,128)}, u32[]{:S(2)}) copy-start(f32[8,225]{1,0:T(8,128)} %block_ref.1) | copy-start | bytes 21604
  2.6 18.1 %copy-start.1 = (f32[8,225]{1,0:T(8,128)S(1)}, f32[8,225]{1,0:T(8,128)}, u32[]{:S(2)}) copy-start(f32[8,225]{1,0:T(8,128)} %grid_ref.1) | copy-start | bytes 21604
  2.6 8.8 %collective-permute-start = (bf16[8,256]{1,0:T(8,128)(2,1)S(1)}, bf16[8,256]{1,0:T(8,128)(2,1)S(1)}, u32[]{:S(2)}, u32[]{:S(2)}) collective-permute-start(bf16[8,256]{1,0:T(8,128)(2,1)S(1)} %get-tuple-element.60), channel_id=1, source_target_pairs={{0,1},{1,2},{2,3},{3,4},{4,5},{5,6},{6,7},{7,8},{8,9},{9,10},{10,1... | collective-permute-start | bytes 12296 | tf_op jit(solution)/shard_map/ppermute | solution.py:780
  9.5 6.4 %collective-permute-start.1 = (bf16[8,256]{1,0:T(8,128)(2,1)S(1)}, bf16[8,256]{1,0:T(8,128)(2,1)S(1)}, u32[]{:S(2)}, u32[]{:S(2)}) collective-permute-start(bf16[8,256]{1,0:T(8,128)(2,1)S(1)} %get-tuple-element.61), channel_id=1, source_target_pairs={{1,0},{2,1},{3,2},{4,3},{5,4},{6,5},{7,6},{8,7},{9,8},{10,9},{11,1... | collective-permute-start | bytes 12296 | tf_op jit(solution)/shard_map/ppermute | solution.py:780
  15.9 8.5 %copy-start.2 = (f32[256]{0:T(256)S(1)}, f32[256]{0:T(256)}, u32[]{:S(2)}) copy-start(f32[256]{0:T(256)} %param.22) | copy-start | bytes 3076
  15.9 8.5 %copy-start.3 = (f32[256]{0:T(256)S(1)}, f32[256]{0:T(256)}, u32[]{:S(2)}) copy-start(f32[256]{0:T(256)} %param.26) | copy-start | bytes 3076
  15.9 8.5 %copy-start.4 = (f32[256]{0:T(256)S(1)}, f32[256]{0:T(256)}, u32[]{:S(2)}) copy-start(f32[256]{0:T(256)} %param.18) | copy-start | bytes 3076
  16.0 8.5 %copy-start.5 = (f32[256]{0:T(256)S(1)}, f32[256]{0:T(256)}, u32[]{:S(2)}) copy-start(f32[256]{0:T(256)} %param.17) | copy-start | bytes 3076
  16.0 5.3 %collective-permute-start.2 = (bf16[144,256]{1,0:T(8,128)(2,1)S(1)}, bf16[144,256]{1,0:T(8,128)(2,1)S(1)}, u32[]{:S(2)}, u32[]{:S(2)}) collective-permute-start(bf16[144,256]{1,0:T(8,128)(2,1)S(1)} %get-tuple-element.62), channel_id=1, source_target_pairs={{0,16},{16,32},{32,48},{48,64},{64,80},{80,96},{96,112},{1,17},{17... | collective-permute-start | bytes 221192 | tf_op jit(solution)/shard_map/ppermute | solution.py:772
  19.3 5.1 %collective-permute-start.3 = (bf16[144,256]{1,0:T(8,128)(2,1)S(1)}, bf16[144,256]{1,0:T(8,128)(2,1)S(1)}, u32[]{:S(2)}, u32[]{:S(2)}) collective-permute-start(bf16[144,256]{1,0:T(8,128)(2,1)S(1)} %get-tuple-element.63), channel_id=1, source_target_pairs={{16,0},{32,16},{48,32},{64,48},{80,64},{96,80},{112,96},{17,1},{33... | collective-permute-start | bytes 221192 | tf_op jit(solution)/shard_map/ppermute | solution.py:772
  76.8 17.0 %copy-start.8 = (f32[2048,128]{1,0:T(8,128)}, f32[2048,128]{1,0:T(8,128)S(1)}, u32[]{:S(2)}) copy-start(f32[2048,128]{1,0:T(8,128)S(1)} %get-tuple-element.96.grid_total_ref) | copy-start | bytes 3145732
  98.5 0.7 copy-start.14
  99.2 11.9 %collective-permute-start.4 = (bf16[8,8,128]{2,1,0:T(8,128)(2,1)S(1)}, bf16[8,8,128]{2,1,0:T(8,128)(2,1)S(1)}, u32[]{:S(2)}, u32[]{:S(2)}) collective-permute-start(bf16[8,8,128]{2,1,0:T(8,128)(2,1)S(1)} %get-tuple-element.88), channel_id=1, source_target_pairs={{0,1},{1,2},{2,3},{3,4},{4,5},{5,6},{6,7},{7,8},{8,9},{9,10},{10,1... | collective-permute-start | bytes 49160 | tf_op jit(solution)/shard_map/ppermute | solution.py:780
  104.3 6.8 %collective-permute-start.5 = (bf16[8,8,128]{2,1,0:T(8,128)(2,1)S(1)}, bf16[8,8,128]{2,1,0:T(8,128)(2,1)S(1)}, u32[]{:S(2)}, u32[]{:S(2)}) collective-permute-start(bf16[8,8,128]{2,1,0:T(8,128)(2,1)S(1)} %get-tuple-element.89), channel_id=1, source_target_pairs={{1,0},{2,1},{3,2},{4,3},{5,4},{6,5},{7,6},{8,7},{9,8},{10,9},{11,1... | collective-permute-start | bytes 49160 | tf_op jit(solution)/shard_map/ppermute | solution.py:780
  111.1 3.6 %copy-start.6 = (bf16[8,8,64,128]{3,2,1,0:T(8,128)(2,1)}, bf16[8,8,64,128]{3,2,1,0:T(8,128)(2,1)S(1)}, u32[]{:S(2)}) copy-start(bf16[8,8,64,128]{3,2,1,0:T(8,128)(2,1)S(1)} %get-tuple-element.87.middle_ref) | copy-start | bytes 3145732
  111.1 3.6 %copy-start.10 = (f32[2048,128]{1,0:T(8,128)}, f32[2048,128]{1,0:T(8,128)S(1)}, u32[]{:S(2)}) copy-start(f32[2048,128]{1,0:T(8,128)S(1)} %get-tuple-element.95.block_total_ref) | copy-start | bytes 3145732
  111.1 3.6 %copy-start.12 = (bf16[8,64,256]{2,1,0:T(8,128)(2,1)}, bf16[8,64,256]{2,1,0:T(8,128)(2,1)S(1)}, u32[]{:S(2)}) copy-start(bf16[8,64,256]{2,1,0:T(8,128)(2,1)S(1)} %get-tuple-element.93.middle_ref) | copy-start | bytes 786436
  111.2 10.5 %collective-permute-start.6 = (bf16[8,144,128]{2,1,0:T(8,128)(2,1)S(1)}, bf16[8,144,128]{2,1,0:T(8,128)(2,1)S(1)}, u32[]{:S(2)}, u32[]{:S(2)}) collective-permute-start(bf16[8,144,128]{2,1,0:T(8,128)(2,1)S(1)} %get-tuple-element.90), channel_id=1, source_target_pairs={{0,16},{16,32},{32,48},{48,64},{64,80},{80,96},{96,112},{1,17},{17... | collective-permute-start | bytes 884744 | tf_op jit(solution)/shard_map/ppermute | solution.py:772
  113.3 9.8 %collective-permute-start.7 = (bf16[8,144,128]{2,1,0:T(8,128)(2,1)S(1)}, bf16[8,144,128]{2,1,0:T(8,128)(2,1)S(1)}, u32[]{:S(2)}, u32[]{:S(2)}) collective-permute-start(bf16[8,144,128]{2,1,0:T(8,128)(2,1)S(1)} %get-tuple-element.91), channel_id=1, source_target_pairs={{16,0},{32,16},{48,32},{64,48},{80,64},{96,80},{112,96},{17,1},{33... | collective-permute-start | bytes 884744 | tf_op jit(solution)/shard_map/ppermute | solution.py:772
  114.7 1.2 copy-start.9
  115.9 1.2 copy-start.11
  117.1 0.9 copy-start.13
  118.1 0.9 copy-start.15
  119.0 4.1 %copy-start.7 = (bf16[8,8,64,128]{3,2,1,0:T(8,128)(2,1)S(1)}, bf16[8,8,64,128]{3,2,1,0:T(8,128)(2,1)}, u32[]{:S(2)}) copy-start(bf16[8,8,64,128]{3,2,1,0:T(8,128)(2,1)} %copy-done.6) | copy-start | bytes 3145732
  121.6 11.6 %collective-permute-start.8 = (bf16[3072,128]{1,0:T(8,128)(2,1)S(1)}, bf16[3072,128]{1,0:T(8,128)(2,1)S(1)}, u32[]{:S(2)}, u32[]{:S(2)}) collective-permute-start(bf16[3072,128]{1,0:T(8,128)(2,1)S(1)} %get-tuple-element.100), channel_id=1, source_target_pairs={{0,1},{1,0},{2,3},{3,2},{4,5},{5,4},{6,7},{7,6},{8,9},{9,8},{10,11... | collective-permute-start | bytes 2359304 | tf_op jit(solution)/shard_map/ppermute | solution.py:788
  131.4 1.8 collective-permute-start.9
  187.5 6.1 %collective-permute-start.10 = (bf16[64,72,128]{2,1,0:T(8,128)(2,1)S(1)}, bf16[64,72,128]{2,1,0:T(8,128)(2,1)S(1)}, u32[]{:S(2)}, u32[]{:S(2)}) collective-permute-start(bf16[64,72,128]{2,1,0:T(8,128)(2,1)S(1)} %all_to_all.23.mine_ref), channel_id=1, source_target_pairs={{0,1},{1,0},{2,3},{3,2},{4,5},{5,4},{6,7},{7,6},{8,9},{9,8},{10,11... | collective-permute-start | bytes 3538952 | tf_op jit(solution)/shard_map/ppermute | solution.py:788

commit v3 on v2

--- a/solution.py
+++ b/solution.py
@@ -67,25 +67,15 @@
     )
 
 
-def load_kernel(*refs):
-    count = (len(refs) - 4) // 2
-    sources, targets = refs[:count], refs[count : 2 * count]
-    left_ref, right_ref, sems, ends = refs[2 * count :]
-    copies = [
-        pltpu.make_async_copy(source, target, sems.at[k])
-        for k, (source, target) in enumerate(zip(sources, targets))
-    ]
-    for copy in copies:
-        copy.start()
-    copies[0].wait()
-    x_ref = targets[0]
+def load_kernel(x_in, x_ref, left_ref, right_ref, sem, ends):
+    copy = pltpu.make_async_copy(x_in, x_ref, sem)
+    copy.start()
+    copy.wait()
     for row in range(ROWS):
         ends[0, row : row + 1, :] = x_ref[row, 0:16, :].astype(F32)[0:1]
         ends[1, row : row + 1, :] = x_ref[row, COLS - 16 : COLS, :].astype(F32)[15:16]
     left_ref[...] = ends[0].astype(BF16)
     right_ref[...] = ends[1].astype(BF16)
-    for copy in copies[1:]:
-        copy.wait()
 
 
 def with_corners(cells, left, right):
@@ -224,12 +214,159 @@
         total_ref[1536 + 256 * k : 1792 + 256 * k, :] = total[:, 128 * k : 128 * k + 128]
 
 
+def edge_flags():
+    row_index = lax.axis_index("row")
+    col_index = 2 * lax.axis_index("hi") + lax.axis_index("core")
+    flags = (row_index > 0, row_index < 7, col_index > 0, col_index < 15)
+    return [jnp.where(flag, 1.0, 0.0).astype(F32) for flag in flags]
+
+
+def shift_scale(tokens, scale_ref, shift_ref):
+    return (tokens.astype(F32) * scale_ref[...] + shift_ref[...]).astype(BF16)
+
+
+def copy_all(pairs, sems, first=0):
+    copies = [
+        pltpu.make_async_copy(source, target, sems.at[first + k])
+        for k, (source, target) in enumerate(pairs)
+    ]
+    for copy in copies:
+        copy.start()
+    return copies
+
+
+def wait_all(copies):
+    for copy in copies:
+        copy.wait()
+
+
+def expand_kernel(
+    x_ref,
+    scale_ref,
+    shift_ref,
+    *refs,
+):
+    count = (len(refs) - 6) // 2
+    sources, (lifted_out, slope_pre_out, lifted_ref) = refs[:count], refs[count : count + 3]
+    targets, (slope_pre_ref, sems, load_sems) = refs[count + 3 : -3], refs[-3:]
+    loads = copy_all(list(zip(sources, targets)), load_sems)
+    w_expand_ref = targets[0]
+
+    def stores(row):
+        here = pl.ds(pl.multiple_of(row * COLS, COLS), COLS)
+        return [
+            pltpu.make_async_copy(source.at[:, here, :], target.at[:, here, :], sems.at[row, k])
+            for k, (source, target) in enumerate(
+                ((lifted_ref, lifted_out), (slope_pre_ref, slope_pre_out))
+            )
+        ]
+
+    wait_all(loads[:1])
+
+    @pl.loop(0, ROWS)
+    def _(row):
+        here = pl.ds(pl.multiple_of(row * COLS, COLS), COLS)
+        shifted = shift_scale(x_ref[row], scale_ref, shift_ref)
+        for pair in range(4):
+            value, slope = gelu_pair(
+                dot(shifted, w_expand_ref[:, 256 * pair : 256 * pair + 256], 1, 0)
+            )
+            value = value.astype(BF16)
+            slope = slope.astype(BF16)
+            for k in range(2):
+                lanes = slice(128 * k, 128 * k + 128)
+                lifted_ref[2 * pair + k, here, :] = value[:, lanes]
+                slope_pre_ref[2 * pair + k, here, :] = slope[:, lanes]
+        for copy in stores(row):
+            copy.start()
+
+    wait_all(loads[1:])
+    for row in range(ROWS):
+        wait_all(stores(row))
+
+
+def convolve_rows(pad, block, pad_row, taps, second_ref, slope_conv_ref, row):
+    for chunk in range(4):
+        summed = None
+        for t in range(9):
+            start = LEFT - 1 + t % 3 + 32 * chunk
+            term = taps[t] * pad[block, pad_row + t // 3, start : start + 32, :]
+            summed = term if summed is None else summed + term
+        value, slope = gelu_pair(summed)
+        here = pl.ds(pl.multiple_of(row * COLS + 32 * chunk, 32), 32)
+        second_ref[block, here, :] = value.astype(BF16)
+        slope_conv_ref[block, here, :] = slope.astype(BF16)
+
+
+def taps_of(dw_ref, block):
+    lanes = pl.ds(pl.multiple_of(block * 128, 128), 128)
+    return [dw_ref[t : t + 1, lanes] for t in range(9)]
+
+
+def inner_rows_kernel(
+    lifted_ref,
+    left_ref,
+    right_ref,
+    scale_ref,
+    shift_ref,
+    w_expand_ref,
+    dw_ref,
+    second_out,
+    second_ref,
+    slope_conv_out,
+    side_ref,
+    pad,
+    slope_conv_ref,
+    sems,
+):
+    def stores(block):
+        return [
+            pltpu.make_async_copy(source.at[block], target.at[block], sems.at[block, k])
+            for k, (source, target) in enumerate(
+                ((second_ref, second_out), (slope_conv_ref, slope_conv_out))
+            )
+        ]
+
+    inside = edge_flags()
+    sides = jnp.concatenate([left_ref[...], right_ref[...]], axis=0)
+    shifted = shift_scale(sides, scale_ref, shift_ref)
+    place = lax.broadcasted_iota(jnp.int32, (16, 1), 0)
+    flags = jnp.where(place < 8, inside[2], inside[3])
+    for pair in range(4):
+        value, _ = gelu_pair(dot(shifted, w_expand_ref[:, 256 * pair : 256 * pair + 256], 1, 0))
+        value = value.astype(BF16).astype(F32) * flags
+        for k in range(2):
+            side_ref[2 * pair + k] = value[:, 128 * k : 128 * k + 128]
+
+    @pl.loop(0, BLOCKS)
+    def _(block):
+        taps = taps_of(dw_ref, block)
+        side = side_ref[block]
+        for row in range(ROWS):
+            pad[block, row, LEFT : LEFT + COLS, :] = lifted_ref[
+                block, COLS * row : COLS * row + COLS, :
+            ].astype(F32)
+            pad[block, row, LEFT - 1 : LEFT, :] = side[row : row + 1]
+            pad[block, row, LEFT + COLS : LEFT + COLS + 1, :] = side[8 + row : 9 + row]
+
+        @pl.loop(0, ROWS - 2)
+        def _(row):
+            convolve_rows(pad, block, row, taps, second_ref, slope_conv_ref, row)
+
+        for copy in stores(block):
+            copy.start()
+
+    for block in range(BLOCKS):
+        wait_all(stores(block))
+
+
 def front_kernel(
     x_ref,
     top_ref,
     bottom_ref,
-    left_ref,
-    right_ref,
+    lifted_ref,
+    side_ref,
+    second_mid_ref,
     scale_ref,
     shift_ref,
     w_expand_ref,
@@ -241,53 +378,34 @@
     bias,
     gain_grid_ref,
     grad_output_ref,
-    lifted_out,
-    slope_pre_out,
     second_out,
-    slope_conv_ref,
-    section_one_ref,
-    section_two_ref,
+    slope_edge_out,
+    section_one_out,
+    section_two_out,
     send_ref,
     normed_block_out,
-    joined_ref,
-    probs_ref,
+    joined_out,
+    probs_out,
     mixture_out,
     pad,
     cells,
     outcome,
-    lifted_ref,
-    slope_pre_ref,
     second_ref,
+    slope_edge_ref,
+    section_one_ref,
+    section_two_ref,
     normed_block_ref,
+    joined_ref,
+    probs_ref,
     mixture_ref,
     sems,
+    part_sems,
 ):
-    stores = [
-        pltpu.make_async_copy(source, target, sems.at[k])
-        for k, (source, target) in enumerate(
-            (
-                (lifted_ref, lifted_out),
-                (slope_pre_ref, slope_pre_out),
-                (second_ref, second_out),
-                (normed_block_ref, normed_block_out),
-                (mixture_ref, mixture_out),
-            )
-        )
-    ]
     send_ref[:, 16:32, :] = grad_output_ref[...].reshape(64, 16, D)
     heads_mask = heads_mask_of()
-    row_index = lax.axis_index("row")
-    col_index = 2 * lax.axis_index("hi") + lax.axis_index("core")
-    inside = [
-        jnp.where(flag, 1.0, 0.0).astype(F32)
-        for flag in (row_index > 0, row_index < 7, col_index > 0, col_index < 15)
-    ]
-
-    def shifted_of(tokens):
-        return (tokens.astype(F32) * scale_ref[...] + shift_ref[...]).astype(BF16)
-
-    for source, row, flag in ((top_ref, 0, inside[0]), (bottom_ref, 9, inside[1])):
-        shifted = shifted_of(source[...])
+    inside = edge_flags()
+    for source, row, flag in ((top_ref, 0, inside[0]), (bottom_ref, 5, inside[1])):
+        shifted = shift_scale(source[...], scale_ref, shift_ref)
         for pair in range(4):
             value, _ = gelu_pair(dot(shifted, w_expand_ref[:, 256 * pair : 256 * pair + 256], 1, 0))
             value = value.astype(BF16).astype(F32) * flag
@@ -299,71 +417,63 @@
                 pad[block, row, LEFT + COLS : LEFT + COLS + 1, :] = (
                     part[COLS + 1 : COLS + 2] * inside[3]
                 )
-    shifted = shifted_of(jnp.concatenate([left_ref[...], right_ref[...]], axis=0))
-    place = lax.broadcasted_iota(jnp.int32, (16, 1), 0)
-    flags = jnp.where(place < 8, inside[2], inside[3])
-    for pair in range(4):
-        value, _ = gelu_pair(dot(shifted, w_expand_ref[:, 256 * pair : 256 * pair + 256], 1, 0))
-        value = value.astype(BF16).astype(F32) * flags
-        for k in range(2):
-            block = 2 * pair + k
-            part = value[:, 128 * k : 128 * k + 128]
-            for row in range(ROWS):
-                pad[block, row + 1, LEFT - 1 : LEFT, :] = part[row : row + 1]
-                pad[block, row + 1, LEFT + COLS : LEFT + COLS + 1, :] = part[8 + row : 9 + row]
-
-    @pl.loop(0, ROWS)
-    def _(row):
-        here = pl.ds(pl.multiple_of(row * COLS, COLS), COLS)
-        shifted = shifted_of(x_ref[row])
-        for pair in range(4):
-            value, slope = gelu_pair(
-                dot(shifted, w_expand_ref[:, 256 * pair : 256 * pair + 256], 1, 0)
-            )
-            value = value.astype(BF16)
-            slope = slope.astype(BF16)
-            for k in range(2):
-                lanes = slice(128 * k, 128 * k + 128)
-                lifted_ref[2 * pair + k, here, :] = value[:, lanes]
-                slope_pre_ref[2 * pair + k, here, :] = slope[:, lanes]
-                pad[2 * pair + k, row + 1, LEFT : LEFT + COLS, :] = value[:, lanes].astype(F32)
-
-    stores[0].start()
-    stores[1].start()
 
     @pl.loop(0, BLOCKS)
     def _(block):
-        taps = [
-            dw_ref[t : t + 1, pl.ds(pl.multiple_of(block * 128, 128), 128)] for t in range(9)
+        taps = taps_of(dw_ref, block)
+        side = side_ref[block]
+        for row, place in ((0, 1), (1, 2), (6, 3), (7, 4)):
+            pad[block, place, LEFT : LEFT + COLS, :] = lifted_ref[
+                block, COLS * row : COLS * row + COLS, :
+            ].astype(F32)
+            pad[block, place, LEFT - 1 : LEFT, :] = side[row : row + 1]
+            pad[block, place, LEFT + COLS : LEFT + COLS + 1, :] = side[8 + row : 9 + row]
+        for row in range(2):
+            convolve_rows(pad, block, 3 * row, taps, second_ref, slope_edge_ref, row)
+
+    stores = copy_all(((second_ref, second_out), (slope_edge_ref, slope_edge_out)), sems)
+    for part in range(4):
+        rows = slice(2 * part, 2 * part + 2)
+        summed = x_ref[rows].reshape(256, D).astype(F32)
+        for pair in range(4):
+            pieces = []
+            for block in (2 * pair, 2 * pair + 1):
+                pieces.append(
+                    jnp.concatenate(
+                        [
+                            second_ref[block, COLS * (row // 7) : COLS * (row // 7) + COLS, :]
+                            if row in (0, 7)
+                            else second_mid_ref[block, COLS * (row - 1) : COLS * row, :]
+                            for row in (2 * part, 2 * part + 1)
+                        ],
+                        axis=0,
+                    )
+                )
+            summed = summed + dot(
+                jnp.concatenate(pieces, axis=1), w_project_ref[256 * pair : 256 * pair + 256, :], 1, 0
+            )
+        section_one = summed.astype(BF16)
+        section_one_ref[rows] = section_one.reshape(2, COLS, D)
+        cells[rows] = section_one.astype(F32).reshape(2, COLS, D)
+
+    stores += copy_all([(section_one_ref, section_one_out)], sems, first=2)
+
+    def part_stores(part):
+        here = pl.ds(pl.multiple_of(part * 256, 256), 256)
+        columns = pl.ds(pl.multiple_of(part * 32, 32), 32)
+        eight = pl.ds(part * 8, 8)
+        return [
+            pltpu.make_async_copy(source, target, part_sems.at[part, k])
+            for k, (source, target) in enumerate(
+                (
+                    (normed_block_ref.at[here, :], normed_block_out.at[here, :]),
+                    (joined_ref.at[here, :], joined_out.at[here, :]),
+                    (mixture_ref.at[here, :], mixture_out.at[here, :]),
+                    (probs_ref.at[eight], probs_out.at[eight]),
+                    (section_two_ref.at[:, columns, :], section_two_out.at[:, columns, :]),
+                )
+            )
         ]
-
-        @pl.loop(0, ROWS)
-        def _(row):
-            for chunk in range(4):
-                summed = None
-                for t in range(9):
-                    start = LEFT - 1 + t % 3 + 32 * chunk
-                    term = taps[t] * pad[block, row + t // 3, start : start + 32, :]
-                    summed = term if summed is None else summed + term
-                value, slope = gelu_pair(summed)
-                here = pl.ds(pl.multiple_of(row * COLS + 32 * chunk, 32), 32)
-                second_ref[block, here, :] = value.astype(BF16)
-                slope_conv_ref[block, here, :] = slope.astype(BF16)
-
-    stores[2].start()
-
-    @pl.loop(0, 4)
-    def _(part):
-        here = pl.ds(pl.multiple_of(part * 256, 256), 256)
-        summed = x_ref[pl.ds(2 * part, 2)].reshape(256, D).astype(F32)
-        for pair in range(4):
-            joined = jnp.concatenate(
-                [second_ref[2 * pair, here, :], second_ref[2 * pair + 1, here, :]], axis=1
-            )
-            summed = summed + dot(joined, w_project_ref[256 * pair : 256 * pair + 256, :], 1, 0)
-        section_one = summed.astype(BF16)
-        section_one_ref[pl.ds(2 * part, 2)] = section_one.reshape(2, COLS, D)
-        cells[pl.ds(2 * part, 2)] = section_one.astype(F32).reshape(2, COLS, D)
 
     @pl.loop(0, 4)
     def _(part):
@@ -379,16 +489,16 @@
             probs_ref[part * 8 + index] = probs[index]
         mixture_ref[here, :] = mixture
         section_two = (section_one + dot(mixture, w_out_ref[...], 1, 0)).astype(BF16).astype(F32)
-        cells[:, columns, :] = from_four_windows(section_two)
+        section_two_ref[:, columns, :] = from_four_windows(section_two).astype(BF16)
+        for copy in part_stores(part):
+            copy.start()
         normed = norm_parts(section_two)[0] * gain_grid_ref[...]
         outcome[:, columns, :] = from_four_windows(normed)
 
-    stores[3].start()
-    stores[4].start()
     send_ref[:, 0:16, :] = outcome[...].astype(BF16).reshape(64, 16, D)
-    section_two_ref[...] = cells[...].astype(BF16)
-    for copy in stores:
-        copy.wait()
+    wait_all(stores)
+    for part in range(4):
+        wait_all(part_stores(part))
 
 
 def grid_kernel(
@@ -423,84 +533,109 @@
     parts,
     returned_ref,
     grad_output_ref,
-    section_two_ref,
-    section_one_ref,
-    joined_ref,
-    probs_ref,
-    slope_conv_ref,
+    section_two_in,
+    section_one_in,
+    joined_in,
+    probs_in,
+    slope_mid_in,
+    slope_edge_in,
+    normed_block_in,
+    mixture_in,
     gain_grid_ref,
     gain_block_ref,
     w_qkv_ref,
     w_out_ref,
     w_project_ref,
-    normed_block_in,
-    mixture_in,
     *rest,
 ):
-    normed_block_ref, mixture_ref, sems = rest[-3:]
-    if len(rest) == 9:
+    (
+        section_two_ref,
+        section_one_ref,
+        joined_ref,
+        probs_ref,
+        slope_ref,
+        normed_block_ref,
+        mixture_ref,
+        grad_one_ref,
+        fetch_sems,
+        sems,
+    ) = rest[-10:]
+    if len(rest) == 16:
         before_ref = None
-        grad_one_ref, inner_ref, total_ref, left_ref, right_ref, ends = rest[:-3]
+        grad_one_out, inner_ref, total_ref, left_ref, right_ref, ends = rest[:-10]
     else:
-        before_ref, grad_one_ref, inner_ref, total_ref = rest[:-3]
+        before_ref, grad_one_out, inner_ref, total_out, total_ref = rest[:-10]
     fetches = []
+    stores = []
     for index, part in enumerate(parts):
-        for k, (source, target) in enumerate(
-            ((normed_block_in, normed_block_ref), (mixture_in, mixture_ref))
-        ):
-            fetches.append(
-                pltpu.make_async_copy(
-                    source.at[pl.ds(256 * part, 256), :],
-                    target.at[pl.ds(256 * index, 256), :],
-                    sems.at[2 * index + k],
-                )
+        here = pl.ds(256 * part, 256)
+        target = pl.ds(256 * index, 256)
+        columns = pl.ds(32 * part, 32)
+        to = pl.ds(32 * index, 32)
+        fetches.append(
+            copy_all(
+                (
+                    (section_two_in.at[:, columns, :], section_two_ref.at[:, to, :]),
+                    (joined_in.at[here, :], joined_ref.at[target, :]),
+                    (probs_in.at[pl.ds(8 * part, 8)], probs_ref.at[pl.ds(8 * index, 8)]),
+                    (section_one_in.at[:, columns, :], section_one_ref.at[:, to, :]),
+                    (
+                        slope_mid_in.at[:, :, columns, :],
+                        slope_ref.at[:, pl.ds(1, 6), to, :],
+                    ),
+                    (
+                        slope_edge_in.at[:, pl.ds(0, 1), columns, :],
+                        slope_ref.at[:, pl.ds(0, 1), to, :],
+                    ),
+                    (
+                        slope_edge_in.at[:, pl.ds(1, 1), columns, :],
+                        slope_ref.at[:, pl.ds(7, 1), to, :],
+                    ),
+                    (normed_block_in.at[here, :], normed_block_ref.at[target, :]),
+                    (mixture_in.at[here, :], mixture_ref.at[target, :]),
+                ),
+                fetch_sems.at[index],
             )
-            fetches[-1].start()
+        )
     heads_mask = heads_mask_of()
     all_windows = []
     all_joined = []
     for index, part in enumerate(parts):
-        here = slice(256 * part, 256 * part + 256)
+        here = slice(256 * index, 256 * index + 256)
         columns = slice(32 * part, 32 * part + 32)
         out_columns = slice(32 * index, 32 * index + 32)
 
-        def windows_of(ref):
+        def windows_of(ref, columns):
             return four_windows(ref[:, columns, :].astype(F32))
 
-        grad_two = windows_of(grad_output_ref) + norm_back(
-            windows_of(section_two_ref), gain_grid_ref[...], windows_of(returned_ref)
+        wait_all(fetches[index][:1])
+        grad_two = windows_of(grad_output_ref, columns) + norm_back(
+            windows_of(section_two_ref, out_columns),
+            gain_grid_ref[...],
+            windows_of(returned_ref, columns),
         )
         grad_windows = grad_two.astype(BF16)
         grad_two = grad_windows.astype(F32)
+        grad_mix = dot(grad_windows, w_out_ref[...], 1, 1).astype(BF16)
+        wait_all(fetches[index][1:3])
         joined = joined_ref[here, :]
-        grad_mix = dot(grad_windows, w_out_ref[...], 1, 1).astype(BF16)
-        probs = [probs_ref[part * 8 + k] for k in range(8)]
+        probs = [probs_ref[index * 8 + k] for k in range(8)]
         grad_joined = attend_back(joined, probs, grad_mix, heads_mask)
         all_windows.append(grad_windows)
         all_joined.append(grad_joined)
         grad_normed = dot(grad_joined, w_qkv_ref[...], 1, 1).astype(BF16).astype(F32)
+        wait_all(fetches[index][3:4])
         grad_one = grad_two + norm_back(
-            windows_of(section_one_ref), gain_block_ref[...], grad_normed
+            windows_of(section_one_ref, out_columns), gain_block_ref[...], grad_normed
         )
-        grad_one = from_four_windows(grad_one).astype(BF16)
-        grad_one_ref[:, out_columns, :] = grad_one
-        grad_one = grad_one.reshape(256, D)
-        for pair in range(4):
-            through = dot(grad_one, w_project_ref[256 * pair : 256 * pair + 256, :], 1, 1)
-            for k in range(2):
-                block = 2 * pair + k
-                slope = slope_conv_ref[block, :, columns, :].astype(F32)
-                inner = through[:, 128 * k : 128 * k + 128].reshape(ROWS, 32, 128) * slope
-                inner_ref[block, :, out_columns, :] = inner.astype(BF16)
-                if before_ref is None:
-                    side, column = (0, 0) if part == 0 else (1, 31)
-                    for row in range(ROWS):
-                        ends[side, block, row : row + 1, :] = inner[row, column : column + 1]
-    if before_ref is None:
-        left_ref[...] = ends[0].astype(BF16)
-        right_ref[...] = ends[1].astype(BF16)
-    for copy in fetches:
-        copy.wait()
+        grad_one_ref[:, out_columns, :] = from_four_windows(grad_one).astype(BF16)
+        stores += copy_all(
+            [(grad_one_ref.at[:, out_columns, :], grad_one_out.at[:, out_columns, :])],
+            sems,
+            first=index,
+        )
+    for index in range(2):
+        wait_all(fetches[index][7:])
     joined = jnp.concatenate(all_joined, axis=0)
     windows = jnp.concatenate(all_windows, axis=0)
     products = [
@@ -512,40 +647,146 @@
             place = slice(start + 256 * k, start + 256 * k + 256)
             value = total[:, 128 * k : 128 * k + 128]
             total_ref[place, :] = value if before_ref is None else before_ref[place, :] + value
+    if before_ref is not None:
+        stores += copy_all([(total_ref, total_out)], sems, first=2)
+    for index, part in enumerate(parts):
+        wait_all(fetches[index][4:7])
+        out_columns = slice(32 * index, 32 * index + 32)
+        grad_one = grad_one_ref[:, out_columns, :].reshape(256, D)
+        for pair in range(4):
+            through = dot(grad_one, w_project_ref[256 * pair : 256 * pair + 256, :], 1, 1)
+            for k in range(2):
+                block = 2 * pair + k
+                slope = slope_ref[block, :, out_columns, :].astype(F32)
+                inner = through[:, 128 * k : 128 * k + 128].reshape(ROWS, 32, 128) * slope
+                inner_ref[block, :, out_columns, :] = inner.astype(BF16)
+                if before_ref is None:
+                    side, column = (0, 0) if part == 0 else (1, 31)
+                    for row in range(ROWS):
+                        ends[side, block, row : row + 1, :] = inner[row, column : column + 1]
+    if before_ref is None:
+        left_ref[...] = ends[0].astype(BF16)
+        right_ref[...] = ends[1].astype(BF16)
+    wait_all(stores)
 
 
 def total_kernel(
     core_ref,
-    outer_ref,
-    middle_ref,
-    second_in,
-    block_total_ref,
-    grid_total_ref,
+    outer_in,
+    middle_in,
+    second_mid_in,
+    second_edge_in,
+    block_total_in,
+    grid_total_in,
+    _,
     grad_one_ref,
     early_send_ref,
     early_keep_ref,
     total_ref,
     second_ref,
-    sem,
+    sems,
 ):
-    fetch = pltpu.make_async_copy(second_in, second_ref, sem)
-    fetch.start()
-    grad_one = whole_row(outer_ref[...], middle_ref[...])
-    grad_one_ref[...] = grad_one
-    grad_one = grad_one.reshape(TOKENS, D)
-    total_ref[0:2048, :] = block_total_ref[...]
-    total_ref[4096:6144, :] = grid_total_ref[...]
-    fetch.wait()
+    rows = (pl.ds(0, COLS), pl.ds(COLS, 6 * COLS), pl.ds(7 * COLS, COLS))
+    fetches = copy_all(
+        (
+            (outer_in.at[:, pl.ds(0, 32), :], grad_one_ref.at[:, pl.ds(0, 32), :]),
+            (outer_in.at[:, pl.ds(32, 32), :], grad_one_ref.at[:, pl.ds(96, 32), :]),
+            (middle_in, grad_one_ref.at[:, pl.ds(32, 64), :]),
+            (second_edge_in.at[:, pl.ds(0, COLS), :], second_ref.at[:, rows[0], :]),
+            (second_mid_in, second_ref.at[:, rows[1], :]),
+            (second_edge_in.at[:, pl.ds(COLS, COLS), :], second_ref.at[:, rows[2], :]),
+            (block_total_in, total_ref.at[pl.ds(0, 2048), :]),
+            (grid_total_in, total_ref.at[pl.ds(4096, 2048), :]),
+        ),
+        sems,
+    )
+    wait_all(fetches[:6])
+    grad_one = grad_one_ref[...].reshape(TOKENS, D)
     for pair in range(4):
         joined = jnp.concatenate([second_ref[2 * pair], second_ref[2 * pair + 1]], axis=1)
         total = dot(joined, grad_one, 0, 0)
         for k in range(2):
             start = 2048 + 1024 * k + 256 * pair
             total_ref[start : start + 256, :] = total[:, 128 * k : 128 * k + 128]
+    wait_all(fetches[6:])
     own = pl.ds(pl.multiple_of(core_ref[0] * 3072, 3072), 3072)
     other = pl.ds(pl.multiple_of((1 - core_ref[0]) * 3072, 3072), 3072)
     early_keep_ref[...] = total_ref[own, :].astype(BF16)
     early_send_ref[...] = total_ref[other, :].astype(BF16)
+
+
+def back_rows(pad, block, pad_row, taps, lifted_ref, slope_pre_ref, preact_ref, row, totals):
+    totals = list(totals)
+    for chunk in range(4):
+        here = pl.ds(pl.multiple_of(row * COLS + 32 * chunk, 32), 32)
+        lifted = lifted_ref[block, here, :].astype(F32)
+        summed = None
+        for t in range(9):
+            start = LEFT + 1 - t % 3 + 32 * chunk
+            cells = pad[block, pad_row + 2 - t // 3, start : start + 32, :]
+            term = taps[t] * cells
+            summed = term if summed is None else summed + term
+            totals[t] = totals[t] + jnp.sum((lifted * cells).reshape(4, 8, 128), axis=0)
+        grad = summed * slope_pre_ref[block, here, :].astype(F32)
+        preact_ref[block, here, :] = grad.astype(BF16)
+    return tuple(totals)
+
+
+def fill_row(pad, block, place, row, outer_ref, middle_ref, left, right):
+    cells = whole_row(outer_ref[block, row], middle_ref[block, row])
+    pad[block, place, LEFT : LEFT + COLS, :] = cells.astype(F32)
+    pad[block, place, LEFT - 1 : LEFT, :] = left[row : row + 1]
+    pad[block, place, LEFT + COLS : LEFT + COLS + 1, :] = right[row : row + 1]
+
+
+def back_inner_kernel(
+    lifted_in,
+    slope_pre_in,
+    outer_ref,
+    middle_ref,
+    left_ref,
+    right_ref,
+    dw_ref,
+    preact_ref,
+    taps_ref,
+    pad,
+    lifted_ref,
+    slope_pre_ref,
+    sems,
+):
+    rows = pl.ds(COLS, 6 * COLS)
+
+    def fetches(block):
+        return [
+            pltpu.make_async_copy(
+                source.at[block, rows, :], target.at[block], sems.at[block, k]
+            )
+            for k, (source, target) in enumerate(
+                ((lifted_in, lifted_ref), (slope_pre_in, slope_pre_ref))
+            )
+        ]
+
+    for block in range(BLOCKS):
+        for copy in fetches(block):
+            copy.start()
+
+    @pl.loop(0, BLOCKS)
+    def _(block):
+        left = left_ref[block].astype(F32)
+        right = right_ref[block].astype(F32)
+        for row in range(ROWS):
+            fill_row(pad, block, row, row, outer_ref, middle_ref, left, right)
+        wait_all(fetches(block))
+        taps = taps_of(dw_ref, block)
+
+        def step(row, totals):
+            return back_rows(
+                pad, block, row, taps, lifted_ref, slope_pre_ref, preact_ref, row, totals
+            )
+
+        totals = lax.fori_loop(0, ROWS - 2, step, (jnp.zeros((8, 128), F32),) * 9)
+        for t in range(9):
+            taps_ref[t, pl.ds(block, 1), :] = jnp.sum(totals[t], axis=0, keepdims=True)
 
 
 def back_kernel(
@@ -562,80 +803,64 @@
     scale_ref,
     shift_ref,
     dw_ref,
+    preact_mid_ref,
+    taps_mid_ref,
     _,
     preact_ref,
     late_send_ref,
     late_keep_ref,
     pad,
+    lifted_ref,
+    slope_pre_ref,
     shifted_ref,
     total_ref,
     taps_ref,
-    lifted_ref,
-    slope_pre_ref,
     sems,
 ):
-    def fetches(block):
-        return [
-            pltpu.make_async_copy(source.at[block], target.at[block], sems.at[block, k])
-            for k, (source, target) in enumerate(
-                ((lifted_in, lifted_ref), (slope_pre_in, slope_pre_ref))
-            )
-        ]
-
-    for block in range(BLOCKS):
-        for copy in fetches(block):
-            copy.start()
-    for block in range(BLOCKS):
-        for source, row in ((top_ref, 0), (bottom_ref, 9)):
-            cells = source[block].astype(F32)
-            pad[block, row, LEFT : LEFT + COLS, :] = cells[:COLS]
-            pad[block, row, LEFT - 1 : LEFT, :] = cells[COLS : COLS + 1]
-            pad[block, row, LEFT + COLS : LEFT + COLS + 1, :] = cells[COLS + 1 : COLS + 2]
+    first, last = pl.ds(0, COLS), pl.ds(7 * COLS, COLS)
+    second = pl.ds(COLS, COLS)
+    fetches = copy_all(
+        [
+            (source.at[:, rows, :], target.at[:, place, :])
+            for source, target in ((lifted_in, lifted_ref), (slope_pre_in, slope_pre_ref))
+            for rows, place in ((first, first), (last, second))
+        ],
+        sems,
+    )
+    for place, row in enumerate((1, 2, 3, 4, 5, 6, 0, 7)):
+        shifted_ref[COLS * place : COLS * place + COLS, :] = shift_scale(
+            x_ref[row], scale_ref, shift_ref
+        )
+    wait_all(fetches)
+
+    @pl.loop(0, BLOCKS)
+    def _(block):
         left = left_ref[block].astype(F32)
         right = right_ref[block].astype(F32)
-        for row in range(ROWS):
-            pad[block, row + 1, LEFT - 1 : LEFT, :] = left[row : row + 1]
-            pad[block, row + 1, LEFT + COLS : LEFT + COLS + 1, :] = right[row : row + 1]
-
-    @pl.loop(0, BLOCKS)
-    def _(block):
-        for copy in fetches(block):
-            copy.wait()
-        taps = [
-            dw_ref[t : t + 1, pl.ds(pl.multiple_of(block * 128, 128), 128)] for t in range(9)
+        for source, place in ((top_ref, 0), (bottom_ref, 5)):
+            cells = source[block].astype(F32)
+            pad[block, place, LEFT : LEFT + COLS, :] = cells[:COLS]
+            pad[block, place, LEFT - 1 : LEFT, :] = cells[COLS : COLS + 1]
+            pad[block, place, LEFT + COLS : LEFT + COLS + 1, :] = cells[COLS + 1 : COLS + 2]
+        for row, place in ((0, 1), (1, 2), (6, 3), (7, 4)):
+            fill_row(pad, block, place, row, outer_ref, middle_ref, left, right)
+        taps = taps_of(dw_ref, block)
+        totals = (jnp.zeros((8, 128), F32),) * 9
+        for row in range(2):
+            totals = back_rows(
+                pad, block, 3 * row, taps, lifted_ref, slope_pre_ref, preact_ref, row, totals
+            )
+        for t in range(9):
+            taps_ref[t, pl.ds(block, 1), :] = taps_mid_ref[t, pl.ds(block, 1), :] + jnp.sum(
+                totals[t], axis=0, keepdims=True
+            )
+
+    for pair in range(4):
+        pieces = [
+            jnp.concatenate([preact_mid_ref[block], preact_ref[block]], axis=0)
+            for block in (2 * pair, 2 * pair + 1)
         ]
-
-        @pl.loop(0, ROWS)
-        def _(row):
-            cells = whole_row(outer_ref[block, row], middle_ref[block, row])
-            pad[block, row + 1, LEFT : LEFT + COLS, :] = cells.astype(F32)
-
-        def step(row, totals):
-            totals = list(totals)
-            for chunk in range(4):
-                here = pl.ds(pl.multiple_of(row * COLS + 32 * chunk, 32), 32)
-                lifted = lifted_ref[block, here, :].astype(F32)
-                summed = None
-                for t in range(9):
-                    start = LEFT + 1 - t % 3 + 32 * chunk
-                    cells = pad[block, row + 2 - t // 3, start : start + 32, :]
-                    term = taps[t] * cells
-                    summed = term if summed is None else summed + term
-                    totals[t] = totals[t] + jnp.sum((lifted * cells).reshape(4, 8, 128), axis=0)
-                grad = summed * slope_pre_ref[block, here, :].astype(F32)
-                preact_ref[block, here, :] = grad.astype(BF16)
-            return tuple(totals)
-
-        totals = lax.fori_loop(0, ROWS, step, (jnp.zeros((8, 128), F32),) * 9)
-        for t in range(9):
-            taps_ref[t, pl.ds(block, 1), :] = jnp.sum(totals[t], axis=0, keepdims=True)
-
-    shifted_ref[...] = (
-        x_ref[...].reshape(TOKENS, D).astype(F32) * scale_ref[...] + shift_ref[...]
-    ).astype(BF16)
-    for pair in range(4):
-        joined = jnp.concatenate([preact_ref[2 * pair], preact_ref[2 * pair + 1]], axis=1)
-        total = dot(shifted_ref[...], joined, 0, 0)
+        total = dot(shifted_ref[...], jnp.concatenate(pieces, axis=1), 0, 0)
         for k in range(2):
             start = 256 * (2 * pair + k)
             total_ref[start : start + 256, :] = total[:, 128 * k : 128 * k + 128]
@@ -648,17 +873,25 @@
             target[index] = jnp.concatenate([large[index], taps], axis=0).astype(BF16)
 
 
-def input_kernel(preact_ref, grad_one_ref, w_expand_ref, scale_ref, grad_input_ref):
-    for part in range(4):
-        here = slice(256 * part, 256 * part + 256)
+def input_kernel(
+    preact_mid_ref, preact_edge_ref, grad_one_ref, w_expand_ref, scale_ref, grad_input_ref
+):
+    for rows, source, first in (
+        ((0, 7), preact_edge_ref, 0),
+        ((1, 2), preact_mid_ref, 0),
+        ((3, 4), preact_mid_ref, 256),
+        ((5, 6), preact_mid_ref, 512),
+    ):
         summed = jnp.zeros((256, D), F32)
         for pair in range(4):
             joined = jnp.concatenate(
-                [preact_ref[2 * pair, here, :], preact_ref[2 * pair + 1, here, :]], axis=1
+                [source[2 * pair + k, first : first + 256, :] for k in range(2)], axis=1
             )
             summed = summed + dot(joined, w_expand_ref[:, 256 * pair : 256 * pair + 256], 1, 1)
-        grad_one = grad_one_ref[2 * part : 2 * part + 2].reshape(256, D).astype(F32)
-        grad_input_ref[here, :] = (grad_one + summed * scale_ref[...]).astype(BF16)
+        summed = summed * scale_ref[...]
+        for k, row in enumerate(rows):
+            value = grad_one_ref[row].astype(F32) + summed[COLS * k : COLS * k + COLS]
+            grad_input_ref[row] = value.astype(BF16)
 
 
 VMEM = pl.BlockSpec(memory_space=pltpu.VMEM)
@@ -811,45 +1044,82 @@
     gain_block = gain_block.reshape(1, D)
     gain_grid = gain_grid.reshape(1, D)
     hidden = shape((BLOCKS, TOKENS, 128), BF16)
-    hidden_vmem = pltpu.VMEM((BLOCKS, TOKENS, 128), BF16)
+    hidden_mid = shape((BLOCKS, 6 * COLS, 128), BF16)
+    hidden_edge = shape((BLOCKS, 2 * COLS, 128), BF16)
+    hidden_vmem = pltpu.VMEM(hidden.shape, BF16)
+    mid_vmem = pltpu.VMEM(hidden_mid.shape, BF16)
+    edge_vmem = pltpu.VMEM(hidden_edge.shape, BF16)
+    pad_inner = pltpu.VMEM((BLOCKS, ROWS, WIDE, 128), F32)
+    pad_edge = pltpu.VMEM((BLOCKS, 6, WIDE, 128), F32)
     tile = shape((ROWS, COLS, D), BF16)
     tokens = shape((TOKENS, D), BF16)
     tokens_vmem = pltpu.VMEM((TOKENS, D), BF16)
     edge_row = shape((144, D), BF16)
     edge_column = shape((ROWS, D), BF16)
-    large = [
-        x_input,
+    dma = pltpu.SemaphoreType.DMA
+
+    x_input, x_left, x_right = call(
+        load_kernel,
+        [x_input],
+        [tile, edge_column, edge_column],
+        [dma, pltpu.VMEM((2, ROWS, D), F32)],
+        far=(0,),
+        keep=range(3),
+        limit=4,
+    )
+    x_left, x_right = beside_columns(x_left, x_right)
+    later = [
         w_expand,
+        dw_kernel,
         grad_output,
         w_project,
         w_qkv_block,
         w_out_block,
         w_qkv_grid,
         w_out_grid,
-        dw_kernel,
     ]
     (
-        x_input,
+        lifted_far,
+        slope_pre,
+        lifted,
         w_expand,
+        dw_kernel,
         grad_output,
         w_project,
         w_qkv_block,
         w_out_block,
         w_qkv_grid,
         w_out_grid,
-        dw_kernel,
-        x_left,
-        x_right,
     ) = call(
-        load_kernel,
-        large,
-        [shape(v.shape, v.dtype) for v in large] + [edge_column, edge_column],
-        [pltpu.SemaphoreType.DMA((len(large),)), pltpu.VMEM((2, ROWS, D), F32)],
-        far=range(len(large)),
-        keep=range(len(large) + 2),
+        expand_kernel,
+        [x_input, scale, shift] + later,
+        [hidden, hidden, hidden] + [shape(v.shape, v.dtype) for v in later],
+        [hidden_vmem, dma((ROWS, 2)), dma((len(later),))],
+        far=range(3, 3 + len(later)),
+        far_out=(0, 1),
+        keep=range(2, 3 + len(later)),
+        limit=8,
+        flops=4 * 10**9,
+    )
+    x_first, x_last = call(
+        x_edge_kernel,
+        [x_input, x_left, x_right],
+        [edge_row, edge_row],
+        [],
+        keep=(0, 1),
         limit=4,
     )
-    x_left, x_right = beside_columns(x_left, x_right)
+    x_top, x_bottom = beside_rows(x_first, x_last)
+    second_mid_far, second_mid, slope_mid, side_lifted = call(
+        inner_rows_kernel,
+        [lifted, x_left, x_right, scale, shift, w_expand, dw_kernel],
+        [hidden_mid, hidden_mid, hidden_mid, shape((BLOCKS, 16, 128), F32)],
+        [pad_inner, mid_vmem, dma((BLOCKS, 2))],
+        far_out=(0, 2),
+        keep=(1, 3),
+        limit=12,
+        flops=4 * 10**9,
+    )
     cube = shape((2, 64, 256), F32)
     cube_block, cube_grid = call(
         bias_kernel,
@@ -859,20 +1129,9 @@
         keep=(0, 1),
         limit=8,
     )
-    x_first, x_last = call(
-        x_edge_kernel,
-        [x_input, x_left, x_right],
-        [edge_row, edge_row],
-        [],
-        keep=(0, 1),
-        limit=4,
-    )
-    x_top, x_bottom = beside_rows(x_first, x_last)
     (
-        lifted,
-        slope_pre,
-        second,
-        slope_conv,
+        second_edge_far,
+        slope_edge,
         section_one,
         section_two,
         sendable,
@@ -886,8 +1145,9 @@
             x_input,
             x_top,
             x_bottom,
-            x_left,
-            x_right,
+            lifted,
+            side_lifted,
+            second_mid,
             scale,
             shift,
             w_expand,
@@ -901,10 +1161,8 @@
             grad_output,
         ],
         [
-            hidden,
-            hidden,
-            hidden,
-            hidden,
+            hidden_edge,
+            hidden_edge,
             tile,
             tile,
             shape((64, 32, D), BF16),
@@ -914,19 +1172,23 @@
             tokens,
         ],
         [
-            pltpu.VMEM((BLOCKS, ROWS + 2, WIDE, 128), F32),
+            pad_edge,
             pltpu.VMEM((ROWS, COLS, D), F32),
             pltpu.VMEM((ROWS, COLS, D), F32),
-            hidden_vmem,
-            hidden_vmem,
-            hidden_vmem,
+            edge_vmem,
+            edge_vmem,
+            pltpu.VMEM(tile.shape, BF16),
+            pltpu.VMEM(tile.shape, BF16),
             tokens_vmem,
+            pltpu.VMEM((TOKENS, 3 * D), BF16),
+            pltpu.VMEM((32, 64, 256), F32),
             tokens_vmem,
-            pltpu.SemaphoreType.DMA((5,)),
+            dma((3,)),
+            dma((4, 5)),
         ],
-        keep=(3, 4, 5, 6, 8, 9),
-        far_out=(0, 1, 2, 7, 10),
-        limit=24,
+        keep=(4,),
+        far_out=(0, 1, 2, 3, 5, 6, 7, 8),
+        limit=20,
     )
 
     got = across(sendable).transpose(1, 0, 2).reshape(2, TOKENS, D)
@@ -943,6 +1205,7 @@
     def block_half(parts, before):
         edge = [] if before else [shape((BLOCKS, ROWS, 128), BF16)] * 2
         half_vmem = pltpu.VMEM((TOKENS // 2, D), BF16)
+        half_tile = pltpu.VMEM((ROWS, COLS // 2, D), BF16)
         return call(
             functools.partial(block_kernel, parts),
             [
@@ -952,14 +1215,15 @@
                 section_one,
                 joined,
                 probs,
-                slope_conv.reshape(BLOCKS, ROWS, COLS, 128),
+                slope_mid.reshape(BLOCKS, 6, COLS, 128),
+                slope_edge.reshape(BLOCKS, 2, COLS, 128),
+                normed_block,
+                mixture,
                 gain_grid,
                 gain_block,
                 w_qkv_block,
                 w_out_block,
                 w_project,
-                normed_block,
-                mixture,
             ]
             + before,
             [
@@ -969,10 +1233,23 @@
             ]
             + edge,
             ([] if before else [pltpu.VMEM((2, BLOCKS, ROWS, 128), F32)])
-            + [half_vmem, half_vmem, pltpu.SemaphoreType.DMA((4,))],
-            far=(12, 13),
-            keep=range(3 + len(edge)),
-            limit=8,
+            + ([pltpu.VMEM((2048, 128), F32)] if before else [])
+            + [
+                half_tile,
+                half_tile,
+                pltpu.VMEM((TOKENS // 2, 3 * D), BF16),
+                pltpu.VMEM((16, 64, 256), F32),
+                pltpu.VMEM((BLOCKS, ROWS, COLS // 2, 128), BF16),
+                half_vmem,
+                half_vmem,
+                half_tile,
+                dma((2, 9)),
+                dma((3,)),
+            ],
+            far=range(2, 10),
+            far_out=(0, 2) if before else (0,),
+            keep=(1,) if before else (1, 2, 3, 4),
+            limit=12,
             flops=4*10**9,
         )
 
@@ -992,24 +1269,43 @@
     early = shape((3072, 128), BF16)
     grad_one, early_send, early_keep = call(
         total_kernel,
-        [core_flag, one_outer, one_middle, second, block_total, grid_total],
+        [
+            core_flag,
+            one_outer,
+            one_middle,
+            second_mid_far,
+            second_edge_far,
+            block_total,
+            grid_total,
+            first,
+        ],
         [tile, early, early],
-        [pltpu.VMEM((6144, 128), F32), hidden_vmem, pltpu.SemaphoreType.DMA],
+        [pltpu.VMEM((6144, 128), F32), hidden_vmem, dma((8,))],
         smem=(0,),
-        far=(3,),
+        far=range(1, 7),
         keep=range(3),
         limit=8,
-        flops=3*10**9,
+        flops=3 * 10**9,
+    )
+    preact_mid, taps_mid = call(
+        back_inner_kernel,
+        [lifted_far, slope_pre, inner_outer, inner_middle, left, right, dw_kernel],
+        [hidden_mid, shape((9, BLOCKS, 128), F32)],
+        [pad_inner, mid_vmem, mid_vmem, dma((BLOCKS, 2))],
+        far=(0, 1),
+        keep=(0, 1),
+        limit=12,
+        flops=4 * 10**9,
     )
     early_got = sibling(early_send)
     late = shape((CHUNKS, 24, 128), BF16)
     parts = shape((CHUNKS, CHUNK, 128), BF16)
-    preact, late_send, late_keep = call(
+    preact_edge, late_send, late_keep = call(
         back_kernel,
         [
             core_flag,
             x_input,
-            lifted,
+            lifted_far,
             slope_pre,
             inner_outer,
             inner_middle,
@@ -1020,26 +1316,28 @@
             scale,
             shift,
             dw_kernel,
+            preact_mid,
+            taps_mid,
             early_keep,
         ],
-        [hidden, late, late],
+        [hidden_edge, late, late],
         [
-            pltpu.VMEM((BLOCKS, ROWS + 2, WIDE, 128), F32),
+            pad_edge,
+            edge_vmem,
+            edge_vmem,
             tokens_vmem,
             pltpu.VMEM((2048, 128), F32),
             pltpu.VMEM((9, BLOCKS, 128), F32),
-            hidden_vmem,
-            hidden_vmem,
-            pltpu.SemaphoreType.DMA((BLOCKS, 2)),
+            dma((4,)),
         ],
         smem=(0,),
         far=(2, 3),
         keep=(0, 1, 2),
-        limit=20,
-        flops=10**10,
+        limit=12,
+        flops=4 * 10**9,
     )
     (grad_input,) = call(
-        input_kernel, [preact, grad_one, w_expand, scale], [tokens], [], limit=8
+        input_kernel, [preact_mid, preact_edge, grad_one, w_expand, scale], [tile], [], limit=8
     )
 
     (paired,) = call(
@@ -1068,7 +1366,7 @@
         smem=(0,),
         limit=16,
     )
-    return (grad_input.reshape(ROWS, COLS, D), *totals)
+    return (grad_input, *totals)
 
 
 def solution(mesh):

time: 197 us -> 186 us (0.944)
  blocking collectives: 98.8 us -> 76.5 us
  starting transfers between devices: 27.8 us -> 36.4 us
  Pallas kernels: 50.7 us -> 57.2 us
  local copies, waits for them, and re-layouts: 5.98 us -> 1.76 us
    all_to_all x4 -> x3, blocking collectives: 98.8 us -> 76.5 us  [across(): lax.all_to_all(values, ('row', 'hi'), split_axis=0, concat_axis=0, tiled=...]
    all_to_all x0 -> x1, waiting for transfers between devices: none -> 10.5 us  [across(): lax.all_to_all(values, ('row', 'hi'), split_axis=0, concat_axis=0, tiled=...]
    pallas_call x14 -> x17, Pallas kernels: 50.7 us -> 57.2 us  [call(): pl.pallas_call(kernel, out_shape=[pltpu.VMEM(o.shape, o.dtype) if k in ke...]
    all_to_all x0 -> x1, starting transfers between devices: none -> 6.12 us  [across(): lax.all_to_all(values, ('row', 'hi'), split_axis=0, concat_axis=0, tiled=...]
    unnamed x32 -> x14, local copies, waits for them, and re-layouts: 5.1 us -> 0.04 us
    ppermute x4, waiting for transfers between devices: 4.54 us -> 0.01 us  [beside_rows(): return (lax.ppermute(last, 'row', down), lax.ppermute(first, 'row', up))]
    ppermute x4, waiting for transfers between devices: 4.5 us -> 0.01 us  [beside_columns(): return (lax.ppermute(last, axes, right), lax.ppermute(first, axes, left))]
    ppermute x4, starting transfers between devices: 16 us -> 18.1 us  [beside_columns(): return (lax.ppermute(last, axes, right), lax.ppermute(first, axes, left))]
  transfers between devices with their start and end apart: 11 -> 12, of which waited for: 5 -> 3; matrix products, arithmetic and copies ran while one was open for 0% -> 0% of each run, Pallas kernels for 9% -> 17%
where the time goes in v3:
time: 186 us
  blocking collectives  76.5 us (41%)
  Pallas kernels  57.2 us (31%)
  starting transfers between devices  36.4 us (20%)
  waiting for transfers between devices  12.8 us (7%)
    all_to_all x3, blocking collectives, across(): lax.all_to_all(values, ('row', 'hi'), split_axis=0, concat_axis=0, tiled=...  76.5 us
    pallas_call x17, Pallas kernels, call(): pl.pallas_call(kernel, out_shape=[pltpu.VMEM(o.shape, o.dtype) if k in ke...  57.2 us
    ppermute x4, starting transfers between devices, beside_columns(): return (lax.ppermute(last, axes, right), lax.ppermute(first, axes, left))  18.1 us
    all_to_all x1, waiting for transfers between devices, across(): lax.all_to_all(values, ('row', 'hi'), split_axis=0, concat_axis=0, tiled=...  10.5 us
    ppermute x4, starting transfers between devices, beside_rows(): return (lax.ppermute(last, 'row', down), lax.ppermute(first, 'row', up))  7.91 us
    all_to_all x1, starting transfers between devices, across(): lax.all_to_all(values, ('row', 'hi'), split_axis=0, concat_axis=0, tiled=...  6.12 us
    ppermute x3, starting transfers between devices, sibling(): return lax.ppermute(values, 'core', [(0, 1), (1, 0)])  4.27 us
  transfers between devices with their start and end apart: 12, of which 3 were waited for; matrix products, arithmetic and copies ran while one was open for 0% of the time, Pallas kernels for 17%

profile of v3, /device:TPU:1, one launch (start us, length us, event | category | flops | bytes accessed | tf_op | source)
XLA Modules:
  0.0 185.7 jit_solution(10364141957366691394)
XLA Ops:
  0.7 1.1 shard_map.206
  1.7 6.9 %collective-permute-start = (bf16[8,256]{1,0:T(8,128)(2,1)S(1)}, bf16[8,256]{1,0:T(8,128)(2,1)S(1)}, u32[]{:S(2)}, u32[]{:S(2)}) collective-permute-start(bf16[8,256]{1,0:T(8,128)(2,1)S(1)} %get-tuple-element.69), channel_id=1, source_target_pairs={{0,1},{1,2},{2,3},{3,4},{4,5},{5,6},{6,7},{7,8},{8,9},{9,10},{10,1... | collective-permute-start | bytes 12296 | tf_op jit(solution)/shard_map/ppermute | solution.py:1013
  8.7 1.9 %collective-permute-start.1 = (bf16[8,256]{1,0:T(8,128)(2,1)S(1)}, bf16[8,256]{1,0:T(8,128)(2,1)S(1)}, u32[]{:S(2)}, u32[]{:S(2)}) collective-permute-start(bf16[8,256]{1,0:T(8,128)(2,1)S(1)} %get-tuple-element.70), channel_id=1, source_target_pairs={{1,0},{2,1},{3,2},{4,3},{5,4},{6,5},{7,6},{8,7},{9,8},{10,9},{11,1... | collective-permute-start | bytes 12296 | tf_op jit(solution)/shard_map/ppermute | solution.py:1013
  10.6 0.0 copy-start.4
  10.6 0.0 copy-start.5
  10.6 5.4 %shard_map.207 = (bf16[8,1024,128]{2,1,0:T(8,128)(2,1)}, bf16[8,1024,128]{2,1,0:T(8,128)(2,1)}, bf16[8,1024,128]{2,1,0:T(8,128)(2,1)S(1)}, bf16[256,1024]{1,0:T(...) custom-call(bf16[8,128,256]{2,1,0:T(8,128)(2,1)S(1)} %get-tuple-elem, ...), custom_call_target="tpu_custom_call" | custom-call | flops 4000000000 | bytes 40000000 | tf_op jit(solution)/shard_map/pallas_call | solution.py:909
  16.1 0.6 shard_map.210
  16.7 0.0 collective-permute-done.left_ref
  16.7 3.2 %collective-permute-start.2 = (bf16[144,256]{1,0:T(8,128)(2,1)S(1)}, bf16[144,256]{1,0:T(8,128)(2,1)S(1)}, u32[]{:S(2)}, u32[]{:S(2)}) collective-permute-start(bf16[144,256]{1,0:T(8,128)(2,1)S(1)} %get-tuple-element.71), channel_id=1, source_target_pairs={{0,16},{16,32},{32,48},{48,64},{64,80},{80,96},{96,112},{1,17},{17... | collective-permute-start | bytes 221192 | tf_op jit(solution)/shard_map/ppermute | solution.py:1005
  20.0 1.3 collective-permute-start.3
  21.3 0.0 copy-start
  21.3 0.0 copy-start.1
  21.3 5.5 %shard_map.209 = (bf16[8,768,128]{2,1,0:T(8,128)(2,1)}, bf16[8,768,128]{2,1,0:T(8,128)(2,1)S(1)}, bf16[8,768,128]{2,1,0:T(8,128)(2,1)}, f32[8,16,128]{2,1,0:T(8,128)S(1)}) custom-call(bf16[8,1024,128]{2,1,0:T(8,128)(2,1)S(1)} %get-tuple-element.73.lifted_ref, bf16[8,256]{1,0:T(8,128)(2,1)S(1)} %collective-permute-done.left_ref, ...), custom_call_target="tpu_custom_call" | custom-call | flops 4000000000 | bytes 40000000 | tf_op jit(solution)/shard_map/pallas_call | solution.py:909
  26.8 0.0 collective-permute-done.3.bottom_ref
  26.8 9.0 %shard_map.211 = (bf16[8,256,128]{2,1,0:T(8,128)(2,1)}, bf16[8,256,128]{2,1,0:T(8,128)(2,1)}, bf16[8,128,256]{2,1,0:T(8,128)(2,1)}, bf16[8,128,256]{2,1,0:T(8,12...) custom-call(bf16[8,128,256]{2,1,0:T(8,128)(2,1)S(1)} %get-tuple-elem, ...), custom_call_target="tpu_custom_call" | custom-call | flops 1000000000 | bytes 10000000 | tf_op jit(solution)/shard_map/pallas_call | solution.py:909
  35.8 23.6 %all_to_all.20 = bf16[64,32,256]{2,1,0:T(8,128)(2,1)S(1)} all-to-all(bf16[64,32,256]{2,1,0:T(8,128)(2,1)S(1)} %get-tuple-element.83), channel_id=1, replica_groups=mesh['row'=8,'hi'=8,'core'=2] {'row','hi'}, dimensions={0} | all-to-all | bytes 2097152 | tf_op jit(solution)/shard_map/all_to_all | solution.py:1017
  59.4 0.6 copy.23
  60.0 7.0 %shard_map.212 = (bf16[1024,256]{1,0:T(8,128)(2,1)S(1)}, f32[2048,128]{1,0:T(8,128)S(1)}) custom-call(bf16[2,1024,256]{2,1,0:T(8,128)(2,1)S(1)} %bitcast.14, bf16[256,768]{1,0:T(8,128)(2,1)S(1)} %get-tuple-element.84.w_qkv_ref, bf16[256,256]{1,0:T(8,128)(2,1)S(1)} %get-tuple-element.85.w_out_ref, f32[2,64,256]{2,1,0:T(8,128)S(1)} %get-tuple-element.86.bias), custom_call_target="tpu_custom_call" | custom-call | flops 1000000000 | bytes 10000000 | tf_op jit(solution)/shard_map/pallas_call | solution.py:909
  67.0 0.0 copy-start.6
  67.0 1.1 copy.26
  68.1 6.1 %all-to-all-start.1 = ((bf16[64,16,256]{2,1,0:T(8,128)(2,1)}), bf16[64,16,256]{2,1,0:T(8,128)(2,1)S(1)}, u32[]{:S(2)}, u32[]{:S(2)}) async-start(bf16[64,16,256]{2,1,0:T(8,128)(2,1)} %bitcast.34), calls=%async_computation.1 | async-start | bytes 1048576 | tf_op jit(solution)/shard_map/all_to_all | solution.py:1017
  74.3 10.5 %all-to-all-done.1 = bf16[64,16,256]{2,1,0:T(8,128)(2,1)S(1)} async-done(((bf16[64,16,256]{2,1,0:T(8,128)(2,1)}), bf16[64,16,256]{2,1,0:T(8,128)(2,1)S(1)}, u32[]{:S(2)}, u32[]{:S(2)}) %all-to-all-start.1) | async-done | bytes 524320 | tf_op jit(solution)/shard_map/all_to_all | solution.py:1017
  84.8 5.8 %shard_map.213 = (bf16[8,64,256]{2,1,0:T(8,128)(2,1)}, bf16[8,8,64,128]{3,2,1,0:T(8,128)(2,1)S(1)}, f32[2048,128]{1,0:T(8,128)S(1)}, bf16[8,8,128]{2,1,0:T(8,128)(2,1)S(1)}, bf16[8,8,128]{2,1,0:T(8,128)(2,1)S(1)}) custom-call(bf16[8,128,256]{2,1,0:T(8,128)(2,1)S(1)} %bitcast.15, bf16[8,128,256]{2,1,0:T(8,128)(2,1)S(1)} %get-tuple-element.82.grad_output_ref, ...), custom_call_target="tpu_custom_call" | custom-call | flops 4000000000 | bytes 40000000 | tf_op jit(solution)/shard_map/pallas_call | solution.py:909
  90.6 7.3 %collective-permute-start.4 = (bf16[8,8,128]{2,1,0:T(8,128)(2,1)S(1)}, bf16[8,8,128]{2,1,0:T(8,128)(2,1)S(1)}, u32[]{:S(2)}, u32[]{:S(2)}) collective-permute-start(bf16[8,8,128]{2,1,0:T(8,128)(2,1)S(1)} %get-tuple-element.99), channel_id=1, source_target_pairs={{0,1},{1,2},{2,3},{3,4},{4,5},{5,6},{6,7},{7,8},{8,9},{9,10},{10,1... | collective-permute-start | bytes 49160 | tf_op jit(solution)/shard_map/ppermute | solution.py:1013
  97.9 1.9 %collective-permute-start.5 = (bf16[8,8,128]{2,1,0:T(8,128)(2,1)S(1)}, bf16[8,8,128]{2,1,0:T(8,128)(2,1)S(1)}, u32[]{:S(2)}, u32[]{:S(2)}) collective-permute-start(bf16[8,8,128]{2,1,0:T(8,128)(2,1)S(1)} %get-tuple-element.100), channel_id=1, source_target_pairs={{1,0},{2,1},{3,2},{4,3},{5,4},{6,5},{7,6},{8,7},{9,8},{10,9},{11,1... | collective-permute-start | bytes 49160 | tf_op jit(solution)/shard_map/ppermute | solution.py:1013
  99.9 6.1 %shard_map.214 = (bf16[8,64,256]{2,1,0:T(8,128)(2,1)}, bf16[8,8,64,128]{3,2,1,0:T(8,128)(2,1)S(1)}, f32[2048,128]{1,0:T(8,128)}) custom-call(bf16[8,128,256]{2,1,0:T(8,128)(2,1)S(1)} %bitcast.16, bf16[8,128,256]{2,1,0:T(8,128)(2,1)S(1)} %get-tuple-element.82.grad_output_ref, bf16[8,128,256]{2,1,0:T(8,128)(2,1)} %get-tuple-element.88.section_two_in, ...), custom_call_target="tpu_custom_call" | custom-call | flops 4000000000 | bytes 40000000 | tf_op jit(solution)/shard_map/pallas_call | solution.py:909
  106.0 0.0 collective-permute-done.4.left_ref
  106.0 0.0 collective-permute-done.5.right_ref
  106.0 0.1 shard_map.216
  106.1 2.1 %collective-permute-start.6 = (bf16[8,144,128]{2,1,0:T(8,128)(2,1)S(1)}, bf16[8,144,128]{2,1,0:T(8,128)(2,1)S(1)}, u32[]{:S(2)}, u32[]{:S(2)}) collective-permute-start(bf16[8,144,128]{2,1,0:T(8,128)(2,1)S(1)} %get-tuple-element.102), channel_id=1, source_target_pairs={{0,16},{16,32},{32,48},{48,64},{64,80},{80,96},{96,112},{1,17},{17... | collective-permute-start | bytes 884744 | tf_op jit(solution)/shard_map/ppermute | solution.py:1005
  108.2 1.3 collective-permute-start.7
  109.5 2.7 %shard_map.217 = (bf16[8,128,256]{2,1,0:T(8,128)(2,1)S(1)}, bf16[3072,128]{1,0:T(8,128)(2,1)S(1)}, bf16[3072,128]{1,0:T(8,128)(2,1)S(1)}) custom-call(s32[1]{0:T(128)} %bitcast.11.core_ref, bf16[8,64,256]{2,1,0:T(8,128)(2,1)} %get-tuple-element.105.outer_in, bf16[8,64,256]{2,1,0:T(8,128)(2,1)} %get-tuple-element.106.middle_in, ...), custom_call_target="tpu_custom_call" | custom-call | flops 3000000000 | bytes 30000000 | tf_op jit(solution)/shard_map/pallas_call | solution.py:909
  112.3 0.1 collective-permute-start.8
  112.4 5.7 %shard_map.215 = (bf16[8,768,128]{2,1,0:T(8,128)(2,1)S(1)}, f32[9,8,128]{2,1,0:T(8,128)S(1)}) custom-call(bf16[8,1024,128]{2,1,0:T(8,128)(2,1)} %get-tuple-element.67.lifted_in, bf16[8,1024,128]{2,1,0:T(8,128)(2,1)} %get-tuple-element.68.slope_pre_in, bf16[8,8,64,128]{3,2,1,0:T(8,128)(2,1)S(1)} %get-tuple-element.96.outer_ref, ...), custom_call_target="tpu_custom_call" | custom-call | flops 4000000000 | bytes 40000000 | tf_op jit(solution)/shard_map/pallas_call | solution.py:909
  118.1 0.0 collective-permute-done.6.top_ref
  118.1 0.0 collective-permute-done.7.bottom_ref
  118.1 3.7 %shard_map.218 = (bf16[8,256,128]{2,1,0:T(8,128)(2,1)S(1)}, bf16[64,24,128]{2,1,0:T(8,128)(2,1)S(1)}, bf16[64,24,128]{2,1,0:T(8,128)(2,1)S(1)}) custom-call(s32[1]{0:T(128)} %bitcast.11.core_ref, bf16[8,128,256]{2,1,0:T(8,128)(2,1)S(1)} %get-tuple-element.66.x_ref, bf16[8,1024,128]{2,1,0:T(8,128)(2,1)} %get-tuple-element.67.lifted_in, ...), custom_call_target="tpu_custom_call" | custom-call | flops 4000000000 | bytes 40000000 | tf_op jit(solution)/shard_map/pallas_call | solution.py:909
  121.8 0.6 collective-permute-start.9
  122.4 1.3 collective-permute-done.9.late_got_ref
  123.8 0.0 collective-permute-done.8.early_got_ref
  123.8 0.3 shard_map.220
  124.0 30.3 %all_to_all.21.got_ref = bf16[64,72,128]{2,1,0:T(8,128)(2,1)S(1)} all-to-all(bf16[64,72,128]{2,1,0:T(8,128)(2,1)S(1)} %shard_map.220), channel_id=1, replica_groups=mesh['row'=8,'hi'=8,'core'=2] {'row','hi'}, dimensions={0} | all-to-all | bytes 2359296 | tf_op jit(solution)/shard_map/all_to_all | solution.py:1017
  154.3 0.3 shard_map.221
  154.6 22.6 %all_to_all.22.mine_ref = bf16[64,72,128]{2,1,0:T(8,128)(2,1)S(1)} all-to-all(bf16[64,72,128]{2,1,0:T(8,128)(2,1)S(1)} %shard_map.221), channel_id=1, replica_groups=mesh['row'=8,'hi'=8,'core'=2] {'row','hi'}, dimensions={0} | all-to-all | bytes 2359296 | tf_op jit(solution)/shard_map/all_to_all | solution.py:1017
  177.2 3.6 %collective-permute-start.10 = (bf16[64,72,128]{2,1,0:T(8,128)(2,1)S(1)}, bf16[64,72,128]{2,1,0:T(8,128)(2,1)S(1)}, u32[]{:S(2)}, u32[]{:S(2)}) collective-permute-start(bf16[64,72,128]{2,1,0:T(8,128)(2,1)S(1)} %all_to_all.22.mine_ref), channel_id=1, source_target_pairs={{0,1},{1,0},{2,3},{3,2},{4,5},{5,4},{6,7},{7,6},{8,9},{9,8},{10,11... | collective-permute-start | bytes 3538952 | tf_op jit(solution)/shard_map/ppermute | solution.py:1021
  180.8 1.5 shard_map.219
  182.4 0.9 collective-permute-done.10.other_ref
  183.3 2.4 %shard_map.222 = (f32[256,1024]{1,0:T(8,128)}, f32[9,1024]{1,0:T(8,128)}, f32[1024,256]{1,0:T(8,128)}, f32[256,768]{1,0:T(8,128)}, f32[256,256]{1,0:T(8,128)}, /*index=5*/f32[256,768]{1,0:T(8,128)}, f32[256,256]{1,0:T(8,128)}) custom-call(s32[1]{0:T(128)} %bitcast.11.core_ref, bf16[64,72,128]{2,1,0:T(8,128)(2,1)S(1)} %all_to_all.22.mine_ref, ...), custom_call_target="tpu_custom_call" | custom-call | flops 1000000000 | bytes 10000000 | tf_op jit(solution)/shard_map/pallas_call | solution.py:909
  (12 shorter events, 0.0 us)
Async XLA Ops:
  0.6 9.9 %copy-start.3 = (f32[256]{0:T(256)S(1)}, f32[256]{0:T(256)}, u32[]{:S(2)}) copy-start(f32[256]{0:T(256)} %param.17) | copy-start | bytes 3076
  0.6 9.9 %copy-start.2 = (f32[256]{0:T(256)S(1)}, f32[256]{0:T(256)}, u32[]{:S(2)}) copy-start(f32[256]{0:T(256)} %param.18) | copy-start | bytes 3076
  1.7 15.0 %collective-permute-start = (bf16[8,256]{1,0:T(8,128)(2,1)S(1)}, bf16[8,256]{1,0:T(8,128)(2,1)S(1)}, u32[]{:S(2)}, u32[]{:S(2)}) collective-permute-start(bf16[8,256]{1,0:T(8,128)(2,1)S(1)} %get-tuple-element.69), channel_id=1, source_target_pairs={{0,1},{1,2},{2,3},{3,4},{4,5},{5,6},{6,7},{7,8},{8,9},{9,10},{10,1... | collective-permute-start | bytes 12296 | tf_op jit(solution)/shard_map/ppermute | solution.py:1013
  8.7 8.1 %collective-permute-start.1 = (bf16[8,256]{1,0:T(8,128)(2,1)S(1)}, bf16[8,256]{1,0:T(8,128)(2,1)S(1)}, u32[]{:S(2)}, u32[]{:S(2)}) collective-permute-start(bf16[8,256]{1,0:T(8,128)(2,1)S(1)} %get-tuple-element.70), channel_id=1, source_target_pairs={{1,0},{2,1},{3,2},{4,3},{5,4},{6,5},{7,6},{8,7},{9,8},{10,9},{11,1... | collective-permute-start | bytes 12296 | tf_op jit(solution)/shard_map/ppermute | solution.py:1013
  10.6 5.5 %copy-start.4 = (f32[8,225]{1,0:T(8,128)S(1)}, f32[8,225]{1,0:T(8,128)}, u32[]{:S(2)}) copy-start(f32[8,225]{1,0:T(8,128)} %block_ref.1) | copy-start | bytes 21604
  10.6 5.5 %copy-start.5 = (f32[8,225]{1,0:T(8,128)S(1)}, f32[8,225]{1,0:T(8,128)}, u32[]{:S(2)}) copy-start(f32[8,225]{1,0:T(8,128)} %grid_ref.1) | copy-start | bytes 21604
  16.7 10.0 %collective-permute-start.2 = (bf16[144,256]{1,0:T(8,128)(2,1)S(1)}, bf16[144,256]{1,0:T(8,128)(2,1)S(1)}, u32[]{:S(2)}, u32[]{:S(2)}) collective-permute-start(bf16[144,256]{1,0:T(8,128)(2,1)S(1)} %get-tuple-element.71), channel_id=1, source_target_pairs={{0,16},{16,32},{32,48},{48,64},{64,80},{80,96},{96,112},{1,17},{17... | collective-permute-start | bytes 221192 | tf_op jit(solution)/shard_map/ppermute | solution.py:1005
  20.0 6.8 %collective-permute-start.3 = (bf16[144,256]{1,0:T(8,128)(2,1)S(1)}, bf16[144,256]{1,0:T(8,128)(2,1)S(1)}, u32[]{:S(2)}, u32[]{:S(2)}) collective-permute-start(bf16[144,256]{1,0:T(8,128)(2,1)S(1)} %get-tuple-element.72), channel_id=1, source_target_pairs={{16,0},{32,16},{48,32},{64,48},{80,64},{96,80},{112,96},{17,1},{33... | collective-permute-start | bytes 221192 | tf_op jit(solution)/shard_map/ppermute | solution.py:1005
  21.3 5.5 %copy-start = (f32[256]{0:T(256)S(1)}, f32[256]{0:T(256)}, u32[]{:S(2)}) copy-start(f32[256]{0:T(256)} %param.22) | copy-start | bytes 3076
  21.3 5.5 %copy-start.1 = (f32[256]{0:T(256)S(1)}, f32[256]{0:T(256)}, u32[]{:S(2)}) copy-start(f32[256]{0:T(256)} %param.26) | copy-start | bytes 3076
  67.0 1.1 copy-start.6
  68.1 16.7 %all-to-all-start.1 = ((bf16[64,16,256]{2,1,0:T(8,128)(2,1)}), bf16[64,16,256]{2,1,0:T(8,128)(2,1)S(1)}, u32[]{:S(2)}, u32[]{:S(2)}) async-start(bf16[64,16,256]{2,1,0:T(8,128)(2,1)} %bitcast.34), calls=%async_computation.1 | async-start | bytes 1048576 | tf_op jit(solution)/shard_map/all_to_all | solution.py:1017
  90.6 15.4 %collective-permute-start.4 = (bf16[8,8,128]{2,1,0:T(8,128)(2,1)S(1)}, bf16[8,8,128]{2,1,0:T(8,128)(2,1)S(1)}, u32[]{:S(2)}, u32[]{:S(2)}) collective-permute-start(bf16[8,8,128]{2,1,0:T(8,128)(2,1)S(1)} %get-tuple-element.99), channel_id=1, source_target_pairs={{0,1},{1,2},{2,3},{3,4},{4,5},{5,6},{6,7},{7,8},{8,9},{9,10},{10,1... | collective-permute-start | bytes 49160 | tf_op jit(solution)/shard_map/ppermute | solution.py:1013
  97.9 8.1 %collective-permute-start.5 = (bf16[8,8,128]{2,1,0:T(8,128)(2,1)S(1)}, bf16[8,8,128]{2,1,0:T(8,128)(2,1)S(1)}, u32[]{:S(2)}, u32[]{:S(2)}) collective-permute-start(bf16[8,8,128]{2,1,0:T(8,128)(2,1)S(1)} %get-tuple-element.100), channel_id=1, source_target_pairs={{1,0},{2,1},{3,2},{4,3},{5,4},{6,5},{7,6},{8,7},{9,8},{10,9},{11,1... | collective-permute-start | bytes 49160 | tf_op jit(solution)/shard_map/ppermute | solution.py:1013
  106.1 12.0 %collective-permute-start.6 = (bf16[8,144,128]{2,1,0:T(8,128)(2,1)S(1)}, bf16[8,144,128]{2,1,0:T(8,128)(2,1)S(1)}, u32[]{:S(2)}, u32[]{:S(2)}) collective-permute-start(bf16[8,144,128]{2,1,0:T(8,128)(2,1)S(1)} %get-tuple-element.102), channel_id=1, source_target_pairs={{0,16},{16,32},{32,48},{48,64},{64,80},{80,96},{96,112},{1,17},{17... | collective-permute-start | bytes 884744 | tf_op jit(solution)/shard_map/ppermute | solution.py:1005
  108.2 9.9 %collective-permute-start.7 = (bf16[8,144,128]{2,1,0:T(8,128)(2,1)S(1)}, bf16[8,144,128]{2,1,0:T(8,128)(2,1)S(1)}, u32[]{:S(2)}, u32[]{:S(2)}) collective-permute-start(bf16[8,144,128]{2,1,0:T(8,128)(2,1)S(1)} %get-tuple-element.103._), channel_id=1, source_target_pairs={{16,0},{32,16},{48,32},{64,48},{80,64},{96,80},{112,96},{17,1},{33... | collective-permute-start | bytes 884744 | tf_op jit(solution)/shard_map/ppermute | solution.py:1005
  112.3 11.5 %collective-permute-start.8 = (bf16[3072,128]{1,0:T(8,128)(2,1)S(1)}, bf16[3072,128]{1,0:T(8,128)(2,1)S(1)}, u32[]{:S(2)}, u32[]{:S(2)}) collective-permute-start(bf16[3072,128]{1,0:T(8,128)(2,1)S(1)} %get-tuple-element.114), channel_id=1, source_target_pairs={{0,1},{1,0},{2,3},{3,2},{4,5},{5,4},{6,7},{7,6},{8,9},{9,8},{10,11... | collective-permute-start | bytes 2359304 | tf_op jit(solution)/shard_map/ppermute | solution.py:1021
  121.8 1.9 %collective-permute-start.9 = (bf16[64,24,128]{2,1,0:T(8,128)(2,1)S(1)}, bf16[64,24,128]{2,1,0:T(8,128)(2,1)S(1)}, u32[]{:S(2)}, u32[]{:S(2)}) collective-permute-start(bf16[64,24,128]{2,1,0:T(8,128)(2,1)S(1)} %get-tuple-element.116), channel_id=1, source_target_pairs={{0,1},{1,0},{2,3},{3,2},{4,5},{5,4},{6,7},{7,6},{8,9},{9,8},{10,11... | collective-permute-start | bytes 1179656 | tf_op jit(solution)/shard_map/ppermute | solution.py:1021
  177.2 6.1 %collective-permute-start.10 = (bf16[64,72,128]{2,1,0:T(8,128)(2,1)S(1)}, bf16[64,72,128]{2,1,0:T(8,128)(2,1)S(1)}, u32[]{:S(2)}, u32[]{:S(2)}) collective-permute-start(bf16[64,72,128]{2,1,0:T(8,128)(2,1)S(1)} %all_to_all.22.mine_ref), channel_id=1, source_target_pairs={{0,1},{1,0},{2,3},{3,2},{4,5},{5,4},{6,7},{7,6},{8,9},{9,8},{10,11... | collective-permute-start | bytes 3538952 | tf_op jit(solution)/shard_map/ppermute | solution.py:1021

commit v4 on v3

--- a/solution.py
+++ b/solution.py
@@ -67,15 +67,16 @@
     )
 
 
-def load_kernel(x_in, x_ref, left_ref, right_ref, sem, ends):
+def load_kernel(x_in, x_ref, near_ref, next_ref, sem, ends):
     copy = pltpu.make_async_copy(x_in, x_ref, sem)
     copy.start()
     copy.wait()
     for row in range(ROWS):
         ends[0, row : row + 1, :] = x_ref[row, 0:16, :].astype(F32)[0:1]
         ends[1, row : row + 1, :] = x_ref[row, COLS - 16 : COLS, :].astype(F32)[15:16]
-    left_ref[...] = ends[0].astype(BF16)
-    right_ref[...] = ends[1].astype(BF16)
+    near, after = trade(ends[1], ends[0])
+    near_ref[...] = near.astype(BF16)
+    next_ref[...] = after.astype(BF16)
 
 
 def with_corners(cells, left, right):
@@ -84,20 +85,20 @@
     return jnp.concatenate([cells, corners], axis=0)
 
 
-def x_edge_kernel(x_ref, left_ref, right_ref, first_ref, last_ref):
-    left = left_ref[...].astype(F32)
-    right = right_ref[...].astype(F32)
-    for row, target in ((0, first_ref), (ROWS - 1, last_ref)):
-        target[...] = with_corners(x_ref[row], left[row : row + 1], right[row : row + 1])
-
-
-def inner_edge_kernel(outer_ref, middle_ref, left_ref, right_ref, first_ref, last_ref):
+def x_edge_kernel(x_ref, near_ref, next_ref, pair_ref, other_ref):
+    right, left = trade(near_ref[...], next_ref[...])
+    even = even_row()
+    for last, target in ((even, pair_ref), (1 - even, other_ref)):
+        target[...] = with_corners(x_ref[7 * last], edge_of(last, left), edge_of(last, right))
+
+
+def inner_edge_kernel(outer_ref, middle_ref, near_ref, next_ref, pair_ref, other_ref):
+    even = even_row()
     for block in range(BLOCKS):
-        left = left_ref[block].astype(F32)
-        right = right_ref[block].astype(F32)
-        for row, target in ((0, first_ref), (ROWS - 1, last_ref)):
-            cells = whole_row(outer_ref[block, row], middle_ref[block, row])
-            target[block] = with_corners(cells, left[row : row + 1], right[row : row + 1])
+        right, left = trade(near_ref[block], next_ref[block])
+        for last, target in ((even, pair_ref), (1 - even, other_ref)):
+            cells = whole_row(outer_ref[block, 7 * last], middle_ref[block, 7 * last])
+            target[block] = with_corners(cells, edge_of(last, left), edge_of(last, right))
 
 
 def whole_row(outer, middle):
@@ -225,6 +226,22 @@
     return (tokens.astype(F32) * scale_ref[...] + shift_ref[...]).astype(BF16)
 
 
+def trade(first, second):
+    here = jnp.where(lax.axis_index("core") == 0, 1.0, 0.0).astype(F32)
+    first, second = first.astype(F32), second.astype(F32)
+    there = 1.0 - here
+    return first * here + second * there, first * there + second * here
+
+
+def even_row():
+    return 1 - lax.rem(lax.axis_index("row"), 2)
+
+
+def edge_of(even, value):
+    last = even.astype(F32)
+    return value[7:8] * last + value[0:1] * (1.0 - last)
+
+
 def copy_all(pairs, sems, first=0):
     copies = [
         pltpu.make_async_copy(source, target, sems.at[first + k])
@@ -249,7 +266,7 @@
     count = (len(refs) - 6) // 2
     sources, (lifted_out, slope_pre_out, lifted_ref) = refs[:count], refs[count : count + 3]
     targets, (slope_pre_ref, sems, load_sems) = refs[count + 3 : -3], refs[-3:]
-    loads = copy_all(list(zip(sources, targets)), load_sems)
+    loads = copy_all([(sources[0], targets[0])], load_sems)
     w_expand_ref = targets[0]
 
     def stores(row):
@@ -261,7 +278,8 @@
             )
         ]
 
-    wait_all(loads[:1])
+    wait_all(loads)
+    loads = copy_all(list(zip(sources[1:], targets[1:])), load_sems, first=1)
 
     @pl.loop(0, ROWS)
     def _(row):
@@ -280,7 +298,7 @@
         for copy in stores(row):
             copy.start()
 
-    wait_all(loads[1:])
+    wait_all(loads)
     for row in range(ROWS):
         wait_all(stores(row))
 
@@ -305,8 +323,8 @@
 
 def inner_rows_kernel(
     lifted_ref,
-    left_ref,
-    right_ref,
+    near_ref,
+    next_ref,
     scale_ref,
     shift_ref,
     w_expand_ref,
@@ -328,7 +346,8 @@
         ]
 
     inside = edge_flags()
-    sides = jnp.concatenate([left_ref[...], right_ref[...]], axis=0)
+    right, left = trade(near_ref[...], next_ref[...])
+    sides = jnp.concatenate([left, right], axis=0)
     shifted = shift_scale(sides, scale_ref, shift_ref)
     place = lax.broadcasted_iota(jnp.int32, (16, 1), 0)
     flags = jnp.where(place < 8, inside[2], inside[3])
@@ -349,8 +368,7 @@
             pad[block, row, LEFT - 1 : LEFT, :] = side[row : row + 1]
             pad[block, row, LEFT + COLS : LEFT + COLS + 1, :] = side[8 + row : 9 + row]
 
-        @pl.loop(0, ROWS - 2)
-        def _(row):
+        for row in range(ROWS - 2):
             convolve_rows(pad, block, row, taps, second_ref, slope_conv_ref, row)
 
         for copy in stores(block):
@@ -362,8 +380,8 @@
 
 def front_kernel(
     x_ref,
-    top_ref,
-    bottom_ref,
+    pair_ref,
+    other_ref,
     lifted_ref,
     side_ref,
     second_mid_ref,
@@ -404,7 +422,10 @@
     send_ref[:, 16:32, :] = grad_output_ref[...].reshape(64, 16, D)
     heads_mask = heads_mask_of()
     inside = edge_flags()
-    for source, row, flag in ((top_ref, 0, inside[0]), (bottom_ref, 5, inside[1])):
+    even = even_row()
+    for source, below in ((pair_ref, even), (other_ref, 1 - even)):
+        row = 5 * below
+        flag = inside[1] * below.astype(F32) + inside[0] * (1 - below).astype(F32)
         shifted = shift_scale(source[...], scale_ref, shift_ref)
         for pair in range(4):
             value, _ = gelu_pair(dot(shifted, w_expand_ref[:, 256 * pair : 256 * pair + 256], 1, 0))
@@ -459,8 +480,8 @@
     stores += copy_all([(section_one_ref, section_one_out)], sems, first=2)
 
     def part_stores(part):
-        here = pl.ds(pl.multiple_of(part * 256, 256), 256)
-        columns = pl.ds(pl.multiple_of(part * 32, 32), 32)
+        here = pl.ds(part * 256, 256)
+        columns = pl.ds(part * 32, 32)
         eight = pl.ds(part * 8, 8)
         return [
             pltpu.make_async_copy(source, target, part_sems.at[part, k])
@@ -475,10 +496,9 @@
             )
         ]
 
-    @pl.loop(0, 4)
-    def _(part):
-        here = pl.ds(pl.multiple_of(part * 256, 256), 256)
-        columns = pl.ds(pl.multiple_of(part * 32, 32), 32)
+    for part in range(4):
+        here = slice(256 * part, 256 * part + 256)
+        columns = slice(32 * part, 32 * part + 32)
         section_one = four_windows(cells[:, columns, :])
         normed = (norm_parts(section_one)[0] * gain_block_ref[...]).astype(BF16)
         normed_block_ref[here, :] = normed
@@ -515,9 +535,8 @@
     normed_ref = got_ref.at[0]
     grad_ref = got_ref.at[1]
 
-    @pl.loop(0, 4)
-    def _(part):
-        here = pl.ds(pl.multiple_of(part * 256, 256), 256)
+    for part in range(4):
+        here = slice(256 * part, 256 * part + 256)
         joined = dot(normed_ref[here, :], w_qkv_ref[...], 1, 0).astype(BF16)
         grad_mix = dot(grad_ref[here, :], w_out_ref[...], 1, 1).astype(BF16)
         probs, mixture = attend(joined, bias, heads_mask)
@@ -562,18 +581,20 @@
     ) = rest[-10:]
     if len(rest) == 16:
         before_ref = None
-        grad_one_out, inner_ref, total_ref, left_ref, right_ref, ends = rest[:-10]
+        grad_one_out, inner_ref, total_ref, near_ref, next_ref, ends = rest[:-10]
     else:
         before_ref, grad_one_out, inner_ref, total_out, total_ref = rest[:-10]
-    fetches = []
     stores = []
-    for index, part in enumerate(parts):
+
+    def fetch(index):
+        part = parts[index]
         here = pl.ds(256 * part, 256)
         target = pl.ds(256 * index, 256)
         columns = pl.ds(32 * part, 32)
         to = pl.ds(32 * index, 32)
-        fetches.append(
-            copy_all(
+        return [
+            pltpu.make_async_copy(source, goal, fetch_sems.at[index, k])
+            for k, (source, goal) in enumerate(
                 (
                     (section_two_in.at[:, columns, :], section_two_ref.at[:, to, :]),
                     (joined_in.at[here, :], joined_ref.at[target, :]),
@@ -593,10 +614,13 @@
                     ),
                     (normed_block_in.at[here, :], normed_block_ref.at[target, :]),
                     (mixture_in.at[here, :], mixture_ref.at[target, :]),
-                ),
-                fetch_sems.at[index],
+                )
             )
-        )
+        ]
+
+    fetches = [fetch(0), fetch(1)]
+    for copy in fetches[0][:3]:
+        copy.start()
     heads_mask = heads_mask_of()
     all_windows = []
     all_joined = []
@@ -609,6 +633,9 @@
             return four_windows(ref[:, columns, :].astype(F32))
 
         wait_all(fetches[index][:1])
+        if index == 0:
+            for copy in fetches[0][3:] + fetches[1]:
+                copy.start()
         grad_two = windows_of(grad_output_ref, columns) + norm_back(
             windows_of(section_two_ref, out_columns),
             gain_grid_ref[...],
@@ -665,8 +692,9 @@
                     for row in range(ROWS):
                         ends[side, block, row : row + 1, :] = inner[row, column : column + 1]
     if before_ref is None:
-        left_ref[...] = ends[0].astype(BF16)
-        right_ref[...] = ends[1].astype(BF16)
+        near, after = trade(ends[1], ends[0])
+        near_ref[...] = near.astype(BF16)
+        next_ref[...] = after.astype(BF16)
     wait_all(stores)
 
 
@@ -744,8 +772,8 @@
     slope_pre_in,
     outer_ref,
     middle_ref,
-    left_ref,
-    right_ref,
+    near_ref,
+    next_ref,
     dw_ref,
     preact_ref,
     taps_ref,
@@ -772,8 +800,7 @@
 
     @pl.loop(0, BLOCKS)
     def _(block):
-        left = left_ref[block].astype(F32)
-        right = right_ref[block].astype(F32)
+        right, left = trade(near_ref[block], next_ref[block])
         for row in range(ROWS):
             fill_row(pad, block, row, row, outer_ref, middle_ref, left, right)
         wait_all(fetches(block))
@@ -796,10 +823,10 @@
     slope_pre_in,
     outer_ref,
     middle_ref,
-    top_ref,
-    bottom_ref,
-    left_ref,
-    right_ref,
+    pair_ref,
+    other_ref,
+    near_ref,
+    next_ref,
     scale_ref,
     shift_ref,
     dw_ref,
@@ -832,12 +859,12 @@
             x_ref[row], scale_ref, shift_ref
         )
     wait_all(fetches)
+    even = even_row()
 
     @pl.loop(0, BLOCKS)
     def _(block):
-        left = left_ref[block].astype(F32)
-        right = right_ref[block].astype(F32)
-        for source, place in ((top_ref, 0), (bottom_ref, 5)):
+        right, left = trade(near_ref[block], next_ref[block])
+        for source, place in ((pair_ref, 5 * even), (other_ref, 5 - 5 * even)):
             cells = source[block].astype(F32)
             pad[block, place, LEFT : LEFT + COLS, :] = cells[:COLS]
             pad[block, place, LEFT - 1 : LEFT, :] = cells[COLS : COLS + 1]
@@ -929,7 +956,7 @@
 FACTOR = float((64 * 2048) ** (-0.5))
 
 
-def pair_kernel(early_keep_ref, early_got_ref, late_keep_ref, late_got_ref, parts_ref):
+def pair_kernel(early_keep_ref, early_got_ref, late_keep_ref, late_got_ref, _, parts_ref):
     early = early_keep_ref[...].astype(F32) + early_got_ref[...].astype(F32)
     early = early.reshape(CHUNKS, 48, 128)
     late = late_keep_ref[...].astype(F32) + late_got_ref[...].astype(F32)
@@ -946,71 +973,80 @@
         out_ref[index] = total
 
 
-def unpack_kernel(
-    core_ref,
-    mine_ref,
-    other_ref,
-    expand_ref,
-    kernel_ref,
-    project_ref,
-    qkv_block_ref,
-    out_block_ref,
-    qkv_grid_ref,
-    out_grid_ref,
-):
-    core = core_ref[0]
-
-    targets = (
-        [(qkv_block_ref, 0, 128 * k, 256) for k in range(6)]
-        + [(out_block_ref, 0, 128 * k, 256) for k in range(2)]
-        + [(project_ref, 0, 128 * k, 1024) for k in range(2)]
-        + [(qkv_grid_ref, 0, 128 * k, 256) for k in range(6)]
-        + [(out_grid_ref, 0, 128 * k, 256) for k in range(2)]
-    )
-    early = [
-        (target, first + start, column)
-        for target, first, column, count in targets
+def unpack_half(half, parts_ref, targets):
+    expand, kernel, project, qkv_block, out_block, qkv_grid, out_grid = targets
+    blocks = (
+        [(qkv_block, 128 * k, 256) for k in range(6)]
+        + [(out_block, 128 * k, 256) for k in range(2)]
+        + [(project, 128 * k, 1024) for k in range(2)]
+        + [(qkv_grid, 128 * k, 256) for k in range(6)]
+        + [(out_grid, 128 * k, 256) for k in range(2)]
+    )
+    places = [
+        (target, start, column)
+        for target, column, count in blocks
         for start in range(0, count, 16)
     ]
-
-    def fill(low_ref, high_ref):
-        for half, ref in enumerate((low_ref, high_ref)):
-            for index in range(CHUNKS):
-                value = ref[index].astype(F32) * FACTOR
-                for k in range(3):
-                    target, row, column = early[192 * half + 3 * index + k]
-                    target[row : row + 16, column : column + 128] = value[16 * k : 16 * k + 16]
-                start = 1024 * half + 16 * index
-                column = start // 256 * 128
-                expand_ref[start % 256 : start % 256 + 16, column : column + 128] = value[48:64]
-                if half == 0 and index < 9:
-                    for block in range(BLOCKS):
-                        kernel_ref[index : index + 1, 128 * block : 128 * block + 128] = value[
-                            64 + block : 65 + block
-                        ]
-
-    @pl.when(core == 0)
-    def _():
-        fill(mine_ref, other_ref)
-
-    @pl.when(core == 1)
-    def _():
-        fill(other_ref, mine_ref)
-
-
-def beside_rows(first, last):
+    for index in range(CHUNKS):
+        value = parts_ref[index].astype(F32) * FACTOR
+        for k in range(3):
+            target, row, column = places[192 * half + 3 * index + k]
+            target[row : row + 16, column : column + 128] = value[16 * k : 16 * k + 16]
+        start = 1024 * half + 16 * index
+        column = start // 256 * 128
+        expand[start % 256 : start % 256 + 16, column : column + 128] = value[48:64]
+        if half == 0 and index < 9:
+            for block in range(BLOCKS):
+                kernel[index : index + 1, 128 * block : 128 * block + 128] = value[
+                    64 + block : 65 + block
+                ]
+
+
+def half_pieces(half, arrays):
+    expand, kernel, project, qkv_block, out_block, qkv_grid, out_grid = arrays
+    lanes = pl.ds(128 * half, 128)
+    wide = pl.ds(512 * half, 512)
+    pieces = [project.at[:, lanes], expand.at[:, wide]]
+    return pieces + ([qkv_block, out_block, kernel] if half == 0 else [qkv_grid, out_grid])
+
+
+def mine_kernel(core_ref, mine_ref, *targets):
+    for half in range(2):
+
+        @pl.when(core_ref[0] == half)
+        def _():
+            unpack_half(half, mine_ref, targets)
+
+
+def other_kernel(core_ref, other_ref, *refs):
+    done, outs, targets, sems = refs[:7], refs[7:14], refs[14:21], refs[21]
+    for half in range(2):
+
+        @pl.when(core_ref[0] == half)
+        def _():
+            copies = copy_all(zip(half_pieces(half, done), half_pieces(half, outs)), sems)
+            unpack_half(1 - half, other_ref, targets)
+            copies += copy_all(
+                zip(half_pieces(1 - half, targets), half_pieces(1 - half, outs)), sems, first=5
+            )
+            wait_all(copies)
+
+
+def beside_rows(pair, other):
     count = lax.axis_size("row")
-    down = [(i, i + 1) for i in range(count - 1)]
-    up = [(i + 1, i) for i in range(count - 1)]
-    return lax.ppermute(last, "row", down), lax.ppermute(first, "row", up)
-
-
-def beside_columns(first, last):
+    swaps = []
+    for first in range(2):
+        pairs = [(i, i + 1) for i in range(first, count - 1, 2)]
+        swaps.append(pairs + [(j, i) for i, j in pairs])
+    return lax.ppermute(pair, "row", swaps[0]), lax.ppermute(other, "row", swaps[1])
+
+
+def beside_columns(near, after):
     axes = ("hi", "core")
     count = lax.axis_size("hi") * lax.axis_size("core")
-    right = [(i, i + 1) for i in range(count - 1)]
-    left = [(i + 1, i) for i in range(count - 1)]
-    return lax.ppermute(last, axes, right), lax.ppermute(first, axes, left)
+    pairs = [(i, i + 1) for i in range(1, count - 1, 2)]
+    swap = pairs + [(j, i) for i, j in pairs]
+    return sibling(near), lax.ppermute(after, axes, swap)
 
 
 def across(values):
@@ -1196,7 +1232,10 @@
         grid_kernel,
         [got, w_qkv_grid, w_out_grid, cube_grid],
         [tokens, shape((2048, 128), F32)],
-        [tokens_vmem, pltpu.VMEM((TOKENS, 3 * D), BF16)],
+        [
+            tokens_vmem,
+            pltpu.VMEM((TOKENS, 3 * D), BF16),
+        ],
         keep=(0, 1),
         limit=8,
     )
@@ -1342,29 +1381,42 @@
 
     (paired,) = call(
         pair_kernel,
-        [early_keep, early_got, late_keep, sibling(late_send)],
+        [early_keep, early_got, late_keep, sibling(late_send), grad_input],
         [parts],
         [],
+        far=(4,),
         keep=(0,),
         limit=4,
     )
     (summed,) = call(sum_kernel, [across(paired)], [parts], [], keep=(0,), limit=4)
     mine = across(summed)
-    totals = call(
-        unpack_kernel,
-        [core_flag, mine, sibling(mine)],
-        [
-            shape((D, E), F32),
-            shape((9, E), F32),
-            shape((E, D), F32),
-            shape((D, 3 * D), F32),
-            shape((D, D), F32),
-            shape((D, 3 * D), F32),
-            shape((D, D), F32),
-        ],
+    sums = [
+        shape((D, E), F32),
+        shape((9, E), F32),
+        shape((E, D), F32),
+        shape((D, 3 * D), F32),
+        shape((D, D), F32),
+        shape((D, 3 * D), F32),
+        shape((D, D), F32),
+    ]
+    done = call(
+        mine_kernel,
+        [core_flag, mine],
+        sums,
         [],
         smem=(0,),
-        limit=16,
+        keep=range(7),
+        limit=4,
+        flops=2 * 10**9,
+    )
+    totals = call(
+        other_kernel,
+        [core_flag, sibling(mine), *done],
+        sums,
+        [pltpu.VMEM(o.shape, F32) for o in sums] + [dma((10,))],
+        smem=(0,),
+        far_out=range(7),
+        limit=10,
     )
     return (grad_input, *totals)
 

time: 186 us -> 175 us (0.941)
  starting transfers between devices: 36.4 us -> 25.8 us
  Pallas kernels: 57.2 us -> 53.6 us
  blocking collectives: 76.5 us -> 78.6 us
    ppermute x8 -> x6, starting transfers between devices: 26 us -> 11.1 us  [the longest x2 8.12 us: beside_columns(): return (sibling(near), lax.ppermute(after, axes, swap))]
    ppermute x3 -> x5, starting transfers between devices: 4.27 us -> 8.73 us  [sibling(): return lax.ppermute(values, 'core', [(0, 1), (1, 0)])]
    pallas_call x17 -> x18, Pallas kernels: 57.2 us -> 53.6 us  [call(): pl.pallas_call(kernel, out_shape=[pltpu.VMEM(o.shape, o.dtype) if k in ke...]
    all_to_all x3, blocking collectives: 76.5 us -> 78.6 us  [across(): lax.all_to_all(values, ('row', 'hi'), split_axis=0, concat_axis=0, tiled=...]
  transfers between devices with their start and end apart: 12 -> 12, of which waited for: 3 -> 2; matrix products, arithmetic and copies ran while one was open for 0% -> 0% of each run, Pallas kernels for 17% -> 18%
where the time goes in v4:
time: 175 us; the launch traced here: 174 us
  blocking collectives  78.6 us (45%)
  Pallas kernels  53.6 us (31%)
  starting transfers between devices  25.8 us (15%)
  waiting for transfers between devices  13.5 us (8%)
  local copies, waits for them, and re-layouts  1.76 us (1%)
    all_to_all x3, blocking collectives, across(): lax.all_to_all(values, ('row', 'hi'), split_axis=0, concat_axis=0, tiled=...  78.6 us
    pallas_call x18, Pallas kernels, call(): pl.pallas_call(kernel, out_shape=[pltpu.VMEM(o.shape, o.dtype) if k in ke...  53.6 us
    all_to_all x1, waiting for transfers between devices, across(): lax.all_to_all(values, ('row', 'hi'), split_axis=0, concat_axis=0, tiled=...  11.1 us
    ppermute x5, starting transfers between devices, sibling(): return lax.ppermute(values, 'core', [(0, 1), (1, 0)])  8.73 us
    ppermute x2, starting transfers between devices, beside_columns(): return (sibling(near), lax.ppermute(after, axes, swap))  8.12 us
    all_to_all x1, starting transfers between devices, across(): lax.all_to_all(values, ('row', 'hi'), split_axis=0, concat_axis=0, tiled=...  6.02 us
  transfers between devices with their start and end apart: 12, of which 2 were waited for; matrix products, arithmetic and copies ran while one was open for 0% of the time, Pallas kernels for 18%

profile of v4, /device:TPU:1, one launch (start us, length us, event | category | flops | bytes accessed | tf_op | source)
XLA Modules:
  0.0 174.4 jit_solution(17261482207565484968)
XLA Ops:
  0.7 1.1 shard_map.206
  1.8 1.5 collective-permute-start
  3.3 5.5 %collective-permute-start.1 = (bf16[8,256]{1,0:T(8,128)(2,1)S(1)}, bf16[8,256]{1,0:T(8,128)(2,1)S(1)}, u32[]{:S(2)}, u32[]{:S(2)}) collective-permute-start(bf16[8,256]{1,0:T(8,128)(2,1)S(1)} %get-tuple-element.77), channel_id=1, source_target_pairs={{1,2},{3,4},{5,6},{7,8},{9,10},{11,12},{13,14},{2,1},{4,3},{6,5},{... | collective-permute-start | bytes 12296 | tf_op jit(solution)/shard_map/ppermute | solution.py:1049
  8.8 0.0 copy-start.4
  8.8 0.0 copy-start.5
  8.8 5.5 %shard_map.207 = (bf16[8,1024,128]{2,1,0:T(8,128)(2,1)}, bf16[8,1024,128]{2,1,0:T(8,128)(2,1)}, bf16[8,1024,128]{2,1,0:T(8,128)(2,1)S(1)}, bf16[256,1024]{1,0:T(...) custom-call(bf16[8,128,256]{2,1,0:T(8,128)(2,1)S(1)} %get-tuple-elem, ...), custom_call_target="tpu_custom_call" | custom-call | flops 4000000000 | bytes 40000000 | tf_op jit(solution)/shard_map/pallas_call | solution.py:936
  14.3 0.6 shard_map.210
  14.9 0.0 collective-permute-done.near_ref
  14.9 0.0 collective-permute-done.1.next_ref
  15.0 1.4 collective-permute-start.2
  16.4 0.7 collective-permute-start.3
  17.0 0.0 copy-start
  17.0 0.0 copy-start.1
  17.0 4.8 %shard_map.209 = (bf16[8,768,128]{2,1,0:T(8,128)(2,1)}, bf16[8,768,128]{2,1,0:T(8,128)(2,1)S(1)}, bf16[8,768,128]{2,1,0:T(8,128)(2,1)}, f32[8,16,128]{2,1,0:T(8,128)S(1)}) custom-call(bf16[8,1024,128]{2,1,0:T(8,128)(2,1)S(1)} %get-tuple-element.80.lifted_ref, bf16[8,256]{1,0:T(8,128)(2,1)S(1)} %collective-permute-done.near_ref, ...), custom_call_target="tpu_custom_call" | custom-call | flops 4000000000 | bytes 40000000 | tf_op jit(solution)/shard_map/pallas_call | solution.py:936
  21.8 0.0 collective-permute-done.2.pair_ref
  21.9 7.4 %shard_map.211 = (bf16[8,256,128]{2,1,0:T(8,128)(2,1)}, bf16[8,256,128]{2,1,0:T(8,128)(2,1)}, bf16[8,128,256]{2,1,0:T(8,128)(2,1)}, bf16[8,128,256]{2,1,0:T(8,12...) custom-call(bf16[8,128,256]{2,1,0:T(8,128)(2,1)S(1)} %get-tuple-elem, ...), custom_call_target="tpu_custom_call" | custom-call | flops 1000000000 | bytes 10000000 | tf_op jit(solution)/shard_map/pallas_call | solution.py:936
  29.3 27.0 %all_to_all.20 = bf16[64,32,256]{2,1,0:T(8,128)(2,1)S(1)} all-to-all(bf16[64,32,256]{2,1,0:T(8,128)(2,1)S(1)} %get-tuple-element.90), channel_id=1, replica_groups=mesh['row'=8,'hi'=8,'core'=2] {'row','hi'}, dimensions={0} | all-to-all | bytes 2097152 | tf_op jit(solution)/shard_map/all_to_all | solution.py:1053
  56.3 0.6 copy.23
  56.9 5.6 %shard_map.212 = (bf16[1024,256]{1,0:T(8,128)(2,1)S(1)}, f32[2048,128]{1,0:T(8,128)S(1)}) custom-call(bf16[2,1024,256]{2,1,0:T(8,128)(2,1)S(1)} %bitcast.14, bf16[256,768]{1,0:T(8,128)(2,1)S(1)} %get-tuple-element.91.w_qkv_ref, bf16[256,256]{1,0:T(8,128)(2,1)S(1)} %get-tuple-element.92.w_out_ref, f32[2,64,256]{2,1,0:T(8,128)S(1)} %get-tuple-element.93.bias), custom_call_target="tpu_custom_call" | custom-call | flops 1000000000 | bytes 10000000 | tf_op jit(solution)/shard_map/pallas_call | solution.py:936
  62.5 0.0 copy-start.6
  62.5 1.1 copy.26
  63.7 6.0 %all-to-all-start.1 = ((bf16[64,16,256]{2,1,0:T(8,128)(2,1)}), bf16[64,16,256]{2,1,0:T(8,128)(2,1)S(1)}, u32[]{:S(2)}, u32[]{:S(2)}) async-start(bf16[64,16,256]{2,1,0:T(8,128)(2,1)} %bitcast.34), calls=%async_computation.1 | async-start | bytes 1048576 | tf_op jit(solution)/shard_map/all_to_all | solution.py:1053
  69.7 11.1 %all-to-all-done.1 = bf16[64,16,256]{2,1,0:T(8,128)(2,1)S(1)} async-done(((bf16[64,16,256]{2,1,0:T(8,128)(2,1)}), bf16[64,16,256]{2,1,0:T(8,128)(2,1)S(1)}, u32[]{:S(2)}, u32[]{:S(2)}) %all-to-all-start.1) | async-done | bytes 524320 | tf_op jit(solution)/shard_map/all_to_all | solution.py:1053
  80.8 5.8 %shard_map.213 = (bf16[8,64,256]{2,1,0:T(8,128)(2,1)}, bf16[8,8,64,128]{3,2,1,0:T(8,128)(2,1)S(1)}, f32[2048,128]{1,0:T(8,128)S(1)}, bf16[8,8,128]{2,1,0:T(8,128)(2,1)S(1)}, bf16[8,8,128]{2,1,0:T(8,128)(2,1)S(1)}) custom-call(bf16[8,128,256]{2,1,0:T(8,128)(2,1)S(1)} %bitcast.15, bf16[8,128,256]{2,1,0:T(8,128)(2,1)S(1)} %get-tuple-element.89.grad_output_ref, ...), custom_call_target="tpu_custom_call" | custom-call | flops 4000000000 | bytes 40000000 | tf_op jit(solution)/shard_map/pallas_call | solution.py:936
  86.7 3.0 %collective-permute-start.4 = (bf16[8,8,128]{2,1,0:T(8,128)(2,1)S(1)}, bf16[8,8,128]{2,1,0:T(8,128)(2,1)S(1)}, u32[]{:S(2)}, u32[]{:S(2)}) collective-permute-start(bf16[8,8,128]{2,1,0:T(8,128)(2,1)S(1)} %get-tuple-element.106), channel_id=1, source_target_pairs={{0,1},{1,0},{2,3},{3,2},{4,5},{5,4},{6,7},{7,6},{8,9},{9,8},{10,11... | collective-permute-start | bytes 49160 | tf_op jit(solution)/shard_map/ppermute | solution.py:1057
  89.7 2.6 %collective-permute-start.5 = (bf16[8,8,128]{2,1,0:T(8,128)(2,1)S(1)}, bf16[8,8,128]{2,1,0:T(8,128)(2,1)S(1)}, u32[]{:S(2)}, u32[]{:S(2)}) collective-permute-start(bf16[8,8,128]{2,1,0:T(8,128)(2,1)S(1)} %get-tuple-element.107), channel_id=1, source_target_pairs={{1,2},{3,4},{5,6},{7,8},{9,10},{11,12},{13,14},{2,1},{4,3},{6,5},{... | collective-permute-start | bytes 49160 | tf_op jit(solution)/shard_map/ppermute | solution.py:1049
  92.3 6.1 %shard_map.214 = (bf16[8,64,256]{2,1,0:T(8,128)(2,1)}, bf16[8,8,64,128]{3,2,1,0:T(8,128)(2,1)S(1)}, f32[2048,128]{1,0:T(8,128)}) custom-call(bf16[8,128,256]{2,1,0:T(8,128)(2,1)S(1)} %bitcast.16, bf16[8,128,256]{2,1,0:T(8,128)(2,1)S(1)} %get-tuple-element.89.grad_output_ref, bf16[8,128,256]{2,1,0:T(8,128)(2,1)} %get-tuple-element.95.section_two_in, ...), custom_call_target="tpu_custom_call" | custom-call | flops 4000000000 | bytes 40000000 | tf_op jit(solution)/shard_map/pallas_call | solution.py:936
  98.4 0.0 collective-permute-done.4.near_ref
  98.5 0.1 shard_map.216
  98.6 0.3 collective-permute-start.6
  98.9 0.7 collective-permute-start.7
  99.6 2.7 %shard_map.217 = (bf16[8,128,256]{2,1,0:T(8,128)(2,1)S(1)}, bf16[3072,128]{1,0:T(8,128)(2,1)S(1)}, bf16[3072,128]{1,0:T(8,128)(2,1)S(1)}) custom-call(s32[1]{0:T(128)} %bitcast.11.core_ref, bf16[8,64,256]{2,1,0:T(8,128)(2,1)} %get-tuple-element.112.outer_in, bf16[8,64,256]{2,1,0:T(8,128)(2,1)} %get-tuple-element.113.middle_in, ...), custom_call_target="tpu_custom_call" | custom-call | flops 3000000000 | bytes 30000000 | tf_op jit(solution)/shard_map/pallas_call | solution.py:936
  102.3 0.1 collective-permute-start.8
  102.4 5.7 %shard_map.215 = (bf16[8,768,128]{2,1,0:T(8,128)(2,1)S(1)}, f32[9,8,128]{2,1,0:T(8,128)S(1)}) custom-call(bf16[8,1024,128]{2,1,0:T(8,128)(2,1)} %get-tuple-element.74.lifted_in, bf16[8,1024,128]{2,1,0:T(8,128)(2,1)} %get-tuple-element.75.slope_pre_in, bf16[8,8,64,128]{3,2,1,0:T(8,128)(2,1)S(1)} %get-tuple-element.103.outer_ref, ...), custom_call_target="tpu_custom_call" | custom-call | flops 4000000000 | bytes 40000000 | tf_op jit(solution)/shard_map/pallas_call | solution.py:936
  108.1 0.0 collective-permute-done.6.pair_ref
  108.1 3.7 %shard_map.218 = (bf16[8,256,128]{2,1,0:T(8,128)(2,1)S(1)}, bf16[64,24,128]{2,1,0:T(8,128)(2,1)S(1)}, bf16[64,24,128]{2,1,0:T(8,128)(2,1)S(1)}) custom-call(s32[1]{0:T(128)} %bitcast.11.core_ref, bf16[8,128,256]{2,1,0:T(8,128)(2,1)S(1)} %get-tuple-element.73.x_ref, bf16[8,1024,128]{2,1,0:T(8,128)(2,1)} %get-tuple-element.74.lifted_in, ...), custom_call_target="tpu_custom_call" | custom-call | flops 4000000000 | bytes 40000000 | tf_op jit(solution)/shard_map/pallas_call | solution.py:936
  111.9 0.6 collective-permute-start.9
  112.4 1.5 shard_map.219._
  114.0 0.0 collective-permute-done.9.late_got_ref
  114.0 0.0 collective-permute-done.8.early_got_ref
  114.0 0.3 shard_map.220
  114.2 29.1 %all_to_all.21.got_ref = bf16[64,72,128]{2,1,0:T(8,128)(2,1)S(1)} all-to-all(bf16[64,72,128]{2,1,0:T(8,128)(2,1)S(1)} %shard_map.220), channel_id=1, replica_groups=mesh['row'=8,'hi'=8,'core'=2] {'row','hi'}, dimensions={0} | all-to-all | bytes 2359296 | tf_op jit(solution)/shard_map/all_to_all | solution.py:1053
  143.3 0.3 shard_map.221
  143.6 22.5 %all_to_all.22.mine_ref = bf16[64,72,128]{2,1,0:T(8,128)(2,1)S(1)} all-to-all(bf16[64,72,128]{2,1,0:T(8,128)(2,1)S(1)} %shard_map.221), channel_id=1, replica_groups=mesh['row'=8,'hi'=8,'core'=2] {'row','hi'}, dimensions={0} | all-to-all | bytes 2359296 | tf_op jit(solution)/shard_map/all_to_all | solution.py:1053
  166.1 3.5 %collective-permute-start.10 = (bf16[64,72,128]{2,1,0:T(8,128)(2,1)S(1)}, bf16[64,72,128]{2,1,0:T(8,128)(2,1)S(1)}, u32[]{:S(2)}, u32[]{:S(2)}) collective-permute-start(bf16[64,72,128]{2,1,0:T(8,128)(2,1)S(1)} %all_to_all.22.mine_ref), channel_id=1, source_target_pairs={{0,1},{1,0},{2,3},{3,2},{4,5},{5,4},{6,7},{7,6},{8,9},{9,8},{10,11... | collective-permute-start | bytes 3538952 | tf_op jit(solution)/shard_map/ppermute | solution.py:1057
  169.6 0.2 shard_map.222
  169.8 2.3 %collective-permute-done.10.other_ref = bf16[64,72,128]{2,1,0:T(8,128)(2,1)S(1)} collective-permute-done((bf16[64,72,128]{2,1,0:T(8,128)(2,1)S(1)}, bf16[64,72,128]{2,1,0:T(8,128)(2,1)S(1)}, u32[]{:S(2)}, u32[]{:S(2)}) %collective-permute-start.10) | collective-permute-done | bytes 1179680 | tf_op jit(solution)/shard_map/ppermute | solution.py:1057
  172.1 2.1 %shard_map.223 = (f32[256,1024]{1,0:T(8,128)}, f32[9,1024]{1,0:T(8,128)}, f32[1024,256]{1,0:T(8,128)}, f32[256,768]{1,0:T(8,128)}, f32[256,256]{1,0:T(8,128)}, /*index=5*/f32[256,768]{1,0:T(8,128)}, f32[256,256]{1,0:T(8,128)}) custom-call(s32[1]{0:T(128)} %bitcast.11.core_ref, bf16[64,72,128]{2,1,0:T(8,128)(2,1)S(1)} %collective-permute-done.10.other_ref, ...), custom_call_target="tpu_custom_call" | custom-call | flops 1000000000 | bytes 10000000 | tf_op jit(solution)/shard_map/pallas_call | solution.py:936
  (13 shorter events, 0.1 us)
Async XLA Ops:
  0.6 8.1 %copy-start.3 = (f32[256]{0:T(256)S(1)}, f32[256]{0:T(256)}, u32[]{:S(2)}) copy-start(f32[256]{0:T(256)} %param.17) | copy-start | bytes 3076
  0.6 8.1 %copy-start.2 = (f32[256]{0:T(256)S(1)}, f32[256]{0:T(256)}, u32[]{:S(2)}) copy-start(f32[256]{0:T(256)} %param.18) | copy-start | bytes 3076
  1.8 13.2 %collective-permute-start = (bf16[8,256]{1,0:T(8,128)(2,1)S(1)}, bf16[8,256]{1,0:T(8,128)(2,1)S(1)}, u32[]{:S(2)}, u32[]{:S(2)}) collective-permute-start(bf16[8,256]{1,0:T(8,128)(2,1)S(1)} %get-tuple-element.76), channel_id=1, source_target_pairs={{0,1},{1,0},{2,3},{3,2},{4,5},{5,4},{6,7},{7,6},{8,9},{9,8},{10,11... | collective-permute-start | bytes 12296 | tf_op jit(solution)/shard_map/ppermute | solution.py:1057
  3.3 11.7 %collective-permute-start.1 = (bf16[8,256]{1,0:T(8,128)(2,1)S(1)}, bf16[8,256]{1,0:T(8,128)(2,1)S(1)}, u32[]{:S(2)}, u32[]{:S(2)}) collective-permute-start(bf16[8,256]{1,0:T(8,128)(2,1)S(1)} %get-tuple-element.77), channel_id=1, source_target_pairs={{1,2},{3,4},{5,6},{7,8},{9,10},{11,12},{13,14},{2,1},{4,3},{6,5},{... | collective-permute-start | bytes 12296 | tf_op jit(solution)/shard_map/ppermute | solution.py:1049
  8.8 5.5 %copy-start.4 = (f32[8,225]{1,0:T(8,128)S(1)}, f32[8,225]{1,0:T(8,128)}, u32[]{:S(2)}) copy-start(f32[8,225]{1,0:T(8,128)} %block_ref.1) | copy-start | bytes 21604
  8.8 5.5 %copy-start.5 = (f32[8,225]{1,0:T(8,128)S(1)}, f32[8,225]{1,0:T(8,128)}, u32[]{:S(2)}) copy-start(f32[8,225]{1,0:T(8,128)} %grid_ref.1) | copy-start | bytes 21604
  15.0 6.9 %collective-permute-start.2 = (bf16[144,256]{1,0:T(8,128)(2,1)S(1)}, bf16[144,256]{1,0:T(8,128)(2,1)S(1)}, u32[]{:S(2)}, u32[]{:S(2)}) collective-permute-start(bf16[144,256]{1,0:T(8,128)(2,1)S(1)} %get-tuple-element.78), channel_id=1, source_target_pairs={{0,16},{32,48},{64,80},{96,112},{16,0},{48,32},{80,64},{112,96},{1... | collective-permute-start | bytes 221192 | tf_op jit(solution)/shard_map/ppermute | solution.py:1041
  16.4 5.5 %collective-permute-start.3 = (bf16[144,256]{1,0:T(8,128)(2,1)S(1)}, bf16[144,256]{1,0:T(8,128)(2,1)S(1)}, u32[]{:S(2)}, u32[]{:S(2)}) collective-permute-start(bf16[144,256]{1,0:T(8,128)(2,1)S(1)} %get-tuple-element.79), channel_id=1, source_target_pairs={{16,32},{48,64},{80,96},{32,16},{64,48},{96,80},{17,33},{49,65},{8... | collective-permute-start | bytes 221192 | tf_op jit(solution)/shard_map/ppermute | solution.py:1041
  17.0 4.8 %copy-start = (f32[256]{0:T(256)S(1)}, f32[256]{0:T(256)}, u32[]{:S(2)}) copy-start(f32[256]{0:T(256)} %param.22) | copy-start | bytes 3076
  17.0 4.8 %copy-start.1 = (f32[256]{0:T(256)S(1)}, f32[256]{0:T(256)}, u32[]{:S(2)}) copy-start(f32[256]{0:T(256)} %param.26) | copy-start | bytes 3076
  62.5 1.1 copy-start.6
  63.7 17.2 %all-to-all-start.1 = ((bf16[64,16,256]{2,1,0:T(8,128)(2,1)}), bf16[64,16,256]{2,1,0:T(8,128)(2,1)S(1)}, u32[]{:S(2)}, u32[]{:S(2)}) async-start(bf16[64,16,256]{2,1,0:T(8,128)(2,1)} %bitcast.34), calls=%async_computation.1 | async-start | bytes 1048576 | tf_op jit(solution)/shard_map/all_to_all | solution.py:1053
  86.7 11.8 %collective-permute-start.4 = (bf16[8,8,128]{2,1,0:T(8,128)(2,1)S(1)}, bf16[8,8,128]{2,1,0:T(8,128)(2,1)S(1)}, u32[]{:S(2)}, u32[]{:S(2)}) collective-permute-start(bf16[8,8,128]{2,1,0:T(8,128)(2,1)S(1)} %get-tuple-element.106), channel_id=1, source_target_pairs={{0,1},{1,0},{2,3},{3,2},{4,5},{5,4},{6,7},{7,6},{8,9},{9,8},{10,11... | collective-permute-start | bytes 49160 | tf_op jit(solution)/shard_map/ppermute | solution.py:1057
  89.7 8.8 %collective-permute-start.5 = (bf16[8,8,128]{2,1,0:T(8,128)(2,1)S(1)}, bf16[8,8,128]{2,1,0:T(8,128)(2,1)S(1)}, u32[]{:S(2)}, u32[]{:S(2)}) collective-permute-start(bf16[8,8,128]{2,1,0:T(8,128)(2,1)S(1)} %get-tuple-element.107), channel_id=1, source_target_pairs={{1,2},{3,4},{5,6},{7,8},{9,10},{11,12},{13,14},{2,1},{4,3},{6,5},{... | collective-permute-start | bytes 49160 | tf_op jit(solution)/shard_map/ppermute | solution.py:1049
  98.6 9.5 %collective-permute-start.6 = (bf16[8,144,128]{2,1,0:T(8,128)(2,1)S(1)}, bf16[8,144,128]{2,1,0:T(8,128)(2,1)S(1)}, u32[]{:S(2)}, u32[]{:S(2)}) collective-permute-start(bf16[8,144,128]{2,1,0:T(8,128)(2,1)S(1)} %get-tuple-element.109._), channel_id=1, source_target_pairs={{0,16},{32,48},{64,80},{96,112},{16,0},{48,32},{80,64},{112,96},{1... | collective-permute-start | bytes 884744 | tf_op jit(solution)/shard_map/ppermute | solution.py:1041
  98.9 9.3 %collective-permute-start.7 = (bf16[8,144,128]{2,1,0:T(8,128)(2,1)S(1)}, bf16[8,144,128]{2,1,0:T(8,128)(2,1)S(1)}, u32[]{:S(2)}, u32[]{:S(2)}) collective-permute-start(bf16[8,144,128]{2,1,0:T(8,128)(2,1)S(1)} %get-tuple-element.110), channel_id=1, source_target_pairs={{16,32},{48,64},{80,96},{32,16},{64,48},{96,80},{17,33},{49,65},{8... | collective-permute-start | bytes 884744 | tf_op jit(solution)/shard_map/ppermute | solution.py:1041
  102.3 11.7 %collective-permute-start.8 = (bf16[3072,128]{1,0:T(8,128)(2,1)S(1)}, bf16[3072,128]{1,0:T(8,128)(2,1)S(1)}, u32[]{:S(2)}, u32[]{:S(2)}) collective-permute-start(bf16[3072,128]{1,0:T(8,128)(2,1)S(1)} %get-tuple-element.121), channel_id=1, source_target_pairs={{0,1},{1,0},{2,3},{3,2},{4,5},{5,4},{6,7},{7,6},{8,9},{9,8},{10,11... | collective-permute-start | bytes 2359304 | tf_op jit(solution)/shard_map/ppermute | solution.py:1057
  111.9 2.1 %collective-permute-start.9 = (bf16[64,24,128]{2,1,0:T(8,128)(2,1)S(1)}, bf16[64,24,128]{2,1,0:T(8,128)(2,1)S(1)}, u32[]{:S(2)}, u32[]{:S(2)}) collective-permute-start(bf16[64,24,128]{2,1,0:T(8,128)(2,1)S(1)} %get-tuple-element.123), channel_id=1, source_target_pairs={{0,1},{1,0},{2,3},{3,2},{4,5},{5,4},{6,7},{7,6},{8,9},{9,8},{10,11... | collective-permute-start | bytes 1179656 | tf_op jit(solution)/shard_map/ppermute | solution.py:1057
  166.1 6.0 %collective-permute-start.10 = (bf16[64,72,128]{2,1,0:T(8,128)(2,1)S(1)}, bf16[64,72,128]{2,1,0:T(8,128)(2,1)S(1)}, u32[]{:S(2)}, u32[]{:S(2)}) collective-permute-start(bf16[64,72,128]{2,1,0:T(8,128)(2,1)S(1)} %all_to_all.22.mine_ref), channel_id=1, source_target_pairs={{0,1},{1,0},{2,3},{3,2},{4,5},{5,4},{6,7},{7,6},{8,9},{9,8},{10,11... | collective-permute-start | bytes 3538952 | tf_op jit(solution)/shard_map/ppermute | solution.py:1057

commit v5 on v4

--- a/solution.py
+++ b/solution.py
@@ -67,16 +67,16 @@
     )
 
 
-def load_kernel(x_in, x_ref, near_ref, next_ref, sem, ends):
-    copy = pltpu.make_async_copy(x_in, x_ref, sem)
-    copy.start()
-    copy.wait()
+def load_kernel(x_in, w_expand_in, x_ref, w_expand_ref, near_ref, next_ref, sems, ends):
+    copies = copy_all(((x_in, x_ref), (w_expand_in, w_expand_ref)), sems)
+    copies[0].wait()
     for row in range(ROWS):
         ends[0, row : row + 1, :] = x_ref[row, 0:16, :].astype(F32)[0:1]
         ends[1, row : row + 1, :] = x_ref[row, COLS - 16 : COLS, :].astype(F32)[15:16]
     near, after = trade(ends[1], ends[0])
     near_ref[...] = near.astype(BF16)
     next_ref[...] = after.astype(BF16)
+    copies[1].wait()
 
 
 def with_corners(cells, left, right):
@@ -261,16 +261,16 @@
     x_ref,
     scale_ref,
     shift_ref,
+    w_expand_ref,
     *refs,
 ):
     count = (len(refs) - 6) // 2
     sources, (lifted_out, slope_pre_out, lifted_ref) = refs[:count], refs[count : count + 3]
     targets, (slope_pre_ref, sems, load_sems) = refs[count + 3 : -3], refs[-3:]
-    loads = copy_all([(sources[0], targets[0])], load_sems)
-    w_expand_ref = targets[0]
+    loads = copy_all(list(zip(sources, targets)), load_sems)
 
     def stores(row):
-        here = pl.ds(pl.multiple_of(row * COLS, COLS), COLS)
+        here = pl.ds(row * COLS, COLS)
         return [
             pltpu.make_async_copy(source.at[:, here, :], target.at[:, here, :], sems.at[row, k])
             for k, (source, target) in enumerate(
@@ -278,12 +278,8 @@
             )
         ]
 
-    wait_all(loads)
-    loads = copy_all(list(zip(sources[1:], targets[1:])), load_sems, first=1)
-
-    @pl.loop(0, ROWS)
-    def _(row):
-        here = pl.ds(pl.multiple_of(row * COLS, COLS), COLS)
+    for row in range(ROWS):
+        here = pl.ds(row * COLS, COLS)
         shifted = shift_scale(x_ref[row], scale_ref, shift_ref)
         for pair in range(4):
             value, slope = gelu_pair(
@@ -530,10 +526,17 @@
     total_ref,
     mixture_ref,
     grad_joined_ref,
+    groups_ref,
 ):
     heads_mask = heads_mask_of()
-    normed_ref = got_ref.at[0]
-    grad_ref = got_ref.at[1]
+    for index in range(2):
+        for part in range(4):
+            cells = got_ref[:, 16 * index + 4 * part : 16 * index + 4 * part + 4, :].astype(F32)
+            groups_ref[index, 256 * part : 256 * part + 256, :] = (
+                cells.transpose(1, 0, 2).reshape(256, D).astype(BF16)
+            )
+    normed_ref = groups_ref.at[0]
+    grad_ref = groups_ref.at[1]
 
     for part in range(4):
         here = slice(256 * part, 256 * part + 256)
@@ -548,14 +551,41 @@
     attention_totals(total_ref, normed_ref, grad_joined_ref, mixture_ref, grad_ref)
 
 
+def quarter_fetches(far, near, parts, sems, first):
+    section_two, joined, probs, section_one, slope_mid, slope_edge, normed_block, mixture = far
+    two_ref, joined_ref, probs_ref, one_ref, slope_ref, normed_ref, mixture_ref = near
+    fetches = []
+    for index, part in enumerate(parts):
+        here, columns = pl.ds(256 * part, 256), pl.ds(32 * part, 32)
+        goal, to = pl.ds(256 * index, 256), pl.ds(32 * index, 32)
+        pairs = (
+            (section_two.at[:, columns, :], two_ref.at[:, to, :]),
+            (joined.at[here, :], joined_ref.at[goal, :]),
+            (probs.at[pl.ds(8 * part, 8)], probs_ref.at[pl.ds(8 * index, 8)]),
+            (section_one.at[:, columns, :], one_ref.at[:, to, :]),
+            (slope_mid.at[:, :, columns, :], slope_ref.at[:, pl.ds(1, 6), to, :]),
+            (slope_edge.at[:, pl.ds(0, 1), columns, :], slope_ref.at[:, pl.ds(0, 1), to, :]),
+            (slope_edge.at[:, pl.ds(1, 1), columns, :], slope_ref.at[:, pl.ds(7, 1), to, :]),
+            (normed_block.at[here, :], normed_ref.at[goal, :]),
+            (mixture.at[here, :], mixture_ref.at[goal, :]),
+        )
+        fetches.append(
+            [
+                pltpu.make_async_copy(source, target, sems.at[first + 9 * index + k])
+                for k, (source, target) in enumerate(pairs)
+            ]
+        )
+    return fetches
+
+
 def block_kernel(
     parts,
     returned_ref,
     grad_output_ref,
     section_two_in,
-    section_one_in,
     joined_in,
     probs_in,
+    section_one_in,
     slope_mid_in,
     slope_edge_in,
     normed_block_in,
@@ -567,60 +597,40 @@
     w_project_ref,
     *rest,
 ):
+    far = (
+        section_two_in,
+        joined_in,
+        probs_in,
+        section_one_in,
+        slope_mid_in,
+        slope_edge_in,
+        normed_block_in,
+        mixture_in,
+    )
+    stores = []
+    ahead = []
+    if parts[0] == 0:
+        before_ref = None
+        grad_one_out, inner_ref, total_ref, near_ref, next_ref = rest[:5]
+        ahead_refs, (ends, grad_one_ref), near_refs = rest[5:12], rest[12:14], rest[14:21]
+        sems, fetch_sems = rest[21:]
+        fetches = quarter_fetches(far, near_refs, parts, fetch_sems, 0)
+        ahead = quarter_fetches(far, ahead_refs, (1, 2), fetch_sems, 18)
+        for copy in fetches[0][:3]:
+            copy.start()
+    else:
+        before_ref, grad_one_out, inner_ref, total_out, total_ref, grad_one_ref, sems = rest
+        near_refs = far[:7]
+        fetches = [[], []]
     (
         section_two_ref,
-        section_one_ref,
         joined_ref,
         probs_ref,
+        section_one_ref,
         slope_ref,
         normed_block_ref,
         mixture_ref,
-        grad_one_ref,
-        fetch_sems,
-        sems,
-    ) = rest[-10:]
-    if len(rest) == 16:
-        before_ref = None
-        grad_one_out, inner_ref, total_ref, near_ref, next_ref, ends = rest[:-10]
-    else:
-        before_ref, grad_one_out, inner_ref, total_out, total_ref = rest[:-10]
-    stores = []
-
-    def fetch(index):
-        part = parts[index]
-        here = pl.ds(256 * part, 256)
-        target = pl.ds(256 * index, 256)
-        columns = pl.ds(32 * part, 32)
-        to = pl.ds(32 * index, 32)
-        return [
-            pltpu.make_async_copy(source, goal, fetch_sems.at[index, k])
-            for k, (source, goal) in enumerate(
-                (
-                    (section_two_in.at[:, columns, :], section_two_ref.at[:, to, :]),
-                    (joined_in.at[here, :], joined_ref.at[target, :]),
-                    (probs_in.at[pl.ds(8 * part, 8)], probs_ref.at[pl.ds(8 * index, 8)]),
-                    (section_one_in.at[:, columns, :], section_one_ref.at[:, to, :]),
-                    (
-                        slope_mid_in.at[:, :, columns, :],
-                        slope_ref.at[:, pl.ds(1, 6), to, :],
-                    ),
-                    (
-                        slope_edge_in.at[:, pl.ds(0, 1), columns, :],
-                        slope_ref.at[:, pl.ds(0, 1), to, :],
-                    ),
-                    (
-                        slope_edge_in.at[:, pl.ds(1, 1), columns, :],
-                        slope_ref.at[:, pl.ds(7, 1), to, :],
-                    ),
-                    (normed_block_in.at[here, :], normed_block_ref.at[target, :]),
-                    (mixture_in.at[here, :], mixture_ref.at[target, :]),
-                )
-            )
-        ]
-
-    fetches = [fetch(0), fetch(1)]
-    for copy in fetches[0][:3]:
-        copy.start()
+    ) = near_refs
     heads_mask = heads_mask_of()
     all_windows = []
     all_joined = []
@@ -634,7 +644,7 @@
 
         wait_all(fetches[index][:1])
         if index == 0:
-            for copy in fetches[0][3:] + fetches[1]:
+            for copy in fetches[0][3:] + fetches[1] + sum(ahead, []):
                 copy.start()
         grad_two = windows_of(grad_output_ref, columns) + norm_back(
             windows_of(section_two_ref, out_columns),
@@ -695,7 +705,7 @@
         near, after = trade(ends[1], ends[0])
         near_ref[...] = near.astype(BF16)
         next_ref[...] = after.astype(BF16)
-    wait_all(stores)
+    wait_all(stores + sum(ahead, []))
 
 
 def total_kernel(
@@ -1094,18 +1104,17 @@
     edge_column = shape((ROWS, D), BF16)
     dma = pltpu.SemaphoreType.DMA
 
-    x_input, x_left, x_right = call(
+    x_input, w_expand, x_left, x_right = call(
         load_kernel,
-        [x_input],
-        [tile, edge_column, edge_column],
-        [dma, pltpu.VMEM((2, ROWS, D), F32)],
-        far=(0,),
-        keep=range(3),
+        [x_input, w_expand],
+        [tile, shape((D, E), BF16), edge_column, edge_column],
+        [dma((2,)), pltpu.VMEM((2, ROWS, D), F32)],
+        far=(0, 1),
+        keep=range(4),
         limit=4,
     )
     x_left, x_right = beside_columns(x_left, x_right)
     later = [
-        w_expand,
         dw_kernel,
         grad_output,
         w_project,
@@ -1118,7 +1127,6 @@
         lifted_far,
         slope_pre,
         lifted,
-        w_expand,
         dw_kernel,
         grad_output,
         w_project,
@@ -1128,10 +1136,10 @@
         w_out_grid,
     ) = call(
         expand_kernel,
-        [x_input, scale, shift] + later,
+        [x_input, scale, shift, w_expand] + later,
         [hidden, hidden, hidden] + [shape(v.shape, v.dtype) for v in later],
         [hidden_vmem, dma((ROWS, 2)), dma((len(later),))],
-        far=range(3, 3 + len(later)),
+        far=range(4, 4 + len(later)),
         far_out=(0, 1),
         keep=range(2, 3 + len(later)),
         limit=8,
@@ -1227,7 +1235,7 @@
         limit=20,
     )
 
-    got = across(sendable).transpose(1, 0, 2).reshape(2, TOKENS, D)
+    got = across(sendable)
     grad_groups, grid_total = call(
         grid_kernel,
         [got, w_qkv_grid, w_out_grid, cube_grid],
@@ -1235,66 +1243,65 @@
         [
             tokens_vmem,
             pltpu.VMEM((TOKENS, 3 * D), BF16),
+            pltpu.VMEM((2, TOKENS, D), BF16),
         ],
         keep=(0, 1),
         limit=8,
     )
     returned = across(grad_groups.reshape(16, 64, D).transpose(1, 0, 2)).reshape(ROWS, COLS, D)
 
-    def block_half(parts, before):
-        edge = [] if before else [shape((BLOCKS, ROWS, 128), BF16)] * 2
-        half_vmem = pltpu.VMEM((TOKENS // 2, D), BF16)
-        half_tile = pltpu.VMEM((ROWS, COLS // 2, D), BF16)
-        return call(
-            functools.partial(block_kernel, parts),
-            [
-                returned,
-                grad_output,
-                section_two,
-                section_one,
-                joined,
-                probs,
-                slope_mid.reshape(BLOCKS, 6, COLS, 128),
-                slope_edge.reshape(BLOCKS, 2, COLS, 128),
-                normed_block,
-                mixture,
-                gain_grid,
-                gain_block,
-                w_qkv_block,
-                w_out_block,
-                w_project,
-            ]
-            + before,
-            [
-                shape((ROWS, COLS // 2, D), BF16),
-                shape((BLOCKS, ROWS, COLS // 2, 128), BF16),
-                shape((2048, 128), F32),
-            ]
-            + edge,
-            ([] if before else [pltpu.VMEM((2, BLOCKS, ROWS, 128), F32)])
-            + ([pltpu.VMEM((2048, 128), F32)] if before else [])
-            + [
-                half_tile,
-                half_tile,
-                pltpu.VMEM((TOKENS // 2, 3 * D), BF16),
-                pltpu.VMEM((16, 64, 256), F32),
-                pltpu.VMEM((BLOCKS, ROWS, COLS // 2, 128), BF16),
-                half_vmem,
-                half_vmem,
-                half_tile,
-                dma((2, 9)),
-                dma((3,)),
-            ],
-            far=range(2, 10),
-            far_out=(0, 2) if before else (0,),
-            keep=(1,) if before else (1, 2, 3, 4),
-            limit=12,
-            flops=4*10**9,
-        )
-
-    one_outer, inner_outer, block_total, left, right = block_half((0, 3), [])
-    left, right = beside_columns(left, right)
-    one_middle, inner_middle, block_total = block_half((1, 2), [block_total])
+    half_tile = shape((ROWS, COLS // 2, D), BF16)
+    half_inner = shape((BLOCKS, ROWS, COLS // 2, 128), BF16)
+    block_total = shape((2048, 128), F32)
+    half_read = [
+        half_tile,
+        shape((TOKENS // 2, 3 * D), BF16),
+        shape((16, 64, 256), F32),
+        half_tile,
+        half_inner,
+        shape((TOKENS // 2, D), BF16),
+        shape((TOKENS // 2, D), BF16),
+    ]
+    half_scratch = [pltpu.VMEM(o.shape, o.dtype) for o in half_read]
+    weights = [gain_grid, gain_block, w_qkv_block, w_out_block, w_project]
+    one_outer, inner_outer, first_total, near, after, *ahead = call(
+        functools.partial(block_kernel, (0, 3)),
+        [
+            returned,
+            grad_output,
+            section_two,
+            joined,
+            probs,
+            section_one,
+            slope_mid.reshape(BLOCKS, 6, COLS, 128),
+            slope_edge.reshape(BLOCKS, 2, COLS, 128),
+            normed_block,
+            mixture,
+            *weights,
+        ],
+        [half_tile, half_inner, block_total]
+        + [shape((BLOCKS, ROWS, 128), BF16)] * 2
+        + half_read,
+        [pltpu.VMEM((2, BLOCKS, ROWS, 128), F32), half_scratch[0]]
+        + half_scratch
+        + [dma((3,)), dma((36,))],
+        far=range(2, 10),
+        far_out=(0,),
+        keep=range(1, 12),
+        limit=12,
+        flops=4 * 10**9,
+    )
+    left, right = beside_columns(near, after)
+    one_middle, inner_middle, block_total = call(
+        functools.partial(block_kernel, (1, 2)),
+        [returned, grad_output, *ahead, ahead[0], *weights, first_total],
+        [half_tile, half_inner, block_total],
+        [pltpu.VMEM((2048, 128), F32), half_scratch[0], dma((3,))],
+        far_out=(0, 2),
+        keep=(1,),
+        limit=10,
+        flops=4 * 10**9,
+    )
     edge_cells = shape((BLOCKS, 144, 128), BF16)
     first, last = call(
         inner_edge_kernel,

time: 175 us -> 172 us (0.983)
  Pallas kernels: 53.6 us -> 50.7 us
    pallas_call x18, Pallas kernels: 53.6 us -> 50.7 us  [call(): pl.pallas_call(kernel, out_shape=[pltpu.VMEM(o.shape, o.dtype) if k in ke...]
  transfers between devices with their start and end apart: 12 -> 12, of which waited for: 2 -> 3; matrix products, arithmetic and copies ran while one was open for 0% -> 0% of each run, Pallas kernels for 18% -> 16%
where the time goes in v5:
time: 172 us
  blocking collectives  78.3 us (46%)
  Pallas kernels  50.7 us (29%)
  starting transfers between devices  26 us (15%)
  waiting for transfers between devices  13.5 us (8%)
  local copies, waits for them, and re-layouts  2.11 us (1%)
    all_to_all x3, blocking collectives, across(): lax.all_to_all(values, ('row', 'hi'), split_axis=0, concat_axis=0, tiled=...  78.3 us
    pallas_call x18, Pallas kernels, call(): pl.pallas_call(kernel, out_shape=[pltpu.VMEM(o.shape, o.dtype) if k in ke...  50.7 us
    all_to_all x1, waiting for transfers between devices, across(): lax.all_to_all(values, ('row', 'hi'), split_axis=0, concat_axis=0, tiled=...  11.2 us
    ppermute x5, starting transfers between devices, sibling(): return lax.ppermute(values, 'core', [(0, 1), (1, 0)])  8.72 us
    ppermute x2, starting transfers between devices, beside_columns(): return (sibling(near), lax.ppermute(after, axes, swap))  8.11 us
    all_to_all x1, starting transfers between devices, across(): lax.all_to_all(values, ('row', 'hi'), split_axis=0, concat_axis=0, tiled=...  6.02 us
  transfers between devices with their start and end apart: 12, of which 3 were waited for; matrix products, arithmetic and copies ran while one was open for 0% of the time, Pallas kernels for 16%

profile of v5, /device:TPU:1, one launch (start us, length us, event | category | flops | bytes accessed | tf_op | source)
XLA Modules:
  0.0 171.8 jit_solution(3729060489676337402)
XLA Ops:
  0.7 1.2 shard_map.206
  1.9 1.5 collective-permute-start
  3.4 5.5 %collective-permute-start.1 = (bf16[8,256]{1,0:T(8,128)(2,1)S(1)}, bf16[8,256]{1,0:T(8,128)(2,1)S(1)}, u32[]{:S(2)}, u32[]{:S(2)}) collective-permute-start(bf16[8,256]{1,0:T(8,128)(2,1)S(1)} %get-tuple-element.85), channel_id=1, source_target_pairs={{1,2},{3,4},{5,6},{7,8},{9,10},{11,12},{13,14},{2,1},{4,3},{6,5},{... | collective-permute-start | bytes 12296 | tf_op jit(solution)/shard_map/ppermute | solution.py:1059
  8.9 0.0 copy-start.4
  8.9 0.0 copy-start.5
  8.9 4.4 %shard_map.207 = (bf16[8,1024,128]{2,1,0:T(8,128)(2,1)}, bf16[8,1024,128]{2,1,0:T(8,128)(2,1)}, bf16[8,1024,128]{2,1,0:T(8,128)(2,1)S(1)}, f32[9,1024]{1,0:T(8,1...) custom-call(bf16[8,128,256]{2,1,0:T(8,128)(2,1)S(1)} %get-tuple-elem, ...), custom_call_target="tpu_custom_call" | custom-call | flops 4000000000 | bytes 40000000 | tf_op jit(solution)/shard_map/pallas_call | solution.py:946
  13.4 0.6 shard_map.210
  14.0 0.0 collective-permute-done.near_ref
  14.0 0.0 collective-permute-done.1.next_ref
  14.0 1.4 collective-permute-start.2
  15.4 0.7 collective-permute-start.3
  16.1 0.0 copy-start
  16.1 0.0 copy-start.1
  16.1 4.8 %shard_map.209 = (bf16[8,768,128]{2,1,0:T(8,128)(2,1)}, bf16[8,768,128]{2,1,0:T(8,128)(2,1)S(1)}, bf16[8,768,128]{2,1,0:T(8,128)(2,1)}, f32[8,16,128]{2,1,0:T(8,128)S(1)}) custom-call(bf16[8,1024,128]{2,1,0:T(8,128)(2,1)S(1)} %get-tuple-element.88.lifted_ref, bf16[8,256]{1,0:T(8,128)(2,1)S(1)} %collective-permute-done.near_ref, ...), custom_call_target="tpu_custom_call" | custom-call | flops 4000000000 | bytes 40000000 | tf_op jit(solution)/shard_map/pallas_call | solution.py:946
  20.9 0.0 collective-permute-done.3.other_ref
  20.9 7.4 %shard_map.211 = (bf16[8,256,128]{2,1,0:T(8,128)(2,1)}, bf16[8,256,128]{2,1,0:T(8,128)(2,1)}, bf16[8,128,256]{2,1,0:T(8,128)(2,1)}, bf16[8,128,256]{2,1,0:T(8,12...) custom-call(bf16[8,128,256]{2,1,0:T(8,128)(2,1)S(1)} %get-tuple-elem, ...), custom_call_target="tpu_custom_call" | custom-call | flops 1000000000 | bytes 10000000 | tf_op jit(solution)/shard_map/pallas_call | solution.py:946
  28.4 27.0 %all_to_all.20.got_ref = bf16[64,32,256]{2,1,0:T(8,128)(2,1)S(1)} all-to-all(bf16[64,32,256]{2,1,0:T(8,128)(2,1)S(1)} %get-tuple-element.97), channel_id=1, replica_groups=mesh['row'=8,'hi'=8,'core'=2] {'row','hi'}, dimensions={0} | all-to-all | bytes 2097152 | tf_op jit(solution)/shard_map/all_to_all | solution.py:1063
  55.4 5.8 %shard_map.212 = (bf16[1024,256]{1,0:T(8,128)(2,1)S(1)}, f32[2048,128]{1,0:T(8,128)S(1)}) custom-call(bf16[64,32,256]{2,1,0:T(8,128)(2,1)S(1)} %all_to_all.20.got_ref, bf16[256,768]{1,0:T(8,128)(2,1)S(1)} %get-tuple-element.98.w_qkv_ref, bf16[256,256]{1,0:T(8,128)(2,1)S(1)} %get-tuple-element.99.w_out_ref, f32[2,64,256]{2,1,0:T(8,128)S(1)} %get-tuple-element.100.bias), custom_call_target="tpu_custom_call" | custom-call | flops 1000000000 | bytes 10000000 | tf_op jit(solution)/shard_map/pallas_call | solution.py:946
  61.1 0.0 copy-start.6
  61.1 1.0 copy-done.6
  62.1 1.1 copy.25
  63.2 6.0 %all-to-all-start.1 = ((bf16[64,16,256]{2,1,0:T(8,128)(2,1)}), bf16[64,16,256]{2,1,0:T(8,128)(2,1)S(1)}, u32[]{:S(2)}, u32[]{:S(2)}) async-start(bf16[64,16,256]{2,1,0:T(8,128)(2,1)} %bitcast.30), calls=%async_computation.1 | async-start | bytes 1048576 | tf_op jit(solution)/shard_map/all_to_all | solution.py:1063
  69.2 11.2 %all-to-all-done.1 = bf16[64,16,256]{2,1,0:T(8,128)(2,1)S(1)} async-done(((bf16[64,16,256]{2,1,0:T(8,128)(2,1)}), bf16[64,16,256]{2,1,0:T(8,128)(2,1)S(1)}, u32[]{:S(2)}, u32[]{:S(2)}) %all-to-all-start.1) | async-done | bytes 524320 | tf_op jit(solution)/shard_map/all_to_all | solution.py:1063
  80.4 6.0 %shard_map.213 = (bf16[8,64,256]{2,1,0:T(8,128)(2,1)}, bf16[8,8,64,128]{3,2,1,0:T(8,128)(2,1)S(1)}, f32[2048,128]{1,0:T(8,128)S(1)}, bf16[8,8,128]{2,1,0:T(8,128...) custom-call(bf16[8,128,256]{2,1,0:T(8,128)(2,1)S(1)} %bitcast.12, ...), custom_call_target="tpu_custom_call" | custom-call | flops 4000000000 | bytes 40000000 | tf_op jit(solution)/shard_map/pallas_call | solution.py:946
  86.4 3.0 %collective-permute-start.4 = (bf16[8,8,128]{2,1,0:T(8,128)(2,1)S(1)}, bf16[8,8,128]{2,1,0:T(8,128)(2,1)S(1)}, u32[]{:S(2)}, u32[]{:S(2)}) collective-permute-start(bf16[8,8,128]{2,1,0:T(8,128)(2,1)S(1)} %get-tuple-element.120), channel_id=1, source_target_pairs={{0,1},{1,0},{2,3},{3,2},{4,5},{5,4},{6,7},{7,6},{8,9},{9,8},{10,11... | collective-permute-start | bytes 49160 | tf_op jit(solution)/shard_map/ppermute | solution.py:1067
  89.4 2.6 %collective-permute-start.5 = (bf16[8,8,128]{2,1,0:T(8,128)(2,1)S(1)}, bf16[8,8,128]{2,1,0:T(8,128)(2,1)S(1)}, u32[]{:S(2)}, u32[]{:S(2)}) collective-permute-start(bf16[8,8,128]{2,1,0:T(8,128)(2,1)S(1)} %get-tuple-element.121), channel_id=1, source_target_pairs={{1,2},{3,4},{5,6},{7,8},{9,10},{11,12},{13,14},{2,1},{4,3},{6,5},{... | collective-permute-start | bytes 49160 | tf_op jit(solution)/shard_map/ppermute | solution.py:1059
  92.1 3.8 %shard_map.214 = (bf16[8,64,256]{2,1,0:T(8,128)(2,1)}, bf16[8,8,64,128]{3,2,1,0:T(8,128)(2,1)S(1)}, f32[2048,128]{1,0:T(8,128)}) custom-call(bf16[8,128,256]{2,1,0:T(8,128)(2,1)S(1)} %bitcast.13, bf16[8,128,256]{2,1,0:T(8,128)(2,1)S(1)} %get-tuple-element.96.grad_output_ref, bf16[8,64,256]{2,1,0:T(8,128)(2,1)S(1)} %get-tuple-element.111.section_two_in.mixture_in, ...), custom_call_target="tpu_custom_call" | custom-call | flops 4000000000 | bytes 40000000 | tf_op jit(solution)/shard_map/pallas_call | solution.py:946
  95.9 0.0 collective-permute-done.4.near_ref
  95.9 0.1 collective-permute-done.5.next_ref
  96.0 0.1 shard_map.216
  96.1 0.4 collective-permute-start.6
  96.5 0.7 collective-permute-start.7
  97.2 2.7 %shard_map.217 = (bf16[8,128,256]{2,1,0:T(8,128)(2,1)S(1)}, bf16[3072,128]{1,0:T(8,128)(2,1)S(1)}, bf16[3072,128]{1,0:T(8,128)(2,1)S(1)}) custom-call(s32[1]{0:T(128)} %bitcast.9.core_ref, bf16[8,64,256]{2,1,0:T(8,128)(2,1)} %get-tuple-element.126.outer_in, bf16[8,64,256]{2,1,0:T(8,128)(2,1)} %get-tuple-element.127.middle_in, ...), custom_call_target="tpu_custom_call" | custom-call | flops 3000000000 | bytes 30000000 | tf_op jit(solution)/shard_map/pallas_call | solution.py:946
  99.9 0.1 collective-permute-start.8
  100.0 5.7 %shard_map.215 = (bf16[8,768,128]{2,1,0:T(8,128)(2,1)S(1)}, f32[9,8,128]{2,1,0:T(8,128)S(1)}) custom-call(bf16[8,1024,128]{2,1,0:T(8,128)(2,1)} %get-tuple-element.82.lifted_in, bf16[8,1024,128]{2,1,0:T(8,128)(2,1)} %get-tuple-element.83.slope_pre_in, bf16[8,8,64,128]{3,2,1,0:T(8,128)(2,1)S(1)} %get-tuple-element.110.outer_ref, ...), custom_call_target="tpu_custom_call" | custom-call | flops 4000000000 | bytes 40000000 | tf_op jit(solution)/shard_map/pallas_call | solution.py:946
  105.8 3.7 %shard_map.218 = (bf16[8,256,128]{2,1,0:T(8,128)(2,1)S(1)}, bf16[64,24,128]{2,1,0:T(8,128)(2,1)S(1)}, bf16[64,24,128]{2,1,0:T(8,128)(2,1)S(1)}) custom-call(s32[1]{0:T(128)} %bitcast.9.core_ref, bf16[8,128,256]{2,1,0:T(8,128)(2,1)S(1)} %get-tuple-element.80.x_ref, bf16[8,1024,128]{2,1,0:T(8,128)(2,1)} %get-tuple-element.82.lifted_in, ...), custom_call_target="tpu_custom_call" | custom-call | flops 4000000000 | bytes 40000000 | tf_op jit(solution)/shard_map/pallas_call | solution.py:946
  109.5 0.6 collective-permute-start.9
  110.1 1.6 shard_map.219._
  111.6 0.0 collective-permute-done.9.late_got_ref
  111.6 0.0 collective-permute-done.8.early_got_ref
  111.6 0.3 shard_map.220
  111.9 28.8 %all_to_all.21.got_ref = bf16[64,72,128]{2,1,0:T(8,128)(2,1)S(1)} all-to-all(bf16[64,72,128]{2,1,0:T(8,128)(2,1)S(1)} %shard_map.220), channel_id=1, replica_groups=mesh['row'=8,'hi'=8,'core'=2] {'row','hi'}, dimensions={0} | all-to-all | bytes 2359296 | tf_op jit(solution)/shard_map/all_to_all | solution.py:1063
  140.8 0.3 shard_map.221
  141.0 22.5 %all_to_all.22.mine_ref = bf16[64,72,128]{2,1,0:T(8,128)(2,1)S(1)} all-to-all(bf16[64,72,128]{2,1,0:T(8,128)(2,1)S(1)} %shard_map.221), channel_id=1, replica_groups=mesh['row'=8,'hi'=8,'core'=2] {'row','hi'}, dimensions={0} | all-to-all | bytes 2359296 | tf_op jit(solution)/shard_map/all_to_all | solution.py:1063
  163.5 3.5 %collective-permute-start.10 = (bf16[64,72,128]{2,1,0:T(8,128)(2,1)S(1)}, bf16[64,72,128]{2,1,0:T(8,128)(2,1)S(1)}, u32[]{:S(2)}, u32[]{:S(2)}) collective-permute-start(bf16[64,72,128]{2,1,0:T(8,128)(2,1)S(1)} %all_to_all.22.mine_ref), channel_id=1, source_target_pairs={{0,1},{1,0},{2,3},{3,2},{4,5},{5,4},{6,7},{7,6},{8,9},{9,8},{10,11... | collective-permute-start | bytes 3538952 | tf_op jit(solution)/shard_map/ppermute | solution.py:1067
  167.1 0.2 shard_map.222
  167.3 2.3 %collective-permute-done.10.other_ref = bf16[64,72,128]{2,1,0:T(8,128)(2,1)S(1)} collective-permute-done((bf16[64,72,128]{2,1,0:T(8,128)(2,1)S(1)}, bf16[64,72,128]{2,1,0:T(8,128)(2,1)S(1)}, u32[]{:S(2)}, u32[]{:S(2)}) %collective-permute-start.10) | collective-permute-done | bytes 1179680 | tf_op jit(solution)/shard_map/ppermute | solution.py:1067
  169.5 2.1 %shard_map.223 = (f32[256,1024]{1,0:T(8,128)}, f32[9,1024]{1,0:T(8,128)}, f32[1024,256]{1,0:T(8,128)}, f32[256,768]{1,0:T(8,128)}, f32[256,256]{1,0:T(8,128)}, /*index=5*/f32[256,768]{1,0:T(8,128)}, f32[256,256]{1,0:T(8,128)}) custom-call(s32[1]{0:T(128)} %bitcast.9.core_ref, bf16[64,72,128]{2,1,0:T(8,128)(2,1)S(1)} %collective-permute-done.10.other_ref, ...), custom_call_target="tpu_custom_call" | custom-call | flops 1000000000 | bytes 10000000 | tf_op jit(solution)/shard_map/pallas_call | solution.py:946
  (12 shorter events, 0.1 us)
Async XLA Ops:
  0.6 8.3 %copy-start.3 = (f32[256]{0:T(256)S(1)}, f32[256]{0:T(256)}, u32[]{:S(2)}) copy-start(f32[256]{0:T(256)} %param.17) | copy-start | bytes 3076
  0.6 8.3 %copy-start.2 = (f32[256]{0:T(256)S(1)}, f32[256]{0:T(256)}, u32[]{:S(2)}) copy-start(f32[256]{0:T(256)} %param.18) | copy-start | bytes 3076
  1.9 12.1 %collective-permute-start = (bf16[8,256]{1,0:T(8,128)(2,1)S(1)}, bf16[8,256]{1,0:T(8,128)(2,1)S(1)}, u32[]{:S(2)}, u32[]{:S(2)}) collective-permute-start(bf16[8,256]{1,0:T(8,128)(2,1)S(1)} %get-tuple-element.84), channel_id=1, source_target_pairs={{0,1},{1,0},{2,3},{3,2},{4,5},{5,4},{6,7},{7,6},{8,9},{9,8},{10,11... | collective-permute-start | bytes 12296 | tf_op jit(solution)/shard_map/ppermute | solution.py:1067
  3.4 10.6 %collective-permute-start.1 = (bf16[8,256]{1,0:T(8,128)(2,1)S(1)}, bf16[8,256]{1,0:T(8,128)(2,1)S(1)}, u32[]{:S(2)}, u32[]{:S(2)}) collective-permute-start(bf16[8,256]{1,0:T(8,128)(2,1)S(1)} %get-tuple-element.85), channel_id=1, source_target_pairs={{1,2},{3,4},{5,6},{7,8},{9,10},{11,12},{13,14},{2,1},{4,3},{6,5},{... | collective-permute-start | bytes 12296 | tf_op jit(solution)/shard_map/ppermute | solution.py:1059
  8.9 4.4 %copy-start.4 = (f32[8,225]{1,0:T(8,128)S(1)}, f32[8,225]{1,0:T(8,128)}, u32[]{:S(2)}) copy-start(f32[8,225]{1,0:T(8,128)} %block_ref.1) | copy-start | bytes 21604
  8.9 4.4 %copy-start.5 = (f32[8,225]{1,0:T(8,128)S(1)}, f32[8,225]{1,0:T(8,128)}, u32[]{:S(2)}) copy-start(f32[8,225]{1,0:T(8,128)} %grid_ref.1) | copy-start | bytes 21604
  14.0 6.9 %collective-permute-start.2 = (bf16[144,256]{1,0:T(8,128)(2,1)S(1)}, bf16[144,256]{1,0:T(8,128)(2,1)S(1)}, u32[]{:S(2)}, u32[]{:S(2)}) collective-permute-start(bf16[144,256]{1,0:T(8,128)(2,1)S(1)} %get-tuple-element.86), channel_id=1, source_target_pairs={{0,16},{32,48},{64,80},{96,112},{16,0},{48,32},{80,64},{112,96},{1... | collective-permute-start | bytes 221192 | tf_op jit(solution)/shard_map/ppermute | solution.py:1051
  15.4 5.5 %collective-permute-start.3 = (bf16[144,256]{1,0:T(8,128)(2,1)S(1)}, bf16[144,256]{1,0:T(8,128)(2,1)S(1)}, u32[]{:S(2)}, u32[]{:S(2)}) collective-permute-start(bf16[144,256]{1,0:T(8,128)(2,1)S(1)} %get-tuple-element.87), channel_id=1, source_target_pairs={{16,32},{48,64},{80,96},{32,16},{64,48},{96,80},{17,33},{49,65},{8... | collective-permute-start | bytes 221192 | tf_op jit(solution)/shard_map/ppermute | solution.py:1051
  16.1 4.8 %copy-start = (f32[256]{0:T(256)S(1)}, f32[256]{0:T(256)}, u32[]{:S(2)}) copy-start(f32[256]{0:T(256)} %param.22) | copy-start | bytes 3076
  16.1 4.8 %copy-start.1 = (f32[256]{0:T(256)S(1)}, f32[256]{0:T(256)}, u32[]{:S(2)}) copy-start(f32[256]{0:T(256)} %param.26) | copy-start | bytes 3076
  61.1 1.0 copy-start.6
  63.2 17.2 %all-to-all-start.1 = ((bf16[64,16,256]{2,1,0:T(8,128)(2,1)}), bf16[64,16,256]{2,1,0:T(8,128)(2,1)S(1)}, u32[]{:S(2)}, u32[]{:S(2)}) async-start(bf16[64,16,256]{2,1,0:T(8,128)(2,1)} %bitcast.30), calls=%async_computation.1 | async-start | bytes 1048576 | tf_op jit(solution)/shard_map/all_to_all | solution.py:1063
  86.4 9.5 %collective-permute-start.4 = (bf16[8,8,128]{2,1,0:T(8,128)(2,1)S(1)}, bf16[8,8,128]{2,1,0:T(8,128)(2,1)S(1)}, u32[]{:S(2)}, u32[]{:S(2)}) collective-permute-start(bf16[8,8,128]{2,1,0:T(8,128)(2,1)S(1)} %get-tuple-element.120), channel_id=1, source_target_pairs={{0,1},{1,0},{2,3},{3,2},{4,5},{5,4},{6,7},{7,6},{8,9},{9,8},{10,11... | collective-permute-start | bytes 49160 | tf_op jit(solution)/shard_map/ppermute | solution.py:1067
  89.4 6.5 %collective-permute-start.5 = (bf16[8,8,128]{2,1,0:T(8,128)(2,1)S(1)}, bf16[8,8,128]{2,1,0:T(8,128)(2,1)S(1)}, u32[]{:S(2)}, u32[]{:S(2)}) collective-permute-start(bf16[8,8,128]{2,1,0:T(8,128)(2,1)S(1)} %get-tuple-element.121), channel_id=1, source_target_pairs={{1,2},{3,4},{5,6},{7,8},{9,10},{11,12},{13,14},{2,1},{4,3},{6,5},{... | collective-permute-start | bytes 49160 | tf_op jit(solution)/shard_map/ppermute | solution.py:1059
  96.1 9.7 %collective-permute-start.6 = (bf16[8,144,128]{2,1,0:T(8,128)(2,1)S(1)}, bf16[8,144,128]{2,1,0:T(8,128)(2,1)S(1)}, u32[]{:S(2)}, u32[]{:S(2)}) collective-permute-start(bf16[8,144,128]{2,1,0:T(8,128)(2,1)S(1)} %get-tuple-element.123._), channel_id=1, source_target_pairs={{0,16},{32,48},{64,80},{96,112},{16,0},{48,32},{80,64},{112,96},{1... | collective-permute-start | bytes 884744 | tf_op jit(solution)/shard_map/ppermute | solution.py:1051
  96.5 9.3 %collective-permute-start.7 = (bf16[8,144,128]{2,1,0:T(8,128)(2,1)S(1)}, bf16[8,144,128]{2,1,0:T(8,128)(2,1)S(1)}, u32[]{:S(2)}, u32[]{:S(2)}) collective-permute-start(bf16[8,144,128]{2,1,0:T(8,128)(2,1)S(1)} %get-tuple-element.124), channel_id=1, source_target_pairs={{16,32},{48,64},{80,96},{32,16},{64,48},{96,80},{17,33},{49,65},{8... | collective-permute-start | bytes 884744 | tf_op jit(solution)/shard_map/ppermute | solution.py:1051
  99.9 11.7 %collective-permute-start.8 = (bf16[3072,128]{1,0:T(8,128)(2,1)S(1)}, bf16[3072,128]{1,0:T(8,128)(2,1)S(1)}, u32[]{:S(2)}, u32[]{:S(2)}) collective-permute-start(bf16[3072,128]{1,0:T(8,128)(2,1)S(1)} %get-tuple-element.135), channel_id=1, source_target_pairs={{0,1},{1,0},{2,3},{3,2},{4,5},{5,4},{6,7},{7,6},{8,9},{9,8},{10,11... | collective-permute-start | bytes 2359304 | tf_op jit(solution)/shard_map/ppermute | solution.py:1067
  109.5 2.1 %collective-permute-start.9 = (bf16[64,24,128]{2,1,0:T(8,128)(2,1)S(1)}, bf16[64,24,128]{2,1,0:T(8,128)(2,1)S(1)}, u32[]{:S(2)}, u32[]{:S(2)}) collective-permute-start(bf16[64,24,128]{2,1,0:T(8,128)(2,1)S(1)} %get-tuple-element.137), channel_id=1, source_target_pairs={{0,1},{1,0},{2,3},{3,2},{4,5},{5,4},{6,7},{7,6},{8,9},{9,8},{10,11... | collective-permute-start | bytes 1179656 | tf_op jit(solution)/shard_map/ppermute | solution.py:1067
  163.5 6.0 %collective-permute-start.10 = (bf16[64,72,128]{2,1,0:T(8,128)(2,1)S(1)}, bf16[64,72,128]{2,1,0:T(8,128)(2,1)S(1)}, u32[]{:S(2)}, u32[]{:S(2)}) collective-permute-start(bf16[64,72,128]{2,1,0:T(8,128)(2,1)S(1)} %all_to_all.22.mine_ref), channel_id=1, source_target_pairs={{0,1},{1,0},{2,3},{3,2},{4,5},{5,4},{6,7},{7,6},{8,9},{9,8},{10,11... | collective-permute-start | bytes 3538952 | tf_op jit(solution)/shard_map/ppermute | solution.py:1067

commit v6 on v5

--- a/solution.py
+++ b/solution.py
@@ -209,10 +209,10 @@
         total = dot(normed_ref[...], grad_joined_ref[:, D * part : D * part + D], 0, 0)
         for k in range(2):
             start = 256 * (2 * part + k)
-            total_ref[start : start + 256, :] = total[:, 128 * k : 128 * k + 128]
+            total_ref[start : start + 256, :] = total[:, 128 * k : 128 * k + 128].astype(BF16)
     total = dot(mixture_ref[...], grad_ref[...], 0, 0)
     for k in range(2):
-        total_ref[1536 + 256 * k : 1792 + 256 * k, :] = total[:, 128 * k : 128 * k + 128]
+        total_ref[1536 + 256 * k : 1792 + 256 * k, :] = total[:, 128 * k : 128 * k + 128].astype(BF16)
 
 
 def edge_flags():
@@ -527,6 +527,7 @@
     mixture_ref,
     grad_joined_ref,
     groups_ref,
+    ordered,
 ):
     heads_mask = heads_mask_of()
     for index in range(2):
@@ -546,9 +547,11 @@
         mixture_ref[here, :] = mixture
         grad_joined = attend_back(joined, probs, grad_mix, heads_mask)
         grad_joined_ref[here, :] = grad_joined
-        grad_normed_ref[here, :] = dot(grad_joined, w_qkv_ref[...], 1, 1).astype(BF16)
+        grad_normed = dot(grad_joined, w_qkv_ref[...], 1, 1).reshape(4, 64, D)
+        ordered[:, 4 * part : 4 * part + 4, :] = grad_normed.transpose(1, 0, 2)
 
     attention_totals(total_ref, normed_ref, grad_joined_ref, mixture_ref, grad_ref)
+    grad_normed_ref[...] = ordered[...].astype(BF16)
 
 
 def quarter_fetches(far, near, parts, sems, first):
@@ -683,7 +686,10 @@
         for k in range(2):
             place = slice(start + 256 * k, start + 256 * k + 256)
             value = total[:, 128 * k : 128 * k + 128]
-            total_ref[place, :] = value if before_ref is None else before_ref[place, :] + value
+            if before_ref is None:
+                total_ref[place, :] = value
+            else:
+                total_ref[place, :] = (before_ref[place, :] + value).astype(BF16)
     if before_ref is not None:
         stores += copy_all([(total_ref, total_out)], sems, first=2)
     for index, part in enumerate(parts):
@@ -745,12 +751,12 @@
         total = dot(joined, grad_one, 0, 0)
         for k in range(2):
             start = 2048 + 1024 * k + 256 * pair
-            total_ref[start : start + 256, :] = total[:, 128 * k : 128 * k + 128]
+            total_ref[start : start + 256, :] = total[:, 128 * k : 128 * k + 128].astype(BF16)
     wait_all(fetches[6:])
     own = pl.ds(pl.multiple_of(core_ref[0] * 3072, 3072), 3072)
     other = pl.ds(pl.multiple_of((1 - core_ref[0]) * 3072, 3072), 3072)
-    early_keep_ref[...] = total_ref[own, :].astype(BF16)
-    early_send_ref[...] = total_ref[other, :].astype(BF16)
+    early_keep_ref[...] = total_ref[own, :]
+    early_send_ref[...] = total_ref[other, :]
 
 
 def back_rows(pad, block, pad_row, taps, lifted_ref, slope_pre_ref, preact_ref, row, totals):
@@ -1239,16 +1245,17 @@
     grad_groups, grid_total = call(
         grid_kernel,
         [got, w_qkv_grid, w_out_grid, cube_grid],
-        [tokens, shape((2048, 128), F32)],
+        [shape((64, 16, D), BF16), shape((2048, 128), BF16)],
         [
             tokens_vmem,
             pltpu.VMEM((TOKENS, 3 * D), BF16),
             pltpu.VMEM((2, TOKENS, D), BF16),
+            pltpu.VMEM((64, 16, D), F32),
         ],
         keep=(0, 1),
         limit=8,
     )
-    returned = across(grad_groups.reshape(16, 64, D).transpose(1, 0, 2)).reshape(ROWS, COLS, D)
+    returned = across(grad_groups).reshape(ROWS, COLS, D)
 
     half_tile = shape((ROWS, COLS // 2, D), BF16)
     half_inner = shape((BLOCKS, ROWS, COLS // 2, 128), BF16)
@@ -1295,8 +1302,8 @@
     one_middle, inner_middle, block_total = call(
         functools.partial(block_kernel, (1, 2)),
         [returned, grad_output, *ahead, ahead[0], *weights, first_total],
-        [half_tile, half_inner, block_total],
-        [pltpu.VMEM((2048, 128), F32), half_scratch[0], dma((3,))],
+        [half_tile, half_inner, shape((2048, 128), BF16)],
+        [pltpu.VMEM((2048, 128), BF16), half_scratch[0], dma((3,))],
         far_out=(0, 2),
         keep=(1,),
         limit=10,
@@ -1326,7 +1333,7 @@
             first,
         ],
         [tile, early, early],
-        [pltpu.VMEM((6144, 128), F32), hidden_vmem, dma((8,))],
+        [pltpu.VMEM((6144, 128), BF16), hidden_vmem, dma((8,))],
         smem=(0,),
         far=range(1, 7),
         keep=range(3),

time: 172 us -> 171 us (level)
  no operation moved by 1% of the time
where the time goes in v6:
time: 171 us
  blocking collectives  78.2 us (46%)
  Pallas kernels  50.8 us (30%)
  starting transfers between devices  26 us (15%)
  waiting for transfers between devices  13.8 us (8%)
    all_to_all x3, blocking collectives, across(): lax.all_to_all(values, ('row', 'hi'), split_axis=0, concat_axis=0, tiled=...  78.2 us
    pallas_call x18, Pallas kernels, call(): pl.pallas_call(kernel, out_shape=[pltpu.VMEM(o.shape, o.dtype) if k in ke...  50.8 us
    all_to_all x1, waiting for transfers between devices, across(): lax.all_to_all(values, ('row', 'hi'), split_axis=0, concat_axis=0, tiled=...  11.1 us
    ppermute x5, starting transfers between devices, sibling(): return lax.ppermute(values, 'core', [(0, 1), (1, 0)])  8.74 us
    ppermute x2, starting transfers between devices, beside_columns(): return (sibling(near), lax.ppermute(after, axes, swap))  8.12 us
    all_to_all x1, starting transfers between devices, across(): lax.all_to_all(values, ('row', 'hi'), split_axis=0, concat_axis=0, tiled=...  6.02 us
  transfers between devices with their start and end apart: 12, of which 3 were waited for; matrix products, arithmetic and copies ran while one was open for 0% of the time, Pallas kernels for 16%

profile of v6, /device:TPU:1, one launch (start us, length us, event | category | flops | bytes accessed | tf_op | source)
XLA Modules:
  0.0 170.7 jit_solution(17323061389167277953)
XLA Ops:
  0.7 1.2 shard_map.206
  1.9 1.5 collective-permute-start
  3.4 5.5 %collective-permute-start.1 = (bf16[8,256]{1,0:T(8,128)(2,1)S(1)}, bf16[8,256]{1,0:T(8,128)(2,1)S(1)}, u32[]{:S(2)}, u32[]{:S(2)}) collective-permute-start(bf16[8,256]{1,0:T(8,128)(2,1)S(1)} %get-tuple-element.85), channel_id=1, source_target_pairs={{1,2},{3,4},{5,6},{7,8},{9,10},{11,12},{13,14},{2,1},{4,3},{6,5},{... | collective-permute-start | bytes 12296 | tf_op jit(solution)/shard_map/ppermute | solution.py:1065
  8.9 0.0 copy-start.4
  8.9 0.0 copy-start.5
  8.9 4.4 %shard_map.207 = (bf16[8,1024,128]{2,1,0:T(8,128)(2,1)}, bf16[8,1024,128]{2,1,0:T(8,128)(2,1)}, bf16[8,1024,128]{2,1,0:T(8,128)(2,1)S(1)}, f32[9,1024]{1,0:T(8,1...) custom-call(bf16[8,128,256]{2,1,0:T(8,128)(2,1)S(1)} %get-tuple-elem, ...), custom_call_target="tpu_custom_call" | custom-call | flops 4000000000 | bytes 40000000 | tf_op jit(solution)/shard_map/pallas_call | solution.py:952
  13.4 0.6 shard_map.210
  14.0 0.0 collective-permute-done.near_ref
  14.0 0.0 collective-permute-done.1.next_ref
  14.0 1.4 collective-permute-start.2
  15.4 0.7 collective-permute-start.3
  16.1 0.0 copy-start
  16.1 0.0 copy-start.1
  16.1 4.8 %shard_map.209 = (bf16[8,768,128]{2,1,0:T(8,128)(2,1)}, bf16[8,768,128]{2,1,0:T(8,128)(2,1)S(1)}, bf16[8,768,128]{2,1,0:T(8,128)(2,1)}, f32[8,16,128]{2,1,0:T(8,128)S(1)}) custom-call(bf16[8,1024,128]{2,1,0:T(8,128)(2,1)S(1)} %get-tuple-element.88.lifted_ref, bf16[8,256]{1,0:T(8,128)(2,1)S(1)} %collective-permute-done.near_ref, ...), custom_call_target="tpu_custom_call" | custom-call | flops 4000000000 | bytes 40000000 | tf_op jit(solution)/shard_map/pallas_call | solution.py:952
  20.9 0.0 collective-permute-done.2.pair_ref
  20.9 0.0 collective-permute-done.3.other_ref
  20.9 7.4 %shard_map.211 = (bf16[8,256,128]{2,1,0:T(8,128)(2,1)}, bf16[8,256,128]{2,1,0:T(8,128)(2,1)}, bf16[8,128,256]{2,1,0:T(8,128)(2,1)}, bf16[8,128,256]{2,1,0:T(8,12...) custom-call(bf16[8,128,256]{2,1,0:T(8,128)(2,1)S(1)} %get-tuple-elem, ...), custom_call_target="tpu_custom_call" | custom-call | flops 1000000000 | bytes 10000000 | tf_op jit(solution)/shard_map/pallas_call | solution.py:952
  28.3 27.0 %all_to_all.20.got_ref = bf16[64,32,256]{2,1,0:T(8,128)(2,1)S(1)} all-to-all(bf16[64,32,256]{2,1,0:T(8,128)(2,1)S(1)} %get-tuple-element.97), channel_id=1, replica_groups=mesh['row'=8,'hi'=8,'core'=2] {'row','hi'}, dimensions={0} | all-to-all | bytes 2097152 | tf_op jit(solution)/shard_map/all_to_all | solution.py:1069
  55.3 6.2 %shard_map.212 = (bf16[64,16,256]{2,1,0:T(8,128)(2,1)}, bf16[2048,128]{1,0:T(8,128)(2,1)S(1)}) custom-call(bf16[64,32,256]{2,1,0:T(8,128)(2,1)S(1)} %all_to_all.20.got_ref, bf16[256,768]{1,0:T(8,128)(2,1)S(1)} %get-tuple-element.98.w_qkv_ref, bf16[256,256]{1,0:T(8,128)(2,1)S(1)} %get-tuple-element.99.w_out_ref, f32[2,64,256]{2,1,0:T(8,128)S(1)} %get-tuple-element.100.bias), custom_call_target="tpu_custom_call" | custom-call | flops 1000000000 | bytes 10000000 | tf_op jit(solution)/shard_map/pallas_call | solution.py:952
  61.6 0.8 copy-done.6
  62.4 6.0 %all-to-all-start.1 = ((bf16[64,16,256]{2,1,0:T(8,128)(2,1)}), bf16[64,16,256]{2,1,0:T(8,128)(2,1)S(1)}, u32[]{:S(2)}, u32[]{:S(2)}) async-start(bf16[64,16,256]{2,1,0:T(8,128)(2,1)} %get-tuple-element.101), calls=%async_computation.1 | async-start | bytes 1048576 | tf_op jit(solution)/shard_map/all_to_all | solution.py:1069
  68.4 11.1 %all-to-all-done.1 = bf16[64,16,256]{2,1,0:T(8,128)(2,1)S(1)} async-done(((bf16[64,16,256]{2,1,0:T(8,128)(2,1)}), bf16[64,16,256]{2,1,0:T(8,128)(2,1)S(1)}, u32[]{:S(2)}, u32[]{:S(2)}) %all-to-all-start.1) | async-done | bytes 524320 | tf_op jit(solution)/shard_map/all_to_all | solution.py:1069
  79.5 6.0 %shard_map.213 = (bf16[8,64,256]{2,1,0:T(8,128)(2,1)}, bf16[8,8,64,128]{3,2,1,0:T(8,128)(2,1)S(1)}, f32[2048,128]{1,0:T(8,128)S(1)}, bf16[8,8,128]{2,1,0:T(8,128...) custom-call(bf16[8,128,256]{2,1,0:T(8,128)(2,1)S(1)} %bitcast.8, ...), custom_call_target="tpu_custom_call" | custom-call | flops 4000000000 | bytes 40000000 | tf_op jit(solution)/shard_map/pallas_call | solution.py:952
  85.6 3.0 %collective-permute-start.4 = (bf16[8,8,128]{2,1,0:T(8,128)(2,1)S(1)}, bf16[8,8,128]{2,1,0:T(8,128)(2,1)S(1)}, u32[]{:S(2)}, u32[]{:S(2)}) collective-permute-start(bf16[8,8,128]{2,1,0:T(8,128)(2,1)S(1)} %get-tuple-element.120), channel_id=1, source_target_pairs={{0,1},{1,0},{2,3},{3,2},{4,5},{5,4},{6,7},{7,6},{8,9},{9,8},{10,11... | collective-permute-start | bytes 49160 | tf_op jit(solution)/shard_map/ppermute | solution.py:1073
  88.6 2.6 %collective-permute-start.5 = (bf16[8,8,128]{2,1,0:T(8,128)(2,1)S(1)}, bf16[8,8,128]{2,1,0:T(8,128)(2,1)S(1)}, u32[]{:S(2)}, u32[]{:S(2)}) collective-permute-start(bf16[8,8,128]{2,1,0:T(8,128)(2,1)S(1)} %get-tuple-element.121), channel_id=1, source_target_pairs={{1,2},{3,4},{5,6},{7,8},{9,10},{11,12},{13,14},{2,1},{4,3},{6,5},{... | collective-permute-start | bytes 49160 | tf_op jit(solution)/shard_map/ppermute | solution.py:1065
  91.2 3.6 %shard_map.214 = (bf16[8,64,256]{2,1,0:T(8,128)(2,1)}, bf16[8,8,64,128]{3,2,1,0:T(8,128)(2,1)S(1)}, bf16[2048,128]{1,0:T(8,128)(2,1)}) custom-call(bf16[8,128,256]{2,1,0:T(8,128)(2,1)S(1)} %bitcast.9, bf16[8,128,256]{2,1,0:T(8,128)(2,1)S(1)} %get-tuple-element.96.grad_output_ref, bf16[8,64,256]{2,1,0:T(8,128)(2,1)S(1)} %get-tuple-element.111.section_two_in.mixture_in, ...), custom_call_target="tpu_custom_call" | custom-call | flops 4000000000 | bytes 40000000 | tf_op jit(solution)/shard_map/pallas_call | solution.py:952
  94.8 0.0 collective-permute-done.4.near_ref
  94.8 0.3 collective-permute-done.5.next_ref
  95.2 0.1 shard_map.216
  95.3 0.4 collective-permute-start.6
  95.7 0.7 collective-permute-start.7
  96.4 2.7 %shard_map.217 = (bf16[8,128,256]{2,1,0:T(8,128)(2,1)S(1)}, bf16[3072,128]{1,0:T(8,128)(2,1)S(1)}, bf16[3072,128]{1,0:T(8,128)(2,1)S(1)}) custom-call(s32[1]{0:T(128)} %bitcast.7.core_ref, bf16[8,64,256]{2,1,0:T(8,128)(2,1)} %get-tuple-element.126.outer_in, bf16[8,64,256]{2,1,0:T(8,128)(2,1)} %get-tuple-element.127.middle_in, ...), custom_call_target="tpu_custom_call" | custom-call | flops 3000000000 | bytes 30000000 | tf_op jit(solution)/shard_map/pallas_call | solution.py:952
  99.0 0.1 collective-permute-start.8
  99.1 5.7 %shard_map.215 = (bf16[8,768,128]{2,1,0:T(8,128)(2,1)S(1)}, f32[9,8,128]{2,1,0:T(8,128)S(1)}) custom-call(bf16[8,1024,128]{2,1,0:T(8,128)(2,1)} %get-tuple-element.82.lifted_in, bf16[8,1024,128]{2,1,0:T(8,128)(2,1)} %get-tuple-element.83.slope_pre_in, bf16[8,8,64,128]{3,2,1,0:T(8,128)(2,1)S(1)} %get-tuple-element.110.outer_ref, ...), custom_call_target="tpu_custom_call" | custom-call | flops 4000000000 | bytes 40000000 | tf_op jit(solution)/shard_map/pallas_call | solution.py:952
  104.9 0.0 collective-permute-done.6.pair_ref
  104.9 0.0 collective-permute-done.7.other_ref
  104.9 3.7 %shard_map.218 = (bf16[8,256,128]{2,1,0:T(8,128)(2,1)S(1)}, bf16[64,24,128]{2,1,0:T(8,128)(2,1)S(1)}, bf16[64,24,128]{2,1,0:T(8,128)(2,1)S(1)}) custom-call(s32[1]{0:T(128)} %bitcast.7.core_ref, bf16[8,128,256]{2,1,0:T(8,128)(2,1)S(1)} %get-tuple-element.80.x_ref, bf16[8,1024,128]{2,1,0:T(8,128)(2,1)} %get-tuple-element.82.lifted_in, ...), custom_call_target="tpu_custom_call" | custom-call | flops 4000000000 | bytes 40000000 | tf_op jit(solution)/shard_map/pallas_call | solution.py:952
  108.6 0.6 collective-permute-start.9
  109.1 1.5 shard_map.219._
  110.7 0.0 collective-permute-done.9.late_got_ref
  110.7 0.3 shard_map.220
  111.0 28.7 %all_to_all.21.got_ref = bf16[64,72,128]{2,1,0:T(8,128)(2,1)S(1)} all-to-all(bf16[64,72,128]{2,1,0:T(8,128)(2,1)S(1)} %shard_map.220), channel_id=1, replica_groups=mesh['row'=8,'hi'=8,'core'=2] {'row','hi'}, dimensions={0} | all-to-all | bytes 2359296 | tf_op jit(solution)/shard_map/all_to_all | solution.py:1069
  139.7 0.3 shard_map.221
  139.9 22.5 %all_to_all.22.mine_ref = bf16[64,72,128]{2,1,0:T(8,128)(2,1)S(1)} all-to-all(bf16[64,72,128]{2,1,0:T(8,128)(2,1)S(1)} %shard_map.221), channel_id=1, replica_groups=mesh['row'=8,'hi'=8,'core'=2] {'row','hi'}, dimensions={0} | all-to-all | bytes 2359296 | tf_op jit(solution)/shard_map/all_to_all | solution.py:1069
  162.4 3.5 %collective-permute-start.10 = (bf16[64,72,128]{2,1,0:T(8,128)(2,1)S(1)}, bf16[64,72,128]{2,1,0:T(8,128)(2,1)S(1)}, u32[]{:S(2)}, u32[]{:S(2)}) collective-permute-start(bf16[64,72,128]{2,1,0:T(8,128)(2,1)S(1)} %all_to_all.22.mine_ref), channel_id=1, source_target_pairs={{0,1},{1,0},{2,3},{3,2},{4,5},{5,4},{6,7},{7,6},{8,9},{9,8},{10,11... | collective-permute-start | bytes 3538952 | tf_op jit(solution)/shard_map/ppermute | solution.py:1073
  166.0 0.2 shard_map.222
  166.2 2.3 %collective-permute-done.10.other_ref = bf16[64,72,128]{2,1,0:T(8,128)(2,1)S(1)} collective-permute-done((bf16[64,72,128]{2,1,0:T(8,128)(2,1)S(1)}, bf16[64,72,128]{2,1,0:T(8,128)(2,1)S(1)}, u32[]{:S(2)}, u32[]{:S(2)}) %collective-permute-start.10) | collective-permute-done | bytes 1179680 | tf_op jit(solution)/shard_map/ppermute | solution.py:1073
  168.4 2.1 %shard_map.223 = (f32[256,1024]{1,0:T(8,128)}, f32[9,1024]{1,0:T(8,128)}, f32[1024,256]{1,0:T(8,128)}, f32[256,768]{1,0:T(8,128)}, f32[256,256]{1,0:T(8,128)}, /*index=5*/f32[256,768]{1,0:T(8,128)}, f32[256,256]{1,0:T(8,128)}) custom-call(s32[1]{0:T(128)} %bitcast.7.core_ref, bf16[64,72,128]{2,1,0:T(8,128)(2,1)S(1)} %collective-permute-done.10.other_ref, ...), custom_call_target="tpu_custom_call" | custom-call | flops 1000000000 | bytes 10000000 | tf_op jit(solution)/shard_map/pallas_call | solution.py:952
  (11 shorter events, 0.1 us)
Async XLA Ops:
  0.6 8.3 %copy-start.3 = (f32[256]{0:T(256)S(1)}, f32[256]{0:T(256)}, u32[]{:S(2)}) copy-start(f32[256]{0:T(256)} %param.17) | copy-start | bytes 3076
  0.6 8.3 %copy-start.2 = (f32[256]{0:T(256)S(1)}, f32[256]{0:T(256)}, u32[]{:S(2)}) copy-start(f32[256]{0:T(256)} %param.18) | copy-start | bytes 3076
  1.9 12.1 %collective-permute-start = (bf16[8,256]{1,0:T(8,128)(2,1)S(1)}, bf16[8,256]{1,0:T(8,128)(2,1)S(1)}, u32[]{:S(2)}, u32[]{:S(2)}) collective-permute-start(bf16[8,256]{1,0:T(8,128)(2,1)S(1)} %get-tuple-element.84), channel_id=1, source_target_pairs={{0,1},{1,0},{2,3},{3,2},{4,5},{5,4},{6,7},{7,6},{8,9},{9,8},{10,11... | collective-permute-start | bytes 12296 | tf_op jit(solution)/shard_map/ppermute | solution.py:1073
  3.4 10.6 %collective-permute-start.1 = (bf16[8,256]{1,0:T(8,128)(2,1)S(1)}, bf16[8,256]{1,0:T(8,128)(2,1)S(1)}, u32[]{:S(2)}, u32[]{:S(2)}) collective-permute-start(bf16[8,256]{1,0:T(8,128)(2,1)S(1)} %get-tuple-element.85), channel_id=1, source_target_pairs={{1,2},{3,4},{5,6},{7,8},{9,10},{11,12},{13,14},{2,1},{4,3},{6,5},{... | collective-permute-start | bytes 12296 | tf_op jit(solution)/shard_map/ppermute | solution.py:1065
  8.9 4.4 %copy-start.4 = (f32[8,225]{1,0:T(8,128)S(1)}, f32[8,225]{1,0:T(8,128)}, u32[]{:S(2)}) copy-start(f32[8,225]{1,0:T(8,128)} %block_ref.1) | copy-start | bytes 21604
  8.9 4.4 %copy-start.5 = (f32[8,225]{1,0:T(8,128)S(1)}, f32[8,225]{1,0:T(8,128)}, u32[]{:S(2)}) copy-start(f32[8,225]{1,0:T(8,128)} %grid_ref.1) | copy-start | bytes 21604
  14.0 6.9 %collective-permute-start.2 = (bf16[144,256]{1,0:T(8,128)(2,1)S(1)}, bf16[144,256]{1,0:T(8,128)(2,1)S(1)}, u32[]{:S(2)}, u32[]{:S(2)}) collective-permute-start(bf16[144,256]{1,0:T(8,128)(2,1)S(1)} %get-tuple-element.86), channel_id=1, source_target_pairs={{0,16},{32,48},{64,80},{96,112},{16,0},{48,32},{80,64},{112,96},{1... | collective-permute-start | bytes 221192 | tf_op jit(solution)/shard_map/ppermute | solution.py:1057
  15.4 5.5 %collective-permute-start.3 = (bf16[144,256]{1,0:T(8,128)(2,1)S(1)}, bf16[144,256]{1,0:T(8,128)(2,1)S(1)}, u32[]{:S(2)}, u32[]{:S(2)}) collective-permute-start(bf16[144,256]{1,0:T(8,128)(2,1)S(1)} %get-tuple-element.87), channel_id=1, source_target_pairs={{16,32},{48,64},{80,96},{32,16},{64,48},{96,80},{17,33},{49,65},{8... | collective-permute-start | bytes 221192 | tf_op jit(solution)/shard_map/ppermute | solution.py:1057
  16.1 4.8 %copy-start = (f32[256]{0:T(256)S(1)}, f32[256]{0:T(256)}, u32[]{:S(2)}) copy-start(f32[256]{0:T(256)} %param.22) | copy-start | bytes 3076
  16.1 4.8 %copy-start.1 = (f32[256]{0:T(256)S(1)}, f32[256]{0:T(256)}, u32[]{:S(2)}) copy-start(f32[256]{0:T(256)} %param.26) | copy-start | bytes 3076
  61.6 0.8 copy-start.6
  62.4 17.2 %all-to-all-start.1 = ((bf16[64,16,256]{2,1,0:T(8,128)(2,1)}), bf16[64,16,256]{2,1,0:T(8,128)(2,1)S(1)}, u32[]{:S(2)}, u32[]{:S(2)}) async-start(bf16[64,16,256]{2,1,0:T(8,128)(2,1)} %get-tuple-element.101), calls=%async_computation.1 | async-start | bytes 1048576 | tf_op jit(solution)/shard_map/all_to_all | solution.py:1069
  85.6 9.3 %collective-permute-start.4 = (bf16[8,8,128]{2,1,0:T(8,128)(2,1)S(1)}, bf16[8,8,128]{2,1,0:T(8,128)(2,1)S(1)}, u32[]{:S(2)}, u32[]{:S(2)}) collective-permute-start(bf16[8,8,128]{2,1,0:T(8,128)(2,1)S(1)} %get-tuple-element.120), channel_id=1, source_target_pairs={{0,1},{1,0},{2,3},{3,2},{4,5},{5,4},{6,7},{7,6},{8,9},{9,8},{10,11... | collective-permute-start | bytes 49160 | tf_op jit(solution)/shard_map/ppermute | solution.py:1073
  88.6 6.5 %collective-permute-start.5 = (bf16[8,8,128]{2,1,0:T(8,128)(2,1)S(1)}, bf16[8,8,128]{2,1,0:T(8,128)(2,1)S(1)}, u32[]{:S(2)}, u32[]{:S(2)}) collective-permute-start(bf16[8,8,128]{2,1,0:T(8,128)(2,1)S(1)} %get-tuple-element.121), channel_id=1, source_target_pairs={{1,2},{3,4},{5,6},{7,8},{9,10},{11,12},{13,14},{2,1},{4,3},{6,5},{... | collective-permute-start | bytes 49160 | tf_op jit(solution)/shard_map/ppermute | solution.py:1065
  95.3 9.6 %collective-permute-start.6 = (bf16[8,144,128]{2,1,0:T(8,128)(2,1)S(1)}, bf16[8,144,128]{2,1,0:T(8,128)(2,1)S(1)}, u32[]{:S(2)}, u32[]{:S(2)}) collective-permute-start(bf16[8,144,128]{2,1,0:T(8,128)(2,1)S(1)} %get-tuple-element.123._), channel_id=1, source_target_pairs={{0,16},{32,48},{64,80},{96,112},{16,0},{48,32},{80,64},{112,96},{1... | collective-permute-start | bytes 884744 | tf_op jit(solution)/shard_map/ppermute | solution.py:1057
  95.7 9.2 %collective-permute-start.7 = (bf16[8,144,128]{2,1,0:T(8,128)(2,1)S(1)}, bf16[8,144,128]{2,1,0:T(8,128)(2,1)S(1)}, u32[]{:S(2)}, u32[]{:S(2)}) collective-permute-start(bf16[8,144,128]{2,1,0:T(8,128)(2,1)S(1)} %get-tuple-element.124), channel_id=1, source_target_pairs={{16,32},{48,64},{80,96},{32,16},{64,48},{96,80},{17,33},{49,65},{8... | collective-permute-start | bytes 884744 | tf_op jit(solution)/shard_map/ppermute | solution.py:1057
  99.0 11.7 %collective-permute-start.8 = (bf16[3072,128]{1,0:T(8,128)(2,1)S(1)}, bf16[3072,128]{1,0:T(8,128)(2,1)S(1)}, u32[]{:S(2)}, u32[]{:S(2)}) collective-permute-start(bf16[3072,128]{1,0:T(8,128)(2,1)S(1)} %get-tuple-element.135), channel_id=1, source_target_pairs={{0,1},{1,0},{2,3},{3,2},{4,5},{5,4},{6,7},{7,6},{8,9},{9,8},{10,11... | collective-permute-start | bytes 2359304 | tf_op jit(solution)/shard_map/ppermute | solution.py:1073
  108.6 2.1 %collective-permute-start.9 = (bf16[64,24,128]{2,1,0:T(8,128)(2,1)S(1)}, bf16[64,24,128]{2,1,0:T(8,128)(2,1)S(1)}, u32[]{:S(2)}, u32[]{:S(2)}) collective-permute-start(bf16[64,24,128]{2,1,0:T(8,128)(2,1)S(1)} %get-tuple-element.137), channel_id=1, source_target_pairs={{0,1},{1,0},{2,3},{3,2},{4,5},{5,4},{6,7},{7,6},{8,9},{9,8},{10,11... | collective-permute-start | bytes 1179656 | tf_op jit(solution)/shard_map/ppermute | solution.py:1073
  162.4 6.0 %collective-permute-start.10 = (bf16[64,72,128]{2,1,0:T(8,128)(2,1)S(1)}, bf16[64,72,128]{2,1,0:T(8,128)(2,1)S(1)}, u32[]{:S(2)}, u32[]{:S(2)}) collective-permute-start(bf16[64,72,128]{2,1,0:T(8,128)(2,1)S(1)} %all_to_all.22.mine_ref), channel_id=1, source_target_pairs={{0,1},{1,0},{2,3},{3,2},{4,5},{5,4},{6,7},{7,6},{8,9},{9,8},{10,11... | collective-permute-start | bytes 3538952 | tf_op jit(solution)/shard_map/ppermute | solution.py:1073
